TPU v7x, 256 devices: a whole 4x4x8 slice. The times are simulated.
256 devices in a mesh: row: 8 (over z_lo, core), col: 8 (over y, z_hi), depth: 4 (over x).
Axes of the slice: x: 4, y: 4, z: 8 (z_hi: 2, z_lo: 4; z = z_hi * 4 + z_lo), core: 2. Of those that a mesh axis runs over, the one named last changes fastest.
Arguments:
- blocks: bfloat16 [1024, 28, 64, 64], P(('row', 'col'), 'depth'), may hold values from -6 to 6
- columns: int32 [1024, 28], P(('row', 'col'), 'depth'), may hold values from 0 to 1023, as said below
- counts: int32 [1024], P(('row', 'col')), may hold values from 20 to 28
- aggregate: int32 [1024], P(('row', 'col')), may hold values from 0 to 3
- coarse_slot: int32 [1024, 28], P(('row', 'col'), 'depth'), may hold values from 0 to 27
- prolong: bfloat16 [1024, 64, 64], P(('row', 'col')), may hold values from -0.75 to 0.75
Outputs:
- coarse: float32 [256, 28, 64, 64], P(('row', 'col'), 'depth')
Inputs may be any that keep to these rules, and one draw needn't show every extreme that they name: The fine block row columns[i, s] belongs to a block-row group whose grid position differs from that of row i by at most one along each grid dimension; groups are numbered first dimension slowest, 16 rows each.
All inputs are finite; a program needn't handle non-finite values.
Results may differ from a plain program's by a relative error of at most 0.0029.
Values may be sent and summed in bfloat16 or wider, within the bound.
No kernel may reach another device: no remote copies, remote signals or barrier semaphores. Data moves between devices by JAX's collectives and lax.ppermute only.
A program may use at most 64 MiB of HBM per device.

v0:
```python
import jax
import jax.numpy as jnp
from jax import lax
from jax.sharding import PartitionSpec as P

SC = 28


def padded(block, sides, width):
    for axis, dim in sides:
        count = lax.axis_size(axis)
        forward = [(i, i + 1) for i in range(count - 1)]
        backward = [(target, source) for source, target in forward]
        low = lax.ppermute(
            lax.slice_in_dim(block, block.shape[dim] - width, None, axis=dim), axis, forward
        )
        high = lax.ppermute(lax.slice_in_dim(block, 0, width, axis=dim), axis, backward)
        block = jnp.concatenate([low, block, high], axis=dim)
    return block


def per_device(blocks, columns, counts, aggregate, coarse_slot, prolong):
    rows_here, slots_here, width, _ = blocks.shape
    group = lax.axis_index(("row", "col"))
    depth_at = lax.axis_index("depth")
    n_grid_col = lax.axis_size("col")
    flat_cols = columns.reshape(-1)
    shaped = prolong.reshape(1, 1, rows_here, width, width)
    framed = padded(shaped, (("row", 0), ("col", 1)), 1)
    framed = framed.reshape(9 * rows_here, width, width)
    home_r = group // n_grid_col
    home_c = group % n_grid_col
    owner = flat_cols // rows_here
    local = flat_cols % rows_here
    offset_r = owner // n_grid_col - home_r + 1
    offset_c = owner % n_grid_col - home_c + 1
    neighbours = jnp.take(framed, (offset_r * 3 + offset_c) * rows_here + local, axis=0)
    slot_ids = depth_at * slots_here + jnp.arange(slots_here, dtype=jnp.int32)
    used = (slot_ids[None, :] < counts[:, None]).reshape(-1)
    product = jnp.einsum(
        "nij,njk->nik",
        blocks.reshape(-1, width, width),
        neighbours,
        preferred_element_type=jnp.float32,
    )
    product = jnp.where(used[:, None, None], product, 0.0).astype(jnp.bfloat16)
    product = product.reshape(rows_here, slots_here, width, width)
    term = jnp.einsum("rji,rsjk->rsik", prolong, product, preferred_element_type=jnp.float32)
    term = term.reshape(rows_here * slots_here, width * width)
    target = (aggregate[:, None] * SC + coarse_slot).reshape(-1)
    n_agg = rows_here // 4
    target_ids = jnp.arange(n_agg * SC, dtype=jnp.int32)
    onehot = (target[:, None] == target_ids[None, :]).astype(jnp.float32)
    partial_sum = jnp.einsum("nt,nf->tf", onehot, term, precision=lax.Precision.HIGHEST)
    partial_sum = partial_sum.reshape(n_agg, SC, width, width)
    return lax.psum_scatter(partial_sum, "depth", scatter_dimension=1, tiled=True)


def solution(mesh):
    in_specs = (
        P(("row", "col"), "depth", None, None),
        P(("row", "col"), "depth"),
        P(("row", "col")),
        P(("row", "col")),
        P(("row", "col"), "depth"),
        P(("row", "col"), None, None),
    )
    out_specs = P(("row", "col"), "depth", None, None)
    return jax.shard_map(
        per_device, mesh=mesh, in_specs=in_specs, out_specs=out_specs, check_vma=False
    )
```

profile of v0, /device:TPU:1, one launch (start us, length us, event | category | flops | bytes accessed | tf_op | source)
XLA Modules:
  0.0 183.2 jit_solution(733118558183991110)
XLA Ops:
  6.5 0.0 copy-start
  6.5 0.0 reduce-scatter.2.cloned.1.call-start
  6.5 5.3 %collective-permute-start.1 = (bf16[1,1,16,64,64]{4,3,2,1,0:T(8,128)(2,1)}, bf16[1,1,16,64,64]{4,3,2,1,0:T(8,128)(2,1)S(1)}, u32[]{:S(2)}, u32[]{:S(2)}) collective-permute-start(bf16[1,1,16,64,64]{4,3,2,1,0:T(8,128)(2,1)} %bitcast.33), channel_id=1, source_target_pairs={{32,0},{64,32},{96,64},{128,96},{160,128},{192,160},{224,192},{33,... | collective-permute-start | bytes 393224 | tf_op jit(solution)/shard_map/ppermute | solution.py:17
  11.8 1.9 %collective-permute-start = (bf16[1,1,16,64,64]{4,3,2,1,0:T(8,128)(2,1)}, bf16[1,1,16,64,64]{4,3,2,1,0:T(8,128)(2,1)S(1)}, u32[]{:S(2)}, u32[]{:S(2)}) collective-permute-start(bf16[1,1,16,64,64]{4,3,2,1,0:T(8,128)(2,1)} %bitcast.34), channel_id=1, source_target_pairs={{0,32},{32,64},{64,96},{96,128},{128,160},{160,192},{192,224},{1,3... | collective-permute-start | bytes 393224 | tf_op jit(solution)/shard_map/ppermute | solution.py:14
  13.8 0.8 copy.26
  14.5 0.1 reshape.263
  14.6 0.1 reshape.260
  14.7 0.7 broadcast_multiply_fusion
  15.4 0.7 broadcast_compare_fusion
  16.1 0.1 lt.60
  16.2 0.7 broadcast_add_fusion
  16.9 0.1 copy.25
  17.0 0.1 eq.36
  17.1 0.0 collective-permute-done.1
  17.1 0.2 collective-permute-done
  17.4 1.1 pad_maximum_fusion.1
  18.5 1.3 collective-permute-start.3
  19.8 8.8 %collective-permute-start.2 = (bf16[3,1,16,64,64]{4,3,2,1,0:T(8,128)(2,1)S(1)}, bf16[3,1,16,64,64]{4,3,2,1,0:T(8,128)(2,1)S(1)}, u32[]{:S(2)}, u32[]{:S(2)}) collective-permute-start(bf16[3,1,16,64,64]{4,3,2,1,0:T(8,128)(2,1)S(1)} %pad_maximum_fusion.1), channel_id=1, source_target_pairs={{0,4},{4,8},{8,12},{12,16},{16,20},{20,24},{24,28},{1,5},{5,9},{9,... | collective-permute-start | bytes 1179656 | tf_op jit(solution)/shard_map/ppermute | solution.py:14
  28.7 16.5 %collective-permute-done.3 = bf16[3,1,16,64,64]{4,3,2,1,0:T(8,128)(2,1)S(1)} collective-permute-done((bf16[3,1,16,64,64]{4,3,2,1,0:T(8,128)(2,1)S(1)}, bf16[3,1,16,64,64]{4,3,2,1,0:T(8,128)(2,1)S(1)}, u32[]{:S(2)}, u32[]{:S(2)}) %collective-permute-start.3) | collective-permute-done | bytes 393248 | tf_op jit(solution)/shard_map/ppermute | solution.py:17
  45.1 1.1 collective-permute-done.2
  46.3 2.7 %pad_maximum_fusion = bf16[3,3,16,64,64]{4,3,2,1,0:T(8,128)(2,1)} fusion(bf16[3,1,16,64,64]{4,3,2,1,0:T(8,128)(2,1)S(1)} %collective-permute-done.3, bf16[1,1,16,64,64]{4,3,2,1,0:T(8,128)(2,1)S(1)} %collective-permute-done.1, bf16[1,1,16,64,64]{4,3,2,1,0:T(8,128)(2,1)} %bitcast.36, bf16[1,1,16,64,64]{4,3,2,1,0:T(8,128)(2,1)S(1)} %collective-permute-done, ...), kind=kLoop, calls=%fused_computation.2 | loop fusion | flops 2359296 | bytes 2359296 | tf_op jit(solution)/shard_map/concatenate | solution.py:18
  49.0 3.7 %gather_fusion = bf16[112,64,64]{2,1,0:T(8,128)(2,1)} fusion(bf16[144,64,64]{2,1,0:T(8,128)(2,1)} %bitcast.31, s32[1024]{0:T(1024)S(1)} %pad_clamp_fusion), kind=kCustom, calls=%fused_computation | custom fusion | bytes 1835456 | tf_op jit(solution)/shard_map/jit(_take)/gather | solution.py:37
  52.7 0.0 copy-done
  52.7 0.0 copy-start.1
  52.7 3.0 %select_convert_fusion = bf16[112,64,64]{2,1,0:T(8,128)(2,1)S(1)} fusion(bf16[112,64,64]{2,1,0:T(8,128)(2,1)S(1)} %bitcast.29, bf16[112,64,64]{2,1,0:T(8,128)(2,1)} %gather_fusion, pred[112]{0:T(512)(128)(4,1)S(1)} %compare_and_fusion, pred[112]{0:T(512)(128)(4,1)S(1)} %lt.60), kind=kOutput, calls=%fused_computation.1 | convolution fusion | flops 60096512 | bytes 2752736 | tf_op jit(solution)/shard_map/nij,njk->nik/dot_general | solution.py:40
  55.7 0.0 copy-done.1
  55.7 2.5 %convolution_bitcast_fusion = f32[16,7,64,64]{2,3,1,0:T(8,128)} fusion(bf16[16,7,64,64]{2,3,1,0:T(8,128)(2,1)S(1)} %bitcast.37, bf16[16,64,64]{2,1,0:T(8,128)(2,1)S(1)} %copy-done.1), kind=kOutput, calls=%fused_computation.3 | convolution fusion | flops 58720256 | bytes 2883584 | tf_op jit(solution)/shard_map/rji,rsjk->rsik/dot_general | solution.py:48
  58.1 5.0 %copy.29 = f32[16,7,64,64]{3,2,1,0:T(8,128)} copy(f32[16,7,64,64]{2,3,1,0:T(8,128)} %convolution_bitcast_fusion) | data formatting | bytes 3670016 | tf_op jit(solution)/shard_map/rji,rsjk->rsik/transpose | solution.py:48
  63.1 4.2 %reshape.266 = f32[112,4096]{1,0:T(8,128)} reshape(f32[16,7,64,64]{3,2,1,0:T(8,128)} %copy.29) | data formatting | bytes 3670016 | tf_op jit(solution)/shard_map/reshape | solution.py:49
  67.3 2.9 %copy.30 = f32[4096,112]{1,0:T(8,128)} copy(f32[4096,112]{0,1:T(8,128)} %bitcast.32) | data formatting | bytes 3670016 | tf_op jit(solution)/shard_map/nt,nf->tf/dot_general | solution.py:54
  70.2 5.1 %fusion.4 = f32[4,28,64,64]{3,1,2,0:T(8,128)S(1)} fusion(f32[64,64,112,1]{2,1,0,3:T(8,128)} %bitcast.30, s32[4,28]{1,0:T(4,128)S(1)} %multiply_add_fusion, s32[112]{0:T(128)S(1)} %eq.36), kind=kOutput, calls=%fused_computation.9 | convolution fusion | flops 616575232 | bytes 3670912 | tf_op jit(solution)/shard_map/nt,nf->tf/dot_general | solution.py:54
  75.2 3.9 %copy.31 = f32[4,28,64,64]{3,2,0,1:T(8,128)} copy(f32[4,28,64,64]{3,1,2,0:T(8,128)S(1)} %fusion.4) | data formatting | bytes 3670016 | tf_op jit(solution)/shard_map/nt,nf->tf/dot_general | solution.py:54
  79.1 0.0 reduce-scatter.2.cloned.1.call-update
  79.2 95.0 %reduce-scatter.2.cloned.1.call-done = f32[4,7,64,64]{3,2,0,1:T(8,128)} async-done(((f32[4,28,64,64]{3,2,0,1:T(8,128)}), f32[4,7,64,64]{3,2,0,1:T(8,128)}) %reduce-scatter.2.cloned.1.call-update) | async-done | bytes 458768 | tf_op jit(solution)/shard_map/reduce_scatter | solution.py:56
  174.2 2.2 %copy.32 = f32[4,7,64,64]{3,2,1,0:T(8,128)} copy(f32[4,7,64,64]{3,2,0,1:T(8,128)} %reduce-scatter.2.cloned.1.call-done) | data formatting | bytes 917504 | tf_op jit(solution)/shard_map/reduce_scatter | solution.py:56
  (5 shorter events, 0.1 us)
Async XLA Ops:
  6.5 46.1 %copy-start = (bf16[16,7,64,64]{3,2,1,0:T(8,128)(2,1)S(1)}, bf16[16,7,64,64]{3,2,1,0:T(8,128)(2,1)}, u32[]{:S(2)}) copy-start(bf16[16,7,64,64]{3,2,1,0:T(8,128)(2,1)} %param.6) | copy-start | bytes 2752516
  6.5 167.6 %reduce-scatter.2.cloned.1.call-start = ((), (), s32[]{:S(2)}) async-start(), calls=%async_computation.1 | async-start | bytes 4587520 | tf_op jit(solution)/shard_map/reduce_scatter | solution.py:56
  6.5 10.6 %collective-permute-start.1 = (bf16[1,1,16,64,64]{4,3,2,1,0:T(8,128)(2,1)}, bf16[1,1,16,64,64]{4,3,2,1,0:T(8,128)(2,1)S(1)}, u32[]{:S(2)}, u32[]{:S(2)}) collective-permute-start(bf16[1,1,16,64,64]{4,3,2,1,0:T(8,128)(2,1)} %bitcast.33), channel_id=1, source_target_pairs={{32,0},{64,32},{96,64},{128,96},{160,128},{192,160},{224,192},{33,... | collective-permute-start | bytes 393224 | tf_op jit(solution)/shard_map/ppermute | solution.py:17
  11.8 5.5 %collective-permute-start = (bf16[1,1,16,64,64]{4,3,2,1,0:T(8,128)(2,1)}, bf16[1,1,16,64,64]{4,3,2,1,0:T(8,128)(2,1)S(1)}, u32[]{:S(2)}, u32[]{:S(2)}) collective-permute-start(bf16[1,1,16,64,64]{4,3,2,1,0:T(8,128)(2,1)} %bitcast.34), channel_id=1, source_target_pairs={{0,32},{32,64},{64,96},{96,128},{128,160},{160,192},{192,224},{1,3... | collective-permute-start | bytes 393224 | tf_op jit(solution)/shard_map/ppermute | solution.py:14
  18.5 26.6 %collective-permute-start.3 = (bf16[3,1,16,64,64]{4,3,2,1,0:T(8,128)(2,1)S(1)}, bf16[3,1,16,64,64]{4,3,2,1,0:T(8,128)(2,1)S(1)}, u32[]{:S(2)}, u32[]{:S(2)}) collective-permute-start(bf16[3,1,16,64,64]{4,3,2,1,0:T(8,128)(2,1)S(1)} %pad_maximum_fusion.1), channel_id=1, source_target_pairs={{4,0},{8,4},{12,8},{16,12},{20,16},{24,20},{28,24},{5,1},{9,5},{13... | collective-permute-start | bytes 1179656 | tf_op jit(solution)/shard_map/ppermute | solution.py:17
  19.8 26.5 %collective-permute-start.2 = (bf16[3,1,16,64,64]{4,3,2,1,0:T(8,128)(2,1)S(1)}, bf16[3,1,16,64,64]{4,3,2,1,0:T(8,128)(2,1)S(1)}, u32[]{:S(2)}, u32[]{:S(2)}) collective-permute-start(bf16[3,1,16,64,64]{4,3,2,1,0:T(8,128)(2,1)S(1)} %pad_maximum_fusion.1), channel_id=1, source_target_pairs={{0,4},{4,8},{8,12},{12,16},{16,20},{20,24},{24,28},{1,5},{5,9},{9,... | collective-permute-start | bytes 1179656 | tf_op jit(solution)/shard_map/ppermute | solution.py:14
  52.7 3.0 %copy-start.1 = (bf16[16,64,64]{2,1,0:T(8,128)(2,1)S(1)}, bf16[16,64,64]{2,1,0:T(8,128)(2,1)}, u32[]{:S(2)}) copy-start(bf16[16,64,64]{2,1,0:T(8,128)(2,1)} %param.11) | copy-start | bytes 393220
Sparse Core Ops, SparseCore 0:
  79.3 94.8 reduce-scatter.1
where the time goes:
time: 184 us; the launch traced here: 183 us
  waiting for transfers between devices  113 us (61%)
  local copies, waits for them, and re-layouts  23 us (12%)
  starting transfers between devices  17.3 us (9%)
  between operations  13.5 us (7%)
  matrix products  10.5 us (6%)
  other arithmetic  5.97 us (3%)
    reduce_scatter x1, waiting for transfers between devices, per_device(): lax.psum_scatter(partial_sum, 'depth', scatter_dimension=1, tiled=True)  95 us
    ppermute x2, waiting for transfers between devices, padded(): lax.ppermute(lax.slice_in_dim(block, 0, width, axis=dim), axis, backward)  16.5 us
    ppermute x2, starting transfers between devices, padded(): lax.ppermute(lax.slice_in_dim(block, block.shape[dim] - width, None, axis...  10.7 us
    dot_general x2, local copies, waits for them, and re-layouts, per_device(): jnp.einsum('nt,nf->tf', onehot, term, precision=lax.Precision.HIGHEST)  6.82 us
    ppermute x2, starting transfers between devices, padded(): lax.ppermute(lax.slice_in_dim(block, 0, width, axis=dim), axis, backward)  6.56 us
    dot_general x1, matrix products, per_device(): jnp.einsum('nt,nf->tf', onehot, term, precision=lax.Precision.HIGHEST)  5.06 us
    transpose x1, local copies, waits for them, and re-layouts, per_device(): jnp.einsum('rji,rsjk->rsik', prolong, product, preferred_element_type=jnp...  4.96 us
    reshape x1, local copies, waits for them, and re-layouts, per_device(): term = term.reshape(rows_here * slots_here, width * width)  4.15 us
  transfers between devices with their start and end apart: 5, of which 4 were waited for; matrix products, arithmetic and copies ran while one was open for 2% of the time, Pallas kernels for 0%

commit v1 on v0

v1 whole, which is shorter than its diff:
```python
import functools

import jax
import jax.numpy as jnp
from jax import lax
from jax.experimental import pallas as pl
from jax.experimental.pallas import tpu as pltpu
from jax.sharding import PartitionSpec as P

SC = 28
ALL = ("row", "col", "depth")
VMEM = pl.BlockSpec(memory_space=pltpu.VMEM)
SMEM = pl.BlockSpec(memory_space=pltpu.SMEM)


def fold(block):
    half = block.shape[0] // 2
    return jnp.concatenate([block[:half], block[half:]], axis=1)


def unfold(block):
    half = block.shape[1] // 2
    return jnp.concatenate([block[:, :half], block[:, half:]], axis=0)


def pack_kernel(prolong_ref, out_ref):
    for i in range(prolong_ref.shape[0]):
        out_ref[i] = fold(prolong_ref[i])


def main_kernel(cols_ref, counts_ref, agg_ref, slot_ref, blocks_ref, prolong_ref, low_ref, mid_ref, high_ref,
                own_ref, one_ref, two_ref, three_ref, halo, acc):
    rows, slots = blocks_ref.shape[:2]
    depth = lax.axis_index("depth")
    home_r, home_c = lax.axis_index("row"), lax.axis_index("col")
    acc[...] = jnp.zeros_like(acc)
    group = 3 * rows
    halo[pl.ds(0, group)] = low_ref[...]
    halo[pl.ds(group, group)] = mid_ref[...]
    halo[pl.ds(2 * group, group)] = high_ref[...]
    far_side = jnp.where(depth < 2, 1, -1)

    def row_step(i, carry):
        left = prolong_ref[i].T
        count, agg = counts_ref[i], agg_ref[i]
        for s in range(slots):
            j = cols_ref[s, i]
            owner = j // rows
            dr = owner // 8 - home_r + 1
            dc = owner % 8 - home_c
            side = jnp.where(dc == 0, 0, jnp.where(dc == far_side, 1, 2))
            near = unfold(halo[(dr * 3 + side) * rows + j % rows])
            product = jnp.dot(blocks_ref[i, s], near, preferred_element_type=jnp.float32)
            used = depth * slots + s < count
            product = jnp.where(used, product, 0.0).astype(jnp.bfloat16)
            term = jnp.dot(left, product, preferred_element_type=jnp.float32)
            acc[slot_ref[s, i] * 4 + agg] += fold(term)
        return carry

    lax.fori_loop(0, rows, row_step, 0)
    size = own_ref.shape[0]
    for out, step in ((own_ref, 0), (one_ref, 1), (two_ref, 2), (three_ref, 3)):
        at = lax.rem(depth + step, 4) * size
        out[...] = acc[pl.ds(at, size)].astype(out.dtype)


def sum_kernel(own_ref, one_ref, two_ref, three_ref, out_ref):
    aggs, slots = out_ref.shape[:2]
    for a in range(aggs):
        for s in range(slots):
            at = s * aggs + a
            total = own_ref[at] + (
                one_ref[at].astype(jnp.float32) + two_ref[at].astype(jnp.float32) + three_ref[at].astype(jnp.float32)
            )
            out_ref[a, s] = unfold(total)


def per_device(blocks, columns, counts, aggregate, coarse_slot, prolong):
    rows, slots, width, _ = blocks.shape
    n_row, n_col, n_depth = (lax.axis_size(a) for a in ALL)

    def flat(r, c, d):
        return (r * n_col + c) * n_depth + d

    packed = pl.pallas_call(
        pack_kernel,
        out_shape=jax.ShapeDtypeStruct((rows, width // 2, 2 * width), prolong.dtype),
        in_specs=[VMEM],
        out_specs=VMEM,
        name="pack",
    )(prolong)
    far_perm = []
    for r in range(n_row):
        for c in range(n_col):
            for d in range(n_depth):
                source = c + 1 if d < n_depth // 2 else c - 1
                if 0 <= source < n_col:
                    far_perm.append((flat(r, source, d), flat(r, c, d)))
    far = lax.ppermute(packed, ALL, far_perm)
    other = lax.ppermute(far, "depth", [(d, n_depth - 1 - d) for d in range(n_depth)])
    mid = jnp.concatenate([packed, far, other], axis=0)
    up = [(r, r + 1) for r in range(n_row - 1)]
    low = lax.ppermute(mid, "row", up)
    high = lax.ppermute(mid, "row", [(b, a) for a, b in up])
    chunk = (SC // n_depth * 4, width // 2, 2 * width)
    own, one, two, three = pl.pallas_call(
        main_kernel,
        out_shape=[jax.ShapeDtypeStruct(chunk, jnp.float32)] + [jax.ShapeDtypeStruct(chunk, jnp.bfloat16)] * 3,
        in_specs=[SMEM] * 4 + [VMEM] * 5,
        out_specs=[VMEM] * 4,
        scratch_shapes=[
            pltpu.VMEM((9 * rows, width // 2, 2 * width), jnp.bfloat16),
            pltpu.VMEM((SC * 4, width // 2, 2 * width), jnp.float32),
        ],
        compiler_params=pltpu.CompilerParams(vmem_limit_bytes=40 * 2**20),
        name="galerkin",
    )(columns.T, counts, aggregate, coarse_slot.T, blocks, prolong, low, mid, high)
    got = [
        lax.ppermute(part, "depth", [(d, (d + k) % n_depth) for d in range(n_depth)])
        for k, part in ((1, one), (2, two), (3, three))
    ]
    return pl.pallas_call(
        sum_kernel,
        out_shape=jax.ShapeDtypeStruct((4, SC // n_depth, width, width), jnp.float32),
        in_specs=[VMEM] * 4,
        out_specs=VMEM,
        name="total",
    )(own, *got)


def solution(mesh):
    in_specs = (
        P(("row", "col"), "depth", None, None),
        P(("row", "col"), "depth"),
        P(("row", "col")),
        P(("row", "col")),
        P(("row", "col"), "depth"),
        P(("row", "col"), None, None),
    )
    out_specs = P(("row", "col"), "depth", None, None)
    return jax.shard_map(per_device, mesh=mesh, in_specs=in_specs, out_specs=out_specs, check_vma=False)
```

time: 184 us -> 67.6 us (0.37)
  the two profiles are of different devices: /device:TPU:1 before, /device:TPU:57 now
where the time goes in v1:
time: 67.6 us; the launch traced here: 67.3 us
  starting transfers between devices  26.4 us (39%)
  waiting for transfers between devices  20.3 us (30%)
  Pallas kernels  12.8 us (19%)
  local copies, waits for them, and re-layouts  6.66 us (10%)
  other arithmetic  0.95 us (1%)
    ppermute x3, waiting for transfers between devices, per_device(): lax.ppermute(part, 'depth', [(d, (d + k) % n_depth) for d in range(n_dept...  10.9 us
    pallas_call x1, Pallas kernels, per_device(): pl.pallas_call(main_kernel, out_shape=[jax.ShapeDtypeStruct(chunk, jnp.fl...  8.75 us
    ppermute x1, starting transfers between devices, per_device(): far = lax.ppermute(packed, ALL, far_perm)  8.09 us
    unnamed x20, local copies, waits for them, and re-layouts  6.66 us
    ppermute x1, starting transfers between devices, per_device(): lax.ppermute(far, 'depth', [(d, n_depth - 1 - d) for d in range(n_depth)])  5.17 us
    ppermute x1, starting transfers between devices, per_device(): high = lax.ppermute(mid, 'row', [(b, a) for a, b in up])  5 us
    ppermute x1, starting transfers between devices, per_device(): low = lax.ppermute(mid, 'row', up)  4.33 us
    ppermute x3, starting transfers between devices, per_device(): lax.ppermute(part, 'depth', [(d, (d + k) % n_depth) for d in range(n_dept...  3.86 us
  transfers between devices with their start and end apart: 7, of which 6 were waited for; matrix products, arithmetic and copies ran while one was open for 0% of the time, Pallas kernels for 0%

profile of v1, /device:TPU:57, one launch (start us, length us, event | category | flops | bytes accessed | tf_op | source)
XLA Modules:
  0.0 67.3 jit_solution(5015130635017611306)
XLA Ops:
  0.0 1.7 %pack.1 = bf16[16,32,128]{2,1,0:T(8,128)(2,1)} custom-call(bf16[16,64,64]{2,1,0:T(8,128)(2,1)} %prolong_ref.3), custom_call_target="tpu_custom_call" | custom-call | tf_op jit(solution)/shard_map/pack/pallas_call | solution.py:85
  1.7 8.1 %collective-permute-start = (bf16[16,32,128]{2,1,0:T(8,128)(2,1)}, bf16[16,32,128]{2,1,0:T(8,128)(2,1)S(1)}, u32[]{:S(2)}, u32[]{:S(2)}) collective-permute-start(bf16[16,32,128]{2,1,0:T(8,128)(2,1)} %pack.1), channel_id=1, source_target_pairs={{4,0},{5,1},{8,4},{9,5},{2,6},{3,7},{12,8},{13,9},{6,10},{7,11},{1... | collective-permute-start | bytes 393224 | tf_op jit(solution)/shard_map/ppermute | solution.py:99
  9.8 2.4 %collective-permute-done = bf16[16,32,128]{2,1,0:T(8,128)(2,1)S(1)} collective-permute-done((bf16[16,32,128]{2,1,0:T(8,128)(2,1)}, bf16[16,32,128]{2,1,0:T(8,128)(2,1)S(1)}, u32[]{:S(2)}, u32[]{:S(2)}) %collective-permute-start) | collective-permute-done | bytes 131104 | tf_op jit(solution)/shard_map/ppermute | solution.py:99
  12.2 5.2 %collective-permute-start.1 = (bf16[16,32,128]{2,1,0:T(8,128)(2,1)S(1)}, bf16[16,32,128]{2,1,0:T(8,128)(2,1)S(1)}, u32[]{:S(2)}, u32[]{:S(2)}) collective-permute-start(bf16[16,32,128]{2,1,0:T(8,128)(2,1)S(1)} %collective-permute-done), channel_id=1, source_target_pairs={{0,3},{1,2},{2,1},{3,0},{4,7},{5,6},{6,5},{7,4},{8,11},{9,10},{10,... | collective-permute-start | bytes 393224 | tf_op jit(solution)/shard_map/ppermute | solution.py:100
  17.4 2.4 %collective-permute-done.1 = bf16[16,32,128]{2,1,0:T(8,128)(2,1)S(1)} collective-permute-done((bf16[16,32,128]{2,1,0:T(8,128)(2,1)S(1)}, bf16[16,32,128]{2,1,0:T(8,128)(2,1)S(1)}, u32[]{:S(2)}, u32[]{:S(2)}) %collective-permute-start.1) | collective-permute-done | bytes 131104 | tf_op jit(solution)/shard_map/ppermute | solution.py:100
  19.7 0.9 %pad_maximum_fusion.mid_ref = bf16[48,32,128]{2,1,0:T(8,128)(2,1)S(1)} fusion(bf16[16,32,128]{2,1,0:T(8,128)(2,1)S(1)} %collective-permute-done.1, bf16[16,32,128]{2,1,0:T(8,128)(2,1)S(1)} %collective-permute-done, bf16[16,32,128]{2,1,0:T(8,128)(2,1)} %pack.1), kind=kLoop, calls=%fused_computation | loop fusion | flops 393216 | bytes 786432 | tf_op jit(solution)/shard_map/concatenate | solution.py:101
  20.7 5.0 %collective-permute-start.3 = (bf16[48,32,128]{2,1,0:T(8,128)(2,1)S(1)}, bf16[48,32,128]{2,1,0:T(8,128)(2,1)S(1)}, u32[]{:S(2)}, u32[]{:S(2)}) collective-permute-start(bf16[48,32,128]{2,1,0:T(8,128)(2,1)S(1)} %pad_maximum_fusion.mid_ref), channel_id=1, source_target_pairs={{32,0},{64,32},{96,64},{128,96},{160,128},{192,160},{224,192},{33,... | collective-permute-start | bytes 1179656 | tf_op jit(solution)/shard_map/ppermute | solution.py:104
  25.7 4.3 %collective-permute-start.2 = (bf16[48,32,128]{2,1,0:T(8,128)(2,1)S(1)}, bf16[48,32,128]{2,1,0:T(8,128)(2,1)S(1)}, u32[]{:S(2)}, u32[]{:S(2)}) collective-permute-start(bf16[48,32,128]{2,1,0:T(8,128)(2,1)S(1)} %pad_maximum_fusion.mid_ref), channel_id=1, source_target_pairs={{0,32},{32,64},{64,96},{96,128},{128,160},{160,192},{192,224},{1,3... | collective-permute-start | bytes 1179656 | tf_op jit(solution)/shard_map/ppermute | solution.py:103
  30.0 3.8 %collective-permute-done.3.high_ref = bf16[48,32,128]{2,1,0:T(8,128)(2,1)S(1)} collective-permute-done((bf16[48,32,128]{2,1,0:T(8,128)(2,1)S(1)}, bf16[48,32,128]{2,1,0:T(8,128)(2,1)S(1)}, u32[]{:S(2)}, u32[]{:S(2)}) %collective-permute-start.3) | collective-permute-done | bytes 393248 | tf_op jit(solution)/shard_map/ppermute | solution.py:104
  33.8 0.9 %collective-permute-done.2.low_ref = bf16[48,32,128]{2,1,0:T(8,128)(2,1)S(1)} collective-permute-done((bf16[48,32,128]{2,1,0:T(8,128)(2,1)S(1)}, bf16[48,32,128]{2,1,0:T(8,128)(2,1)S(1)}, u32[]{:S(2)}, u32[]{:S(2)}) %collective-permute-start.2) | collective-permute-done | bytes 393248 | tf_op jit(solution)/shard_map/ppermute | solution.py:103
  34.7 0.0 copy-start
  34.7 1.5 %copy-done = bf16[16,7,64,64]{3,2,1,0:T(8,128)(2,1)S(1)} copy-done((bf16[16,7,64,64]{3,2,1,0:T(8,128)(2,1)S(1)}, bf16[16,7,64,64]{3,2,1,0:T(8,128)(2,1)}, u32[]{:S(2)}) %copy-start) | copy-done | bytes 917528
  36.2 0.0 copy-start.1
  36.2 0.9 %copy-done.1 = bf16[16,64,64]{2,1,0:T(8,128)(2,1)S(1)} copy-done((bf16[16,64,64]{2,1,0:T(8,128)(2,1)S(1)}, bf16[16,64,64]{2,1,0:T(8,128)(2,1)}, u32[]{:S(2)}) %copy-start.1) | copy-done | bytes 131096
  37.1 0.0 copy-start.3
  37.2 0.7 %copy-done.3 = s32[16,7]{0,1:T(8,128)S(1)} copy-done((s32[16,7]{0,1:T(8,128)S(1)}, s32[16,7]{0,1:T(8,128)}, u32[]{:S(2)}) %copy-start.3) | copy-done | bytes 472
  37.8 0.0 copy-start.4
  37.8 0.7 %copy-done.4 = s32[16,7]{0,1:T(8,128)S(1)} copy-done((s32[16,7]{0,1:T(8,128)S(1)}, s32[16,7]{0,1:T(8,128)}, u32[]{:S(2)}) %copy-start.4) | copy-done | bytes 472
  38.5 0.0 copy-start.5
  38.5 0.7 copy-done.5
  39.2 0.0 copy-start.6
  39.2 0.7 copy-done.6
  39.8 8.7 %galerkin.1 = (f32[28,32,128]{2,1,0:T(8,128)S(1)}, bf16[28,32,128]{2,1,0:T(8,128)(2,1)S(1)}, bf16[28,32,128]{2,1,0:T(8,128)(2,1)S(1)}, bf16[28,32,128]{2,1,0:T(8,128)(2,1)S(1)}) custom-call(s32[7,16]{1,0:T(8,128)S(1)} %bitcast.2, s32[16]{0:T(128)S(1)} %copy-done.5, s32[16]{0:T(128)S(1)} %copy-done.6, s32[7,16]{1,0:T(8,128)S(1)} %bitcast.3, ...), custom_call_target="tpu_custom_call" | custom-call | tf_op jit(solution)/shard_map/galerkin/pallas_call | solution.py:106
  48.6 0.0 copy-start.2
  48.6 0.8 %copy-done.2 = f32[28,32,128]{2,1,0:T(8,128)} copy-done((f32[28,32,128]{2,1,0:T(8,128)}, f32[28,32,128]{2,1,0:T(8,128)S(1)}, u32[]{:S(2)}) %copy-start.2) | copy-done | bytes 458776
  49.4 0.0 collective-permute-start.4
  49.4 3.9 %collective-permute-start.5 = (bf16[28,32,128]{2,1,0:T(8,128)(2,1)S(1)}, bf16[28,32,128]{2,1,0:T(8,128)(2,1)S(1)}, u32[]{:S(2)}, u32[]{:S(2)}) collective-permute-start(bf16[28,32,128]{2,1,0:T(8,128)(2,1)S(1)} %get-tuple-element.11), channel_id=1, source_target_pairs={{0,2},{1,3},{2,0},{3,1},{4,6},{5,7},{6,4},{7,5},{8,10},{9,11},{10,... | collective-permute-start | bytes 688136 | tf_op jit(solution)/shard_map/ppermute | solution.py:119
  53.2 0.0 collective-permute-start.6
  53.2 4.5 %collective-permute-done.4.one_ref = bf16[28,32,128]{2,1,0:T(8,128)(2,1)S(1)} collective-permute-done((bf16[28,32,128]{2,1,0:T(8,128)(2,1)S(1)}, bf16[28,32,128]{2,1,0:T(8,128)(2,1)S(1)}, u32[]{:S(2)}, u32[]{:S(2)}) %collective-permute-start.4) | collective-permute-done | bytes 229408 | tf_op jit(solution)/shard_map/ppermute | solution.py:119
  57.7 0.0 copy-start.7
  57.7 6.4 %collective-permute-done.5.two_ref = bf16[28,32,128]{2,1,0:T(8,128)(2,1)S(1)} collective-permute-done((bf16[28,32,128]{2,1,0:T(8,128)(2,1)S(1)}, bf16[28,32,128]{2,1,0:T(8,128)(2,1)S(1)}, u32[]{:S(2)}, u32[]{:S(2)}) %collective-permute-start.5) | collective-permute-done | bytes 229408 | tf_op jit(solution)/shard_map/ppermute | solution.py:119
  64.1 0.0 copy-start.8
  64.1 0.0 collective-permute-done.6.three_ref
  64.1 0.0 copy-start.9
  64.1 0.0 copy-done.7
  64.1 0.7 copy-done.8
  64.8 0.1 copy-done.9
  64.9 2.4 %total.1 = f32[4,7,64,64]{3,2,1,0:T(8,128)} custom-call(f32[28,32,128]{2,1,0:T(8,128)} %copy-done.2, bf16[28,32,128]{2,1,0:T(8,128)(2,1)} %copy-done.7, bf16[28,32,128]{2,1,0:T(8,128)(2,1)} %copy-done.8, bf16[28,32,128]{2,1,0:T(8,128)(2,1)} %copy-done.9), custom_call_target="tpu_custom_call" | custom-call | tf_op jit(solution)/shard_map/total/pallas_call | solution.py:122
Async XLA Ops:
  1.7 10.5 %collective-permute-start = (bf16[16,32,128]{2,1,0:T(8,128)(2,1)}, bf16[16,32,128]{2,1,0:T(8,128)(2,1)S(1)}, u32[]{:S(2)}, u32[]{:S(2)}) collective-permute-start(bf16[16,32,128]{2,1,0:T(8,128)(2,1)} %pack.1), channel_id=1, source_target_pairs={{4,0},{5,1},{8,4},{9,5},{2,6},{3,7},{12,8},{13,9},{6,10},{7,11},{1... | collective-permute-start | bytes 393224 | tf_op jit(solution)/shard_map/ppermute | solution.py:99
  12.2 7.5 %collective-permute-start.1 = (bf16[16,32,128]{2,1,0:T(8,128)(2,1)S(1)}, bf16[16,32,128]{2,1,0:T(8,128)(2,1)S(1)}, u32[]{:S(2)}, u32[]{:S(2)}) collective-permute-start(bf16[16,32,128]{2,1,0:T(8,128)(2,1)S(1)} %collective-permute-done), channel_id=1, source_target_pairs={{0,3},{1,2},{2,1},{3,0},{4,7},{5,6},{6,5},{7,4},{8,11},{9,10},{10,... | collective-permute-start | bytes 393224 | tf_op jit(solution)/shard_map/ppermute | solution.py:100
  20.7 13.2 %collective-permute-start.3 = (bf16[48,32,128]{2,1,0:T(8,128)(2,1)S(1)}, bf16[48,32,128]{2,1,0:T(8,128)(2,1)S(1)}, u32[]{:S(2)}, u32[]{:S(2)}) collective-permute-start(bf16[48,32,128]{2,1,0:T(8,128)(2,1)S(1)} %pad_maximum_fusion.mid_ref), channel_id=1, source_target_pairs={{32,0},{64,32},{96,64},{128,96},{160,128},{192,160},{224,192},{33,... | collective-permute-start | bytes 1179656 | tf_op jit(solution)/shard_map/ppermute | solution.py:104
  25.7 9.0 %collective-permute-start.2 = (bf16[48,32,128]{2,1,0:T(8,128)(2,1)S(1)}, bf16[48,32,128]{2,1,0:T(8,128)(2,1)S(1)}, u32[]{:S(2)}, u32[]{:S(2)}) collective-permute-start(bf16[48,32,128]{2,1,0:T(8,128)(2,1)S(1)} %pad_maximum_fusion.mid_ref), channel_id=1, source_target_pairs={{0,32},{32,64},{64,96},{96,128},{128,160},{160,192},{192,224},{1,3... | collective-permute-start | bytes 1179656 | tf_op jit(solution)/shard_map/ppermute | solution.py:103
  34.7 1.5 %copy-start = (bf16[16,7,64,64]{3,2,1,0:T(8,128)(2,1)S(1)}, bf16[16,7,64,64]{3,2,1,0:T(8,128)(2,1)}, u32[]{:S(2)}) copy-start(bf16[16,7,64,64]{3,2,1,0:T(8,128)(2,1)} %blocks_ref.1) | copy-start | bytes 2752516
  36.2 0.9 %copy-start.1 = (bf16[16,64,64]{2,1,0:T(8,128)(2,1)S(1)}, bf16[16,64,64]{2,1,0:T(8,128)(2,1)}, u32[]{:S(2)}) copy-start(bf16[16,64,64]{2,1,0:T(8,128)(2,1)} %prolong_ref.3) | copy-start | bytes 393220
  37.1 0.7 %copy-start.3 = (s32[16,7]{0,1:T(8,128)S(1)}, s32[16,7]{0,1:T(8,128)}, u32[]{:S(2)}) copy-start(s32[16,7]{0,1:T(8,128)} %param.7) | copy-start | bytes 1348
  37.8 0.7 %copy-start.4 = (s32[16,7]{0,1:T(8,128)S(1)}, s32[16,7]{0,1:T(8,128)}, u32[]{:S(2)}) copy-start(s32[16,7]{0,1:T(8,128)} %param.10) | copy-start | bytes 1348
  38.5 0.7 copy-start.5
  39.2 0.7 copy-start.6
  48.6 0.8 %copy-start.2 = (f32[28,32,128]{2,1,0:T(8,128)}, f32[28,32,128]{2,1,0:T(8,128)S(1)}, u32[]{:S(2)}) copy-start(f32[28,32,128]{2,1,0:T(8,128)S(1)} %get-tuple-element.9.own_ref) | copy-start | bytes 1376260
  49.4 8.4 %collective-permute-start.4 = (bf16[28,32,128]{2,1,0:T(8,128)(2,1)S(1)}, bf16[28,32,128]{2,1,0:T(8,128)(2,1)S(1)}, u32[]{:S(2)}, u32[]{:S(2)}) collective-permute-start(bf16[28,32,128]{2,1,0:T(8,128)(2,1)S(1)} %get-tuple-element.10), channel_id=1, source_target_pairs={{0,1},{1,2},{2,3},{3,0},{4,5},{5,6},{6,7},{7,4},{8,9},{9,10},{10,1... | collective-permute-start | bytes 688136 | tf_op jit(solution)/shard_map/ppermute | solution.py:119
  49.4 14.8 %collective-permute-start.5 = (bf16[28,32,128]{2,1,0:T(8,128)(2,1)S(1)}, bf16[28,32,128]{2,1,0:T(8,128)(2,1)S(1)}, u32[]{:S(2)}, u32[]{:S(2)}) collective-permute-start(bf16[28,32,128]{2,1,0:T(8,128)(2,1)S(1)} %get-tuple-element.11), channel_id=1, source_target_pairs={{0,2},{1,3},{2,0},{3,1},{4,6},{5,7},{6,4},{7,5},{8,10},{9,11},{10,... | collective-permute-start | bytes 688136 | tf_op jit(solution)/shard_map/ppermute | solution.py:119
  53.2 10.9 %collective-permute-start.6 = (bf16[28,32,128]{2,1,0:T(8,128)(2,1)S(1)}, bf16[28,32,128]{2,1,0:T(8,128)(2,1)S(1)}, u32[]{:S(2)}, u32[]{:S(2)}) collective-permute-start(bf16[28,32,128]{2,1,0:T(8,128)(2,1)S(1)} %get-tuple-element.12), channel_id=1, source_target_pairs={{0,3},{1,0},{2,1},{3,2},{4,7},{5,4},{6,5},{7,6},{8,11},{9,8},{10,9... | collective-permute-start | bytes 688136 | tf_op jit(solution)/shard_map/ppermute | solution.py:119
  57.7 6.4 %copy-start.7 = (bf16[28,32,128]{2,1,0:T(8,128)(2,1)}, bf16[28,32,128]{2,1,0:T(8,128)(2,1)S(1)}, u32[]{:S(2)}) copy-start(bf16[28,32,128]{2,1,0:T(8,128)(2,1)S(1)} %collective-permute-done.4.one_ref) | copy-start | bytes 688132
  64.1 0.7 %copy-start.8 = (bf16[28,32,128]{2,1,0:T(8,128)(2,1)}, bf16[28,32,128]{2,1,0:T(8,128)(2,1)S(1)}, u32[]{:S(2)}) copy-start(bf16[28,32,128]{2,1,0:T(8,128)(2,1)S(1)} %collective-permute-done.5.two_ref) | copy-start | bytes 688132
  64.1 0.8 %copy-start.9 = (bf16[28,32,128]{2,1,0:T(8,128)(2,1)}, bf16[28,32,128]{2,1,0:T(8,128)(2,1)S(1)}, u32[]{:S(2)}) copy-start(bf16[28,32,128]{2,1,0:T(8,128)(2,1)S(1)} %collective-permute-done.6.three_ref) | copy-start | bytes 688132

commit v2 on v1

v2 whole, which is shorter than its diff:
```python
import jax
import jax.numpy as jnp
from jax import lax
from jax.experimental import pallas as pl
from jax.experimental.pallas import tpu as pltpu
from jax.sharding import PartitionSpec as P

SC = 28
ALL = ("row", "col", "depth")
HBM = pl.BlockSpec(memory_space=pltpu.HBM)
VMEM = pl.BlockSpec(memory_space=pltpu.VMEM)
SMEM = pl.BlockSpec(memory_space=pltpu.SMEM)
LIMIT = pltpu.CompilerParams(vmem_limit_bytes=16 * 2**20)
BATCH = 56


def fold(block):
    half = block.shape[0] // 2
    return jnp.concatenate([block[:half], block[half:]], axis=1)


def unfold(block):
    half = block.shape[1] // 2
    return jnp.concatenate([block[:, :half], block[:, half:]], axis=0)


def pack_kernel(prolong_ref, out_ref):
    for i in range(prolong_ref.shape[0]):
        out_ref[i] = fold(prolong_ref[i])


def prep_kernel(cols_hbm, counts_hbm, agg_hbm, slot_hbm, blocks_hbm, packed_ref, blocks_ref, turned_ref, table_ref,
                cols_ref, counts_ref, agg_ref, slot_ref, sems):
    pairs = ((cols_hbm, cols_ref), (counts_hbm, counts_ref), (agg_hbm, agg_ref), (slot_hbm, slot_ref), (blocks_hbm, blocks_ref))
    copies = [pltpu.make_async_copy(a, b, sems.at[n]) for n, (a, b) in enumerate(pairs)]
    for copy in copies:
        copy.start()
    slots, rows = cols_ref.shape
    depth = lax.axis_index("depth")
    home_r, home_c = lax.axis_index("row"), lax.axis_index("col")
    across, flip = 1 - 2 * (home_c & 1), 1 - 2 * (home_r & 1)
    for i in range(rows):
        turned_ref[i] = unfold(packed_ref[i]).T
    for copy in copies[:4]:
        copy.wait()

    def row_step(i, carry):
        count, agg = counts_ref[i], agg_ref[i]
        for s in range(slots):
            j = cols_ref[s, i]
            dr = ((j >> 7) - home_r) * flip + 1
            dc = ((j >> 4) & 7) - home_c
            side = jnp.where(dc == 0, 0, jnp.where(dc == across, 1, 2))
            near = (dr * 3 + side) * rows + (j & 15)
            used = depth * slots + s < count
            target = jnp.where(used, slot_ref[s, i] * 4 + agg, SC * 4)
            table_ref[i * slots + s] = (near << 8) + target
        return carry

    lax.fori_loop(0, rows, row_step, 0)
    copies[4].wait()


def main_kernel(table_ref, blocks_ref, turned_ref, own_p, low_p, high_p, far_ref, other_ref, low_ref, high_ref,
                own_ref, one_ref, two_ref, three_ref, halo, acc):
    depth = lax.axis_index("depth")
    rows = own_p.shape[0]
    slots = blocks_ref.shape[0] // rows
    for at, part in enumerate((low_p, low_ref, own_p, far_ref, other_ref, high_p, high_ref)):
        first = (0, 1, 3, 4, 5, 6, 7)[at] * rows
        halo[pl.ds(first, part.shape[0])] = part[...]
    acc[...] = jnp.zeros_like(acc)

    for start in range(0, rows * slots, BATCH):
        items = range(start, start + BATCH)
        entries = [table_ref[n] for n in items]
        products = [
            jnp.dot(blocks_ref[n], unfold(halo[e >> 8]), preferred_element_type=jnp.float32).astype(jnp.bfloat16)
            for n, e in zip(items, entries)
        ]
        for n, e, product in zip(items, entries, products):
            term = jnp.dot(turned_ref[n // slots], product, preferred_element_type=jnp.float32)
            acc[e & 255] += fold(term)
    size = own_ref.shape[0]
    for out, step in ((own_ref, 0), (one_ref, 1), (two_ref, 2), (three_ref, 3)):
        at = lax.rem(depth + step, 4) * size
        out[...] = acc[pl.ds(at, size)].astype(out.dtype)


def sum_kernel(own_ref, one_ref, two_ref, three_ref, out_hbm, total_ref, sems):
    aggs, slots = total_ref.shape[:2]
    copies = []
    for a in range(aggs):
        for s in range(slots):
            at = s * aggs + a
            total = own_ref[at] + (
                one_ref[at].astype(jnp.float32) + two_ref[at].astype(jnp.float32) + three_ref[at].astype(jnp.float32)
            )
            total_ref[a, s] = unfold(total)
        copies.append(pltpu.make_async_copy(total_ref.at[a], out_hbm.at[a], sems.at[a]))
        copies[-1].start()
    for copy in copies:
        copy.wait()


def per_device(blocks, columns, counts, aggregate, coarse_slot, prolong):
    rows, slots, width, _ = blocks.shape
    n_row, n_col, n_depth = (lax.axis_size(a) for a in ALL)
    piece = (width // 2, 2 * width)

    packed = pl.pallas_call(
        pack_kernel,
        out_shape=jax.ShapeDtypeStruct((rows, *piece), prolong.dtype),
        in_specs=[VMEM],
        out_specs=VMEM,
        compiler_params=LIMIT,
        name="pack",
    )(prolong)
    far = lax.ppermute(packed, "col", [(c, c ^ 1) for c in range(n_col)])
    block_vmem, turned, table = pl.pallas_call(
        prep_kernel,
        out_shape=[
            jax.ShapeDtypeStruct((rows * slots, width, width), blocks.dtype),
            jax.ShapeDtypeStruct((rows, width, width), prolong.dtype),
            jax.ShapeDtypeStruct((rows * slots,), jnp.int32),
        ],
        in_specs=[HBM] * 5 + [VMEM],
        out_specs=[VMEM, VMEM, SMEM],
        scratch_shapes=[
            pltpu.SMEM((slots, rows), jnp.int32),
            pltpu.SMEM((rows,), jnp.int32),
            pltpu.SMEM((rows,), jnp.int32),
            pltpu.SMEM((slots, rows), jnp.int32),
            pltpu.SemaphoreType.DMA((5,)),
        ],
        compiler_params=LIMIT,
        cost_estimate=pl.CostEstimate(flops=0, bytes_accessed=4 * 2**20, transcendentals=0),
        name="prep",
    )(columns.T, counts, aggregate, coarse_slot.T, blocks.reshape(rows * slots, width, width), packed)

    core = [(r, r ^ 1) for r in range(n_row)]
    chip = [(r, r - 1) for r in range(2, n_row, 2)] + [(r, r + 1) for r in range(1, n_row - 1, 2)]

    def row_exchange(part):
        same, next_ = lax.ppermute(part, "row", core), lax.ppermute(part, "row", chip)
        even = lax.axis_index("row") % 2 == 0
        return same, next_, even

    far, packed_late, turned = lax.optimization_barrier((far, packed, turned))
    p_core, p_chip, _ = row_exchange(packed_late)
    fetch = [(c - 2, c) for c in range(2, n_col, 2)] + [(c + 2, c) for c in range(1, n_col - 2, 2)]
    other = lax.ppermute(far, "col", fetch)
    both = jnp.concatenate([far, other], axis=0)
    b_core, b_chip, even = row_exchange(both)
    chunk = (SC // n_depth * 4, *piece)

    own, one, two, three = pl.pallas_call(
        main_kernel,
        out_shape=[jax.ShapeDtypeStruct(chunk, jnp.float32)] + [jax.ShapeDtypeStruct(chunk, jnp.bfloat16)] * 3,
        in_specs=[SMEM] + [VMEM] * 9,
        out_specs=[VMEM] * 4,
        scratch_shapes=[
            pltpu.VMEM((9 * rows, *piece), jnp.bfloat16),
            pltpu.VMEM((SC * 4 + 1, *piece), jnp.float32),
        ],
        compiler_params=LIMIT,
        name="galerkin",
    )(table, block_vmem, turned, packed, p_chip, p_core, far, other, b_chip, b_core)
    got = {
        k: lax.ppermute(part, "depth", [(d, (d + k) % n_depth) for d in range(n_depth)])
        for k, part in ((2, two), (1, one), (3, three))
    }
    return pl.pallas_call(
        sum_kernel,
        out_shape=jax.ShapeDtypeStruct((4, SC // n_depth, width, width), jnp.float32),
        in_specs=[VMEM] * 4,
        out_specs=HBM,
        scratch_shapes=[
            pltpu.VMEM((4, SC // n_depth, width, width), jnp.float32),
            pltpu.SemaphoreType.DMA((4,)),
        ],
        compiler_params=LIMIT,
        name="total",
    )(own, got[1], got[2], got[3])


def solution(mesh):
    in_specs = (
        P(("row", "col"), "depth", None, None),
        P(("row", "col"), "depth"),
        P(("row", "col")),
        P(("row", "col")),
        P(("row", "col"), "depth"),
        P(("row", "col"), None, None),
    )
    out_specs = P(("row", "col"), "depth", None, None)
    return jax.shard_map(per_device, mesh=mesh, in_specs=in_specs, out_specs=out_specs, check_vma=False)
```

time: 67.6 us -> 49.1 us (0.73)
  the two profiles are of different devices: /device:TPU:57 before, /device:TPU:40 now
where the time goes in v2:
time: 49.1 us; the launch traced here: 48.8 us
  starting transfers between devices  21.4 us (44%)
  waiting for transfers between devices  16.6 us (34%)
  Pallas kernels  5.64 us (11%)
  local copies, waits for them, and re-layouts  5.16 us (11%)
    ppermute x3, waiting for transfers between devices, per_device(): lax.ppermute(part, 'depth', [(d, (d + k) % n_depth) for d in range(n_dept...  9.27 us
    ppermute x1, starting transfers between devices, per_device(): far = lax.ppermute(packed, 'col', [(c, c ^ 1) for c in range(n_col)])  6.38 us
    ppermute x3, starting transfers between devices, per_device(): lax.ppermute(part, 'depth', [(d, (d + k) % n_depth) for d in range(n_dept...  5.74 us
    ppermute x2, starting transfers between devices, row_exchange(): lax.ppermute(part, 'row', chip)  5.31 us
    unnamed x13, local copies, waits for them, and re-layouts  5.14 us
    ppermute x2, waiting for transfers between devices, row_exchange(): lax.ppermute(part, 'row', chip)  3.95 us
    ppermute x1, starting transfers between devices, per_device(): other = lax.ppermute(far, 'col', fetch)  3.48 us
    ppermute x1, waiting for transfers between devices, per_device(): other = lax.ppermute(far, 'col', fetch)  3.35 us
  transfers between devices with their start and end apart: 9, of which 4 were waited for; matrix products, arithmetic and copies ran while one was open for 0% of the time, Pallas kernels for 5%

profile of v2, /device:TPU:40, one launch (start us, length us, event | category | flops | bytes accessed | tf_op | source)
XLA Modules:
  0.0 48.8 jit_solution(13317600767591114973)
XLA Ops:
  0.0 0.0 copy-start.1
  0.0 0.9 %copy-done.1 = bf16[16,64,64]{2,1,0:T(8,128)(2,1)S(1)} copy-done((bf16[16,64,64]{2,1,0:T(8,128)(2,1)S(1)}, bf16[16,64,64]{2,1,0:T(8,128)(2,1)}, u32[]{:S(2)}) %copy-start.1) | copy-done | bytes 131096
  1.0 0.1 pack.1.packed_ref.own_p
  1.1 6.4 %collective-permute-start = (bf16[16,32,128]{2,1,0:T(8,128)(2,1)S(1)}, bf16[16,32,128]{2,1,0:T(8,128)(2,1)S(1)}, u32[]{:S(2)}, u32[]{:S(2)}) collective-permute-start(bf16[16,32,128]{2,1,0:T(8,128)(2,1)S(1)} %pack.1.packed_ref.own_p), channel_id=1, source_target_pairs={{0,4},{4,0},{8,12},{12,8},{16,20},{20,16},{24,28},{28,24},{1,5},{5... | collective-permute-start | bytes 393224 | tf_op jit(solution)/shard_map/ppermute | solution.py:119
  7.4 0.0 copy-start
  7.4 1.5 %copy-done = bf16[16,7,64,64]{3,2,1,0:T(8,128)(2,1)S(1)} copy-done((bf16[16,7,64,64]{3,2,1,0:T(8,128)(2,1)S(1)}, bf16[16,7,64,64]{3,2,1,0:T(8,128)(2,1)}, u32[]{:S(2)}) %copy-start) | copy-done | bytes 917528
  8.9 0.0 copy-start.2
  8.9 0.7 %copy-done.2 = s32[16,7]{0,1:T(8,128)S(1)} copy-done((s32[16,7]{0,1:T(8,128)S(1)}, s32[16,7]{0,1:T(8,128)}, u32[]{:S(2)}) %copy-start.2) | copy-done | bytes 472
  9.6 0.0 copy-start.3
  9.6 0.7 %copy-done.3 = s32[16,7]{0,1:T(8,128)S(1)} copy-done((s32[16,7]{0,1:T(8,128)S(1)}, s32[16,7]{0,1:T(8,128)}, u32[]{:S(2)}) %copy-start.3) | copy-done | bytes 472
  10.3 0.0 copy-start.4
  10.3 0.7 %copy-done.4 = s32[16]{0:T(128)S(1)} copy-done((s32[16]{0:T(128)S(1)}, s32[16]{0:T(128)}, u32[]{:S(2)}) %copy-start.4) | copy-done | bytes 88
  11.0 0.0 copy-start.5
  11.0 0.7 %copy-done.5 = s32[16]{0:T(128)S(1)} copy-done((s32[16]{0:T(128)S(1)}, s32[16]{0:T(128)}, u32[]{:S(2)}) %copy-start.5) | copy-done | bytes 88
  11.6 2.3 %prep.1 = (bf16[112,64,64]{2,1,0:T(8,128)(2,1)S(1)}, bf16[16,64,64]{2,1,0:T(8,128)(2,1)S(1)}, s32[112]{0:T(128)S(1)}) custom-call(s32[7,16]{1,0:T(8,128)S(1)} %bitcast.4, s32[16]{0:T(128)S(1)} %copy-done.4, s32[16]{0:T(128)S(1)} %copy-done.5, s32[7,16]{1,0:T(8,128)S(1)} %bitcast.5, bf16[112,64,64]{2,1,0:T(8,128)(2,1)S(1)} %bitcast.3, ...), custom_call_target="tpu_custom_call" | custom-call | bytes 4194304 | tf_op jit(solution)/shard_map/prep/pallas_call | solution.py:120
  13.9 0.0 collective-permute-done.far_ref
  13.9 3.5 %collective-permute-start.3 = (bf16[16,32,128]{2,1,0:T(8,128)(2,1)S(1)}, bf16[16,32,128]{2,1,0:T(8,128)(2,1)S(1)}, u32[]{:S(2)}, u32[]{:S(2)}) collective-permute-start(bf16[16,32,128]{2,1,0:T(8,128)(2,1)S(1)} %collective-permute-done.far_ref), channel_id=1, source_target_pairs={{0,8},{8,16},{16,24},{12,4},{20,12},{28,20},{1,9},{9,17},{17,25},{... | collective-permute-start | bytes 393224 | tf_op jit(solution)/shard_map/ppermute | solution.py:152
  17.4 3.4 %collective-permute-done.3.other_ref = bf16[16,32,128]{2,1,0:T(8,128)(2,1)S(1)} collective-permute-done((bf16[16,32,128]{2,1,0:T(8,128)(2,1)S(1)}, bf16[16,32,128]{2,1,0:T(8,128)(2,1)S(1)}, u32[]{:S(2)}, u32[]{:S(2)}) %collective-permute-start.3) | collective-permute-done | bytes 131104 | tf_op jit(solution)/shard_map/ppermute | solution.py:152
  20.8 0.1 collective-permute-start.5
  20.9 3.0 %collective-permute-start.4 = (bf16[32,32,128]{2,1,0:T(8,128)(2,1)S(1)}, bf16[32,32,128]{2,1,0:T(8,128)(2,1)S(1)}, u32[]{:S(2)}, u32[]{:S(2)}) collective-permute-start(bf16[32,32,128]{2,1,0:T(8,128)(2,1)S(1)} %constant_dynamic-update-slice_fusion), channel_id=1, source_target_pairs={{64,32},{128,96},{192,160},{32,64},{96,128},{160,192},{65,33},{129... | collective-permute-start | bytes 786440 | tf_op jit(solution)/shard_map/ppermute | solution.py:145
  23.9 0.4 collective-permute-start.2
  24.3 2.3 %collective-permute-start.1 = (bf16[16,32,128]{2,1,0:T(8,128)(2,1)S(1)}, bf16[16,32,128]{2,1,0:T(8,128)(2,1)S(1)}, u32[]{:S(2)}, u32[]{:S(2)}) collective-permute-start(bf16[16,32,128]{2,1,0:T(8,128)(2,1)S(1)} %pack.1.packed_ref.own_p), channel_id=1, source_target_pairs={{64,32},{128,96},{192,160},{32,64},{96,128},{160,192},{65,33},{129... | collective-permute-start | bytes 393224 | tf_op jit(solution)/shard_map/ppermute | solution.py:145
  26.6 0.0 collective-permute-done.2.high_p
  26.6 4.0 %collective-permute-done.1.low_p = bf16[16,32,128]{2,1,0:T(8,128)(2,1)S(1)} collective-permute-done((bf16[16,32,128]{2,1,0:T(8,128)(2,1)S(1)}, bf16[16,32,128]{2,1,0:T(8,128)(2,1)S(1)}, u32[]{:S(2)}, u32[]{:S(2)}) %collective-permute-start.1) | collective-permute-done | bytes 131104 | tf_op jit(solution)/shard_map/ppermute | solution.py:145
  30.5 0.0 collective-permute-done.5.high_ref
  30.5 0.0 collective-permute-done.4.low_ref
  30.5 2.2 %galerkin.1 = (f32[28,32,128]{2,1,0:T(8,128)S(1)}, bf16[28,32,128]{2,1,0:T(8,128)(2,1)S(1)}, bf16[28,32,128]{2,1,0:T(8,128)(2,1)S(1)}, bf16[28,32,128]{2,1,0:T(8,128)(2,1)S(1)}) custom-call(s32[112]{0:T(128)S(1)} %get-tuple-element.15.table_ref, bf16[112,64,64]{2,1,0:T(8,128)(2,1)S(1)} %get-tuple-element.16.blocks_ref, ...), custom_call_target="tpu_custom_call" | custom-call | tf_op jit(solution)/shard_map/galerkin/pallas_call | solution.py:157
  32.8 1.6 %collective-permute-start.6 = (bf16[28,32,128]{2,1,0:T(8,128)(2,1)S(1)}, bf16[28,32,128]{2,1,0:T(8,128)(2,1)S(1)}, u32[]{:S(2)}, u32[]{:S(2)}) collective-permute-start(bf16[28,32,128]{2,1,0:T(8,128)(2,1)S(1)} %get-tuple-element.22), channel_id=1, source_target_pairs={{0,1},{1,2},{2,3},{3,0},{4,5},{5,6},{6,7},{7,4},{8,9},{9,10},{10,1... | collective-permute-start | bytes 688136 | tf_op jit(solution)/shard_map/ppermute | solution.py:170
  34.3 2.8 %collective-permute-start.7 = (bf16[28,32,128]{2,1,0:T(8,128)(2,1)S(1)}, bf16[28,32,128]{2,1,0:T(8,128)(2,1)S(1)}, u32[]{:S(2)}, u32[]{:S(2)}) collective-permute-start(bf16[28,32,128]{2,1,0:T(8,128)(2,1)S(1)} %get-tuple-element.23), channel_id=1, source_target_pairs={{0,2},{1,3},{2,0},{3,1},{4,6},{5,7},{6,4},{7,5},{8,10},{9,11},{10,... | collective-permute-start | bytes 688136 | tf_op jit(solution)/shard_map/ppermute | solution.py:170
  37.1 1.4 %collective-permute-start.8 = (bf16[28,32,128]{2,1,0:T(8,128)(2,1)S(1)}, bf16[28,32,128]{2,1,0:T(8,128)(2,1)S(1)}, u32[]{:S(2)}, u32[]{:S(2)}) collective-permute-start(bf16[28,32,128]{2,1,0:T(8,128)(2,1)S(1)} %get-tuple-element.24), channel_id=1, source_target_pairs={{0,3},{1,0},{2,1},{3,2},{4,7},{5,4},{6,5},{7,6},{8,11},{9,8},{10,9... | collective-permute-start | bytes 688136 | tf_op jit(solution)/shard_map/ppermute | solution.py:170
  38.5 3.3 %collective-permute-done.6.one_ref = bf16[28,32,128]{2,1,0:T(8,128)(2,1)S(1)} collective-permute-done((bf16[28,32,128]{2,1,0:T(8,128)(2,1)S(1)}, bf16[28,32,128]{2,1,0:T(8,128)(2,1)S(1)}, u32[]{:S(2)}, u32[]{:S(2)}) %collective-permute-start.6) | collective-permute-done | bytes 229408 | tf_op jit(solution)/shard_map/ppermute | solution.py:170
  41.8 6.0 %collective-permute-done.7.two_ref = bf16[28,32,128]{2,1,0:T(8,128)(2,1)S(1)} collective-permute-done((bf16[28,32,128]{2,1,0:T(8,128)(2,1)S(1)}, bf16[28,32,128]{2,1,0:T(8,128)(2,1)S(1)}, u32[]{:S(2)}, u32[]{:S(2)}) %collective-permute-start.7) | collective-permute-done | bytes 229408 | tf_op jit(solution)/shard_map/ppermute | solution.py:170
  47.8 0.0 collective-permute-done.8.three_ref
  47.8 1.1 %total.1 = f32[4,7,64,64]{3,2,1,0:T(8,128)} custom-call(f32[28,32,128]{2,1,0:T(8,128)S(1)} %get-tuple-element.21.own_ref, bf16[28,32,128]{2,1,0:T(8,128)(2,1)S(1)} %collective-permute-done.6.one_ref, bf16[28,32,128]{2,1,0:T(8,128)(2,1)S(1)} %collective-permute-done.7.two_ref, bf16[28,32,128]{2,1,0:T(8,128)(2,1)S(1)} %collective-permute-done.8.three_ref), custom_call_target="tpu_custom_call" | custom-call | tf_op jit(solution)/shard_map/total/pallas_call | solution.py:173
  (2 shorter events, 0.0 us)
Async XLA Ops:
  0.0 0.9 %copy-start.1 = (bf16[16,64,64]{2,1,0:T(8,128)(2,1)S(1)}, bf16[16,64,64]{2,1,0:T(8,128)(2,1)}, u32[]{:S(2)}) copy-start(bf16[16,64,64]{2,1,0:T(8,128)(2,1)} %prolong_ref.1) | copy-start | bytes 393220
  1.1 12.8 %collective-permute-start = (bf16[16,32,128]{2,1,0:T(8,128)(2,1)S(1)}, bf16[16,32,128]{2,1,0:T(8,128)(2,1)S(1)}, u32[]{:S(2)}, u32[]{:S(2)}) collective-permute-start(bf16[16,32,128]{2,1,0:T(8,128)(2,1)S(1)} %pack.1.packed_ref.own_p), channel_id=1, source_target_pairs={{0,4},{4,0},{8,12},{12,8},{16,20},{20,16},{24,28},{28,24},{1,5},{5... | collective-permute-start | bytes 393224 | tf_op jit(solution)/shard_map/ppermute | solution.py:119
  7.4 1.5 %copy-start = (bf16[16,7,64,64]{3,2,1,0:T(8,128)(2,1)S(1)}, bf16[16,7,64,64]{3,2,1,0:T(8,128)(2,1)}, u32[]{:S(2)}) copy-start(bf16[16,7,64,64]{3,2,1,0:T(8,128)(2,1)} %param.6) | copy-start | bytes 2752516
  8.9 0.7 %copy-start.2 = (s32[16,7]{0,1:T(8,128)S(1)}, s32[16,7]{0,1:T(8,128)}, u32[]{:S(2)}) copy-start(s32[16,7]{0,1:T(8,128)} %param.7) | copy-start | bytes 1348
  9.6 0.7 %copy-start.3 = (s32[16,7]{0,1:T(8,128)S(1)}, s32[16,7]{0,1:T(8,128)}, u32[]{:S(2)}) copy-start(s32[16,7]{0,1:T(8,128)} %param.10) | copy-start | bytes 1348
  10.3 0.7 %copy-start.4 = (s32[16]{0:T(128)S(1)}, s32[16]{0:T(128)}, u32[]{:S(2)}) copy-start(s32[16]{0:T(128)} %counts_hbm.1) | copy-start | bytes 196
  11.0 0.7 %copy-start.5 = (s32[16]{0:T(128)S(1)}, s32[16]{0:T(128)}, u32[]{:S(2)}) copy-start(s32[16]{0:T(128)} %agg_hbm.1) | copy-start | bytes 196
  13.9 6.9 %collective-permute-start.3 = (bf16[16,32,128]{2,1,0:T(8,128)(2,1)S(1)}, bf16[16,32,128]{2,1,0:T(8,128)(2,1)S(1)}, u32[]{:S(2)}, u32[]{:S(2)}) collective-permute-start(bf16[16,32,128]{2,1,0:T(8,128)(2,1)S(1)} %collective-permute-done.far_ref), channel_id=1, source_target_pairs={{0,8},{8,16},{16,24},{12,4},{20,12},{28,20},{1,9},{9,17},{17,25},{... | collective-permute-start | bytes 393224 | tf_op jit(solution)/shard_map/ppermute | solution.py:152
  20.8 9.7 %collective-permute-start.5 = (bf16[32,32,128]{2,1,0:T(8,128)(2,1)S(1)}, bf16[32,32,128]{2,1,0:T(8,128)(2,1)S(1)}, u32[]{:S(2)}, u32[]{:S(2)}) collective-permute-start(bf16[32,32,128]{2,1,0:T(8,128)(2,1)S(1)} %constant_dynamic-update-slice_fusion), channel_id=1, source_target_pairs={{0,32},{32,0},{64,96},{96,64},{128,160},{160,128},{192,224},{224,1... | collective-permute-start | bytes 786440 | tf_op jit(solution)/shard_map/ppermute | solution.py:145
  20.9 9.6 %collective-permute-start.4 = (bf16[32,32,128]{2,1,0:T(8,128)(2,1)S(1)}, bf16[32,32,128]{2,1,0:T(8,128)(2,1)S(1)}, u32[]{:S(2)}, u32[]{:S(2)}) collective-permute-start(bf16[32,32,128]{2,1,0:T(8,128)(2,1)S(1)} %constant_dynamic-update-slice_fusion), channel_id=1, source_target_pairs={{64,32},{128,96},{192,160},{32,64},{96,128},{160,192},{65,33},{129... | collective-permute-start | bytes 786440 | tf_op jit(solution)/shard_map/ppermute | solution.py:145
  23.9 2.7 %collective-permute-start.2 = (bf16[16,32,128]{2,1,0:T(8,128)(2,1)S(1)}, bf16[16,32,128]{2,1,0:T(8,128)(2,1)S(1)}, u32[]{:S(2)}, u32[]{:S(2)}) collective-permute-start(bf16[16,32,128]{2,1,0:T(8,128)(2,1)S(1)} %pack.1.packed_ref.own_p), channel_id=1, source_target_pairs={{0,32},{32,0},{64,96},{96,64},{128,160},{160,128},{192,224},{224,1... | collective-permute-start | bytes 393224 | tf_op jit(solution)/shard_map/ppermute | solution.py:145
  24.3 6.3 %collective-permute-start.1 = (bf16[16,32,128]{2,1,0:T(8,128)(2,1)S(1)}, bf16[16,32,128]{2,1,0:T(8,128)(2,1)S(1)}, u32[]{:S(2)}, u32[]{:S(2)}) collective-permute-start(bf16[16,32,128]{2,1,0:T(8,128)(2,1)S(1)} %pack.1.packed_ref.own_p), channel_id=1, source_target_pairs={{64,32},{128,96},{192,160},{32,64},{96,128},{160,192},{65,33},{129... | collective-permute-start | bytes 393224 | tf_op jit(solution)/shard_map/ppermute | solution.py:145
  32.8 9.0 %collective-permute-start.6 = (bf16[28,32,128]{2,1,0:T(8,128)(2,1)S(1)}, bf16[28,32,128]{2,1,0:T(8,128)(2,1)S(1)}, u32[]{:S(2)}, u32[]{:S(2)}) collective-permute-start(bf16[28,32,128]{2,1,0:T(8,128)(2,1)S(1)} %get-tuple-element.22), channel_id=1, source_target_pairs={{0,1},{1,2},{2,3},{3,0},{4,5},{5,6},{6,7},{7,4},{8,9},{9,10},{10,1... | collective-permute-start | bytes 688136 | tf_op jit(solution)/shard_map/ppermute | solution.py:170
  34.3 13.4 %collective-permute-start.7 = (bf16[28,32,128]{2,1,0:T(8,128)(2,1)S(1)}, bf16[28,32,128]{2,1,0:T(8,128)(2,1)S(1)}, u32[]{:S(2)}, u32[]{:S(2)}) collective-permute-start(bf16[28,32,128]{2,1,0:T(8,128)(2,1)S(1)} %get-tuple-element.23), channel_id=1, source_target_pairs={{0,2},{1,3},{2,0},{3,1},{4,6},{5,7},{6,4},{7,5},{8,10},{9,11},{10,... | collective-permute-start | bytes 688136 | tf_op jit(solution)/shard_map/ppermute | solution.py:170
  37.1 10.7 %collective-permute-start.8 = (bf16[28,32,128]{2,1,0:T(8,128)(2,1)S(1)}, bf16[28,32,128]{2,1,0:T(8,128)(2,1)S(1)}, u32[]{:S(2)}, u32[]{:S(2)}) collective-permute-start(bf16[28,32,128]{2,1,0:T(8,128)(2,1)S(1)} %get-tuple-element.24), channel_id=1, source_target_pairs={{0,3},{1,0},{2,1},{3,2},{4,7},{5,4},{6,5},{7,6},{8,11},{9,8},{10,9... | collective-permute-start | bytes 688136 | tf_op jit(solution)/shard_map/ppermute | solution.py:170

commit v3 on v2

v3 whole, which is shorter than its diff:
```python
import jax
import jax.numpy as jnp
from jax import lax
from jax.experimental import pallas as pl
from jax.experimental.pallas import tpu as pltpu
from jax.sharding import PartitionSpec as P

SC = 28
PART = 7
ALL = ("row", "col", "depth")
HBM = pl.BlockSpec(memory_space=pltpu.HBM)
VMEM = pl.BlockSpec(memory_space=pltpu.VMEM)
SMEM = pl.BlockSpec(memory_space=pltpu.SMEM)
LIMIT = pltpu.CompilerParams(vmem_limit_bytes=16 * 2**20)
BATCH = 40
SMALL = pl.CostEstimate(flops=1000, bytes_accessed=1000, transcendentals=0)
LIST = 288
CUTS = 4
MOVED = 8
SEND, OWN = range(2)
TRASH = 2 * SC


def fold(block):
    half = block.shape[0] // 2
    return jnp.concatenate([block[:half], block[half:]], axis=1)


def unfold(block):
    half = block.shape[1] // 2
    return jnp.concatenate([block[:, :half], block[:, half:]], axis=0)


def pack_kernel(prolong_ref, ints_ref, out_ref):
    for i in range(prolong_ref.shape[0]):
        out_ref[i] = fold(prolong_ref[i])


def blocks_kernel(blocks_hbm, packed_ref, ints_ref, first_ref, second_ref, turned_ref, blocks_ref, sems):
    half = first_ref.shape[0] - 1
    size = 2 * half // CUTS
    copies = [
        pltpu.make_async_copy(blocks_hbm.at[pl.ds(c * size, size)], blocks_ref.at[pl.ds(c * size, size)], sems.at[c])
        for c in range(CUTS)
    ]
    for copy in copies:
        copy.start()
    ints = ints_ref[...]
    coded = jnp.concatenate([ints >> 4, ints & 15], axis=0).astype(jnp.float32).astype(first_ref.dtype)
    for out in (first_ref, second_ref):
        out[half] = jnp.zeros(out.shape[1:], out.dtype)
        out[half, :, 0 : ints.shape[1]] = coded
    for i in range(packed_ref.shape[0]):
        turned_ref[i] = unfold(packed_ref[i]).T
    for c, copy in enumerate(copies):
        copy.wait()
        for n in range(c * size, (c + 1) * size):
            if n < half:
                first_ref[n] = fold(blocks_ref[n])
            else:
                second_ref[n - half] = fold(blocks_ref[n])


def entries_of(ints, depth, source, rel_b, row_ok, shift):
    count, agg = ints[2 * PART : 2 * PART + 1], ints[2 * PART + 1 : 2 * PART + 2]
    j, k = ints[:PART], ints[PART : 2 * PART]
    i = lax.broadcasted_iota(jnp.int32, j.shape, 1)
    s = lax.broadcasted_iota(jnp.int32, j.shape, 0)
    home_r, home_c = lax.axis_index("row"), lax.axis_index("col")
    across, flip = 1 - 2 * (home_c & 1), 1 - 2 * (home_r & 1)
    dest = (k * 37) >> 8
    rel = (dest - depth) & 3
    valid = ((rel == 0) | (rel == rel_b)) & (source * PART + s < count) & row_ok
    target = (jnp.where(rel == 3, PART, 0) + k - dest * PART) * 4 + agg
    dr = ((j >> 7) - home_r) * flip
    dc = ((j >> 4) & 7) - home_c
    side = jnp.where(dc == 0, 0, jnp.where(dc == across, 1, 2))
    place = side + 3 * jnp.where(dr == 0, 0, (dr + 3) >> 1)
    entry = (((((i << 8) + shift + i * PART + s) << 8) + place * 16 + (j & 15)) << 8) + target
    kind = jnp.where(rel == 0, OWN, SEND)
    return entry + jnp.where(valid, 1 << (28 + kind), 0)


def decoded(piece, rows):
    values = piece[:, :rows].astype(jnp.float32).astype(jnp.int32)
    return values[: values.shape[0] // 2] * 16 + values[values.shape[0] // 2 :]


def exact_dot(a, b):
    return jnp.dot(a.astype(jnp.bfloat16), b.astype(jnp.bfloat16), preferred_element_type=jnp.float32)


def make_lists(own_ref, prev_ref, next_ref, list_ref, sizes_ref, words_ref, places_ref, word_table, place_table, sems):
    rows = own_ref.shape[1]
    depth = lax.axis_index("depth")
    lane = lax.broadcasted_iota(jnp.int32, (PART, rows), 1)
    first = lane < rows // 2
    before, after = (depth + 3) & 3, (depth + 1) & 3
    own = entries_of(own_ref[...], depth, depth, jnp.where(first, 3, 1), lane >= 0, 0)
    from_prev = entries_of(decoded(prev_ref[prev_ref.shape[0] - 1], rows), depth, before, 1, first, rows * PART)
    from_next = entries_of(decoded(next_ref[next_ref.shape[0] - 1], rows), depth, after, 3, ~first, rows * PART)
    words_ref[...] = jnp.zeros_like(words_ref)
    words_ref[0:PART, 0:rows] = own
    words_ref[8 : 8 + PART, 0:rows] = jnp.where(first, from_prev, from_next)
    words = words_ref[...]
    lanes = words.shape[1]
    earlier = lax.broadcasted_iota(jnp.int32, (lanes, lanes), 0) < lax.broadcasted_iota(jnp.int32, (lanes, lanes), 1)
    above = lax.broadcasted_iota(jnp.int32, (16, 16), 0) > lax.broadcasted_iota(jnp.int32, (16, 16), 1)
    earlier, above = earlier.astype(jnp.float32), above.astype(jnp.float32)
    row = lax.broadcasted_iota(jnp.int32, words.shape, 0)
    places = jnp.full(words.shape, 2 * LIST, jnp.int32)
    for kind in range(2):
        here = (words >> (28 + kind)) & 1
        member = here.astype(jnp.float32)
        count = jnp.sum(member, axis=1, keepdims=True) + jnp.zeros_like(member)
        place = (exact_dot(member, earlier) + exact_dot(above, count)).astype(jnp.int32)
        total = jnp.sum(count, axis=0, keepdims=True).astype(jnp.int32)
        places = jnp.where(here == 1, place + kind * LIST, places)
        places = jnp.where(row == 7 + 8 * kind, total, places)
    places_ref[...] = places
    copies = [
        pltpu.make_async_copy(words_ref, word_table, sems.at[0]),
        pltpu.make_async_copy(places_ref, place_table, sems.at[1]),
    ]
    for copy in copies:
        copy.start()
    for copy in copies:
        copy.wait()

    def row_step(i, carry):
        for s in range(2 * PART):
            at = s + s // PART
            list_ref[place_table[at, i]] = word_table[at, i]
        return carry

    lax.fori_loop(0, rows, row_step, 0)
    for kind in range(2):
        size = place_table[7 + 8 * kind, 0]
        for p in range(BATCH):
            list_ref[kind * LIST + size + p] = TRASH
        sizes_ref[kind] = size


def run_list(list_ref, sizes_ref, kind, blocks_ref, turned_ref, halo_ref, acc_ref):
    def step(b, carry):
        entries = [list_ref[kind * LIST + b * BATCH + p] for p in range(BATCH)]
        products = [
            jnp.dot(
                unfold(blocks_ref[(e >> 16) & 255]), unfold(halo_ref[(e >> 8) & 255]), preferred_element_type=jnp.float32
            ).astype(jnp.bfloat16)
            for e in entries
        ]
        for e, product in zip(entries, products):
            term = jnp.dot(turned_ref[(e >> 24) & 15], product, preferred_element_type=jnp.float32)
            acc_ref[e & 255] += fold(term)
        return carry

    lax.fori_loop(0, lax.div(sizes_ref[kind] + (BATCH - 1), BATCH), step, 0)


def early_kernel(ints_ref, first_ref, second_ref, prev_ref, next_ref, packed_ref, far_ref, other_ref,
                 list_ref, sizes_ref, blocks_ref, halo_ref, words_ref, places_ref, word_table, place_table, sems):
    make_lists(ints_ref, prev_ref, next_ref, list_ref, sizes_ref, words_ref, places_ref, word_table, place_table, sems)
    half = first_ref.shape[0] - 1
    for at, part in enumerate((first_ref, second_ref, prev_ref, next_ref)):
        blocks_ref[pl.ds(at * half, half)] = part[0:half]
    rows = packed_ref.shape[0]
    for at, part in enumerate((packed_ref, far_ref, other_ref)):
        halo_ref[pl.ds(at * rows, part.shape[0])] = part[...]


def late_kernel(list_ref, sizes_ref, blocks_ref, turned_ref, chip_pair, core_pair, chip_ref, core_ref, halo_in,
                halo_ref, after_ref, before_ref, acc_ref):
    rows = halo_ref.shape[0] // 9
    for at, (one, two) in ((3, (chip_pair, chip_ref)), (6, (core_pair, core_ref))):
        halo_ref[pl.ds(at * rows, rows - MOVED)] = one[rows:]
        halo_ref[pl.ds((at + 1) * rows - MOVED, MOVED)] = two[rows:]
        halo_ref[pl.ds((at + 1) * rows, rows)] = one[0:rows]
        halo_ref[pl.ds((at + 2) * rows, rows)] = two[0:rows]
    acc_ref[...] = jnp.zeros_like(acc_ref)
    run_list(list_ref, sizes_ref, SEND, blocks_ref, turned_ref, halo_ref, acc_ref)
    after_ref[...] = acc_ref[0:SC].astype(after_ref.dtype)
    before_ref[...] = acc_ref[SC : 2 * SC].astype(before_ref.dtype)


def own_kernel(list_ref, sizes_ref, blocks_ref, turned_ref, halo_ref, acc_ref):
    acc_ref[...] = jnp.zeros_like(acc_ref)
    run_list(list_ref, sizes_ref, OWN, blocks_ref, turned_ref, halo_ref, acc_ref)


def sum_kernel(own_ref, one_ref, two_ref, out_hbm, total_ref, sems):
    aggs, slots = total_ref.shape[:2]
    copies = []
    for a in range(aggs):
        for s in range(slots):
            at = s * aggs + a
            total = own_ref[at] + (one_ref[at].astype(jnp.float32) + two_ref[at].astype(jnp.float32))
            total_ref[a, s] = unfold(total)
        copies.append(pltpu.make_async_copy(total_ref.at[a], out_hbm.at[a], sems.at[a]))
        copies[-1].start()
    for copy in copies:
        copy.wait()


def per_device(blocks, columns, counts, aggregate, coarse_slot, prolong):
    rows, slots, width, _ = blocks.shape
    n_row, n_col, n_depth = (lax.axis_size(a) for a in ALL)
    piece = (width // 2, 2 * width)
    bf16 = jnp.bfloat16
    tie = lax.optimization_barrier

    def struct(*shape, dtype=bf16):
        return jax.ShapeDtypeStruct(shape, dtype)

    ints = jnp.concatenate([columns.T, coarse_slot.T, counts[None], aggregate[None]], axis=0)
    packed = pl.pallas_call(
        pack_kernel, out_shape=struct(rows, *piece), in_specs=[VMEM, HBM], out_specs=VMEM, compiler_params=LIMIT, name="pack"
    )(prolong, ints)
    far = lax.ppermute(packed, "col", [(c, c ^ 1) for c in range(n_col)])

    half = rows * slots // 2
    first, second, turned = pl.pallas_call(
        blocks_kernel,
        out_shape=[struct(half + 1, *piece), struct(half + 1, *piece), struct(rows, width, width)],
        in_specs=[HBM, VMEM, VMEM],
        out_specs=[VMEM] * 3,
        scratch_shapes=[pltpu.VMEM((rows * slots, width, width), bf16), pltpu.SemaphoreType.DMA((CUTS,))],
        compiler_params=LIMIT,
        cost_estimate=SMALL,
        name="blocks",
    )(pltpu.with_memory_space_constraint(blocks.reshape(rows * slots, width, width), pltpu.HBM), packed, ints)
    up = [(d, (d + 1) % n_depth) for d in range(n_depth)]
    down = [(b, a) for a, b in up]
    from_prev, from_next = lax.ppermute(first, "depth", up), lax.ppermute(second, "depth", down)

    core = [(r, r ^ 1) for r in range(n_row)]
    chip = [(r, r - 1) for r in range(2, n_row, 2)] + [(r, r + 1) for r in range(1, n_row - 1, 2)]

    far, turned = tie((far, turned))
    fetch = [(c - 2, c) for c in range(2, n_col, 2)] + [(c + 2, c) for c in range(1, n_col - 2, 2)]
    other = lax.ppermute(far, "col", fetch)
    pair = jnp.concatenate([far, packed[: rows - MOVED]], axis=0)
    other_and = jnp.concatenate([other, packed[rows - MOVED :]], axis=0)
    chip_pair, core_pair = lax.ppermute(pair, "row", chip), lax.ppermute(pair, "row", core)
    chip_other, core_other = lax.ppermute(other_and, "row", chip), lax.ppermute(other_and, "row", core)

    sends = struct(TRASH + 1, *piece, dtype=jnp.float32)
    halos = struct(9 * rows, *piece)
    entries, sizes, all_blocks, halo = pl.pallas_call(
        early_kernel,
        out_shape=[
            struct(2 * LIST + 1, dtype=jnp.int32),
            struct(2, dtype=jnp.int32),
            struct(2 * rows * slots, *piece),
            halos,
        ],
        in_specs=[VMEM] * 8,
        out_specs=[SMEM] * 2 + [VMEM] * 2,
        scratch_shapes=[
            pltpu.VMEM((16, 128), jnp.int32),
            pltpu.VMEM((16, 128), jnp.int32),
            pltpu.SMEM((16, 128), jnp.int32),
            pltpu.SMEM((16, 128), jnp.int32),
            pltpu.SemaphoreType.DMA((2,)),
        ],
        compiler_params=LIMIT,
        name="early",
    )(ints, first, second, from_prev, from_next, packed, far, other)
    halo, after, before = pl.pallas_call(
        late_kernel,
        out_shape=[halos, struct(SC, *piece), struct(SC, *piece)],
        in_specs=[SMEM] * 2 + [VMEM] * 7,
        out_specs=[VMEM] * 3,
        scratch_shapes=[pltpu.VMEM((TRASH + 1, *piece), jnp.float32)],
        input_output_aliases={8: 0},
        compiler_params=LIMIT,
        name="late",
    )(entries, sizes, all_blocks, turned, chip_pair, core_pair, chip_other, core_other, halo)
    got_prev, got_next = lax.ppermute(after, "depth", up), lax.ppermute(before, "depth", down)
    own = pl.pallas_call(
        own_kernel,
        out_shape=sends,
        in_specs=[SMEM] * 2 + [VMEM] * 3,
        out_specs=VMEM,
        compiler_params=LIMIT,
        name="own",
    )(entries, sizes, all_blocks, turned, halo)
    return pl.pallas_call(
        sum_kernel,
        out_shape=struct(4, SC // n_depth, width, width, dtype=jnp.float32),
        in_specs=[VMEM] * 3,
        out_specs=HBM,
        scratch_shapes=[
            pltpu.VMEM((4, SC // n_depth, width, width), jnp.float32),
            pltpu.SemaphoreType.DMA((4,)),
        ],
        compiler_params=LIMIT,
        name="total",
    )(own, got_prev, got_next)


def solution(mesh):
    in_specs = (
        P(("row", "col"), "depth", None, None),
        P(("row", "col"), "depth"),
        P(("row", "col")),
        P(("row", "col")),
        P(("row", "col"), "depth"),
        P(("row", "col"), None, None),
    )
    out_specs = P(("row", "col"), "depth", None, None)
    return jax.shard_map(per_device, mesh=mesh, in_specs=in_specs, out_specs=out_specs, check_vma=False)
```

time: 49.1 us -> 42.2 us (0.86)
  the two profiles are of different devices: /device:TPU:40 before, /device:TPU:1 now
where the time goes in v3:
time: 42.2 us; the launch traced here: 42 us
  starting transfers between devices  25.7 us (61%)
  Pallas kernels  9.16 us (22%)
  waiting for transfers between devices  5.22 us (12%)
  local copies, waits for them, and re-layouts  0.96 us (2%)
  other arithmetic  0.79 us (2%)
    ppermute x1, starting transfers between devices, per_device(): far = lax.ppermute(packed, 'col', [(c, c ^ 1) for c in range(n_col)])  7.83 us
    ppermute x1, starting transfers between devices, per_device(): lax.ppermute(pair, 'row', chip)  5.62 us
    ppermute x1, waiting for transfers between devices, per_device(): lax.ppermute(after, 'depth', up)  3.4 us
    ppermute x1, starting transfers between devices, per_device(): lax.ppermute(other_and, 'row', chip)  3.37 us
    ppermute x1, starting transfers between devices, per_device(): other = lax.ppermute(far, 'col', fetch)  3.2 us
    pallas_call x1, Pallas kernels, per_device(): pl.pallas_call(late_kernel, out_shape=[halos, struct(SC, *piece), struct(...  2.14 us
    pallas_call x1, Pallas kernels, per_device(): pl.pallas_call(early_kernel, out_shape=[struct(2 * LIST + 1, dtype=jnp.in...  2.08 us
    pallas_call x1, Pallas kernels, per_device(): pl.pallas_call(own_kernel, out_shape=sends, in_specs=[SMEM] * 2 + [VMEM]...  2.05 us
  transfers between devices with their start and end apart: 10, of which 3 were waited for; matrix products, arithmetic and copies ran while one was open for 0% of the time, Pallas kernels for 14%

profile of v3, /device:TPU:1, one launch (start us, length us, event | category | flops | bytes accessed | tf_op | source)
XLA Modules:
  0.0 42.0 jit_solution(12500788970312059006)
XLA Ops:
  0.0 0.7 %pad_add_fusion.ints_ref = s32[16,16]{1,0:T(8,128)S(1)} fusion(s32[1,16]{1,0:T(1,128)} %bitcast.8, s32[1,16]{1,0:T(1,128)} %bitcast.9, s32[7,16]{1,0:T(8,128)} %bitcast.6, s32[7,16]{1,0:T(8,128)} %bitcast.7), kind=kLoop, calls=%fused_computation.2 | loop fusion | flops 768 | bytes 2048 | tf_op jit(solution)/shard_map/concatenate | solution.py:215
  0.7 0.0 copy-start
  0.8 0.9 %copy-done = bf16[16,64,64]{2,1,0:T(8,128)(2,1)S(1)} copy-done((bf16[16,64,64]{2,1,0:T(8,128)(2,1)S(1)}, bf16[16,64,64]{2,1,0:T(8,128)(2,1)}, u32[]{:S(2)}) %copy-start) | copy-done | bytes 131096
  1.7 0.1 pack.1.packed_ref
  1.8 7.8 %collective-permute-start.2 = (bf16[16,32,128]{2,1,0:T(8,128)(2,1)S(1)}, bf16[16,32,128]{2,1,0:T(8,128)(2,1)S(1)}, u32[]{:S(2)}, u32[]{:S(2)}) collective-permute-start(bf16[16,32,128]{2,1,0:T(8,128)(2,1)S(1)} %pack.1.packed_ref), channel_id=1, source_target_pairs={{0,4},{4,0},{8,12},{12,8},{16,20},{20,16},{24,28},{28,24},{1,5},{5... | collective-permute-start | bytes 393224 | tf_op jit(solution)/shard_map/ppermute | solution.py:219
  9.6 1.7 %blocks.1 = (bf16[57,32,128]{2,1,0:T(8,128)(2,1)S(1)}, bf16[57,32,128]{2,1,0:T(8,128)(2,1)S(1)}, bf16[16,64,64]{2,1,0:T(8,128)(2,1)S(1)}) custom-call(bf16[112,64,64]{2,1,0:T(8,128)(2,1)} %bitcast.5, bf16[16,32,128]{2,1,0:T(8,128)(2,1)S(1)} %pack.1.packed_ref, s32[16,16]{1,0:T(8,128)S(1)} %pad_add_fusion.ints_ref), custom_call_target="tpu_custom_call" | custom-call | flops 1000 | bytes 1000 | tf_op jit(solution)/shard_map/blocks/pallas_call | solution.py:222
  11.4 1.3 %collective-permute-start = (bf16[57,32,128]{2,1,0:T(8,128)(2,1)S(1)}, bf16[57,32,128]{2,1,0:T(8,128)(2,1)S(1)}, u32[]{:S(2)}, u32[]{:S(2)}) collective-permute-start(bf16[57,32,128]{2,1,0:T(8,128)(2,1)S(1)} %get-tuple-element.17.first_ref), channel_id=1, source_target_pairs={{0,1},{1,2},{2,3},{3,0},{4,5},{5,6},{6,7},{7,4},{8,9},{9,10},{10,1... | collective-permute-start | bytes 1400840 | tf_op jit(solution)/shard_map/ppermute | solution.py:234
  12.7 1.5 %collective-permute-start.1 = (bf16[57,32,128]{2,1,0:T(8,128)(2,1)S(1)}, bf16[57,32,128]{2,1,0:T(8,128)(2,1)S(1)}, u32[]{:S(2)}, u32[]{:S(2)}) collective-permute-start(bf16[57,32,128]{2,1,0:T(8,128)(2,1)S(1)} %get-tuple-element.18.second_ref), channel_id=1, source_target_pairs={{1,0},{2,1},{3,2},{0,3},{5,4},{6,5},{7,6},{4,7},{9,8},{10,9},{11,1... | collective-permute-start | bytes 1400840 | tf_op jit(solution)/shard_map/ppermute | solution.py:234
  14.1 0.0 collective-permute-done.2.far_ref
  14.1 3.2 %collective-permute-start.3 = (bf16[16,32,128]{2,1,0:T(8,128)(2,1)S(1)}, bf16[16,32,128]{2,1,0:T(8,128)(2,1)S(1)}, u32[]{:S(2)}, u32[]{:S(2)}) collective-permute-start(bf16[16,32,128]{2,1,0:T(8,128)(2,1)S(1)} %collective-permute-done.2.far_ref), channel_id=1, source_target_pairs={{0,8},{8,16},{16,24},{12,4},{20,12},{28,20},{1,9},{9,17},{17,25},{... | collective-permute-start | bytes 393224 | tf_op jit(solution)/shard_map/ppermute | solution.py:241
  17.4 5.6 %collective-permute-start.4 = (bf16[24,32,128]{2,1,0:T(8,128)(2,1)S(1)}, bf16[24,32,128]{2,1,0:T(8,128)(2,1)S(1)}, u32[]{:S(2)}, u32[]{:S(2)}) collective-permute-start(bf16[24,32,128]{2,1,0:T(8,128)(2,1)S(1)} %pad_maximum_fusion), channel_id=1, source_target_pairs={{64,32},{128,96},{192,160},{32,64},{96,128},{160,192},{65,33},{129... | collective-permute-start | bytes 589832 | tf_op jit(solution)/shard_map/ppermute | solution.py:244
  23.0 0.1 collective-permute-start.5
  23.1 0.0 collective-permute-done.3.other_ref
  23.1 3.4 %collective-permute-start.6 = (bf16[24,32,128]{2,1,0:T(8,128)(2,1)S(1)}, bf16[24,32,128]{2,1,0:T(8,128)(2,1)S(1)}, u32[]{:S(2)}, u32[]{:S(2)}) collective-permute-start(bf16[24,32,128]{2,1,0:T(8,128)(2,1)S(1)} %pad_maximum_fusion.1), channel_id=1, source_target_pairs={{64,32},{128,96},{192,160},{32,64},{96,128},{160,192},{65,33},{129... | collective-permute-start | bytes 589832 | tf_op jit(solution)/shard_map/ppermute | solution.py:245
  26.5 0.0 collective-permute-done.prev_ref
  26.5 0.1 collective-permute-start.7
  26.6 0.0 collective-permute-done.1.next_ref
  26.6 2.1 %early.1 = (s32[577]{0:T(1024)S(1)}, s32[2]{0:T(128)S(1)}, bf16[224,32,128]{2,1,0:T(8,128)(2,1)S(1)}, bf16[144,32,128]{2,1,0:T(8,128)(2,1)S(1)}) custom-call(s32[16,16]{1,0:T(8,128)S(1)} %pad_add_fusion.ints_ref, bf16[57,32,128]{2,1,0:T(8,128)(2,1)S(1)} %get-tuple-element.17.first_ref, bf16[57,32,128]{2,1,0:T(8,128)(2,1)S(1)} %get-tuple-element.18.second_ref, ...), custom_call_target="tpu_custom_call" | custom-call | tf_op jit(solution)/shard_map/early/pallas_call | solution.py:249
  28.7 0.0 collective-permute-done.4.chip_pair
  28.7 0.0 collective-permute-done.5.core_pair
  28.8 1.4 %collective-permute-done.6.chip_ref = bf16[24,32,128]{2,1,0:T(8,128)(2,1)S(1)} collective-permute-done((bf16[24,32,128]{2,1,0:T(8,128)(2,1)S(1)}, bf16[24,32,128]{2,1,0:T(8,128)(2,1)S(1)}, u32[]{:S(2)}, u32[]{:S(2)}) %collective-permute-start.6) | collective-permute-done | bytes 196640 | tf_op jit(solution)/shard_map/ppermute | solution.py:245
  30.1 0.0 collective-permute-done.7.core_ref
  30.1 2.1 %late.1 = (bf16[144,32,128]{2,1,0:T(8,128)(2,1)S(1)}, bf16[28,32,128]{2,1,0:T(8,128)(2,1)S(1)}, bf16[28,32,128]{2,1,0:T(8,128)(2,1)S(1)}) custom-call(s32[577]{0:T(1024)S(1)} %get-tuple-element.21.list_ref, s32[2]{0:T(128)S(1)} %get-tuple-element.22.sizes_ref, ...), custom_call_target="tpu_custom_call", output_to_operand_aliasing={{0}: (8, {})} | custom-call | tf_op jit(solution)/shard_map/late/pallas_call | solution.py:269
  32.3 1.3 %collective-permute-start.8 = (bf16[28,32,128]{2,1,0:T(8,128)(2,1)S(1)}, bf16[28,32,128]{2,1,0:T(8,128)(2,1)S(1)}, u32[]{:S(2)}, u32[]{:S(2)}) collective-permute-start(bf16[28,32,128]{2,1,0:T(8,128)(2,1)S(1)} %get-tuple-element.27), channel_id=1, source_target_pairs={{0,1},{1,2},{2,3},{3,0},{4,5},{5,6},{6,7},{7,4},{8,9},{9,10},{10,1... | collective-permute-start | bytes 688136 | tf_op jit(solution)/shard_map/ppermute | solution.py:279
  33.6 1.5 %collective-permute-start.9 = (bf16[28,32,128]{2,1,0:T(8,128)(2,1)S(1)}, bf16[28,32,128]{2,1,0:T(8,128)(2,1)S(1)}, u32[]{:S(2)}, u32[]{:S(2)}) collective-permute-start(bf16[28,32,128]{2,1,0:T(8,128)(2,1)S(1)} %get-tuple-element.28), channel_id=1, source_target_pairs={{1,0},{2,1},{3,2},{0,3},{5,4},{6,5},{7,6},{4,7},{9,8},{10,9},{11,1... | collective-permute-start | bytes 688136 | tf_op jit(solution)/shard_map/ppermute | solution.py:279
  35.0 2.0 %own.1.own_ref = f32[57,32,128]{2,1,0:T(8,128)S(1)} custom-call(s32[577]{0:T(1024)S(1)} %get-tuple-element.21.list_ref, s32[2]{0:T(128)S(1)} %get-tuple-element.22.sizes_ref, bf16[224,32,128]{2,1,0:T(8,128)(2,1)S(1)} %get-tuple-element.23.blocks_ref, bf16[16,64,64]{2,1,0:T(8,128)(2,1)S(1)} %get-tuple-element.24.turned_ref, ...), custom_call_target="tpu_custom_call" | custom-call | tf_op jit(solution)/shard_map/own/pallas_call | solution.py:280
  37.1 3.4 %collective-permute-done.8.one_ref = bf16[28,32,128]{2,1,0:T(8,128)(2,1)S(1)} collective-permute-done((bf16[28,32,128]{2,1,0:T(8,128)(2,1)S(1)}, bf16[28,32,128]{2,1,0:T(8,128)(2,1)S(1)}, u32[]{:S(2)}, u32[]{:S(2)}) %collective-permute-start.8) | collective-permute-done | bytes 229408 | tf_op jit(solution)/shard_map/ppermute | solution.py:279
  40.5 0.4 %collective-permute-done.9.two_ref = bf16[28,32,128]{2,1,0:T(8,128)(2,1)S(1)} collective-permute-done((bf16[28,32,128]{2,1,0:T(8,128)(2,1)S(1)}, bf16[28,32,128]{2,1,0:T(8,128)(2,1)S(1)}, u32[]{:S(2)}, u32[]{:S(2)}) %collective-permute-start.9) | collective-permute-done | bytes 229408 | tf_op jit(solution)/shard_map/ppermute | solution.py:279
  40.9 1.1 %total.1 = f32[4,7,64,64]{3,2,1,0:T(8,128)} custom-call(f32[57,32,128]{2,1,0:T(8,128)S(1)} %own.1.own_ref, bf16[28,32,128]{2,1,0:T(8,128)(2,1)S(1)} %collective-permute-done.8.one_ref, bf16[28,32,128]{2,1,0:T(8,128)(2,1)S(1)} %collective-permute-done.9.two_ref), custom_call_target="tpu_custom_call" | custom-call | tf_op jit(solution)/shard_map/total/pallas_call | solution.py:288
  (3 shorter events, 0.1 us)
Async XLA Ops:
  0.7 0.9 %copy-start = (bf16[16,64,64]{2,1,0:T(8,128)(2,1)S(1)}, bf16[16,64,64]{2,1,0:T(8,128)(2,1)}, u32[]{:S(2)}) copy-start(bf16[16,64,64]{2,1,0:T(8,128)(2,1)} %prolong_ref.1) | copy-start | bytes 393220
  1.8 12.3 %collective-permute-start.2 = (bf16[16,32,128]{2,1,0:T(8,128)(2,1)S(1)}, bf16[16,32,128]{2,1,0:T(8,128)(2,1)S(1)}, u32[]{:S(2)}, u32[]{:S(2)}) collective-permute-start(bf16[16,32,128]{2,1,0:T(8,128)(2,1)S(1)} %pack.1.packed_ref), channel_id=1, source_target_pairs={{0,4},{4,0},{8,12},{12,8},{16,20},{20,16},{24,28},{28,24},{1,5},{5... | collective-permute-start | bytes 393224 | tf_op jit(solution)/shard_map/ppermute | solution.py:219
  11.4 15.2 %collective-permute-start = (bf16[57,32,128]{2,1,0:T(8,128)(2,1)S(1)}, bf16[57,32,128]{2,1,0:T(8,128)(2,1)S(1)}, u32[]{:S(2)}, u32[]{:S(2)}) collective-permute-start(bf16[57,32,128]{2,1,0:T(8,128)(2,1)S(1)} %get-tuple-element.17.first_ref), channel_id=1, source_target_pairs={{0,1},{1,2},{2,3},{3,0},{4,5},{5,6},{6,7},{7,4},{8,9},{9,10},{10,1... | collective-permute-start | bytes 1400840 | tf_op jit(solution)/shard_map/ppermute | solution.py:234
  12.7 14.0 %collective-permute-start.1 = (bf16[57,32,128]{2,1,0:T(8,128)(2,1)S(1)}, bf16[57,32,128]{2,1,0:T(8,128)(2,1)S(1)}, u32[]{:S(2)}, u32[]{:S(2)}) collective-permute-start(bf16[57,32,128]{2,1,0:T(8,128)(2,1)S(1)} %get-tuple-element.18.second_ref), channel_id=1, source_target_pairs={{1,0},{2,1},{3,2},{0,3},{5,4},{6,5},{7,6},{4,7},{9,8},{10,9},{11,1... | collective-permute-start | bytes 1400840 | tf_op jit(solution)/shard_map/ppermute | solution.py:234
  14.1 9.0 %collective-permute-start.3 = (bf16[16,32,128]{2,1,0:T(8,128)(2,1)S(1)}, bf16[16,32,128]{2,1,0:T(8,128)(2,1)S(1)}, u32[]{:S(2)}, u32[]{:S(2)}) collective-permute-start(bf16[16,32,128]{2,1,0:T(8,128)(2,1)S(1)} %collective-permute-done.2.far_ref), channel_id=1, source_target_pairs={{0,8},{8,16},{16,24},{12,4},{20,12},{28,20},{1,9},{9,17},{17,25},{... | collective-permute-start | bytes 393224 | tf_op jit(solution)/shard_map/ppermute | solution.py:241
  17.4 11.4 %collective-permute-start.4 = (bf16[24,32,128]{2,1,0:T(8,128)(2,1)S(1)}, bf16[24,32,128]{2,1,0:T(8,128)(2,1)S(1)}, u32[]{:S(2)}, u32[]{:S(2)}) collective-permute-start(bf16[24,32,128]{2,1,0:T(8,128)(2,1)S(1)} %pad_maximum_fusion), channel_id=1, source_target_pairs={{64,32},{128,96},{192,160},{32,64},{96,128},{160,192},{65,33},{129... | collective-permute-start | bytes 589832 | tf_op jit(solution)/shard_map/ppermute | solution.py:244
  23.0 5.7 %collective-permute-start.5 = (bf16[24,32,128]{2,1,0:T(8,128)(2,1)S(1)}, bf16[24,32,128]{2,1,0:T(8,128)(2,1)S(1)}, u32[]{:S(2)}, u32[]{:S(2)}) collective-permute-start(bf16[24,32,128]{2,1,0:T(8,128)(2,1)S(1)} %pad_maximum_fusion), channel_id=1, source_target_pairs={{0,32},{32,0},{64,96},{96,64},{128,160},{160,128},{192,224},{224,1... | collective-permute-start | bytes 589832 | tf_op jit(solution)/shard_map/ppermute | solution.py:244
  23.1 7.0 %collective-permute-start.6 = (bf16[24,32,128]{2,1,0:T(8,128)(2,1)S(1)}, bf16[24,32,128]{2,1,0:T(8,128)(2,1)S(1)}, u32[]{:S(2)}, u32[]{:S(2)}) collective-permute-start(bf16[24,32,128]{2,1,0:T(8,128)(2,1)S(1)} %pad_maximum_fusion.1), channel_id=1, source_target_pairs={{64,32},{128,96},{192,160},{32,64},{96,128},{160,192},{65,33},{129... | collective-permute-start | bytes 589832 | tf_op jit(solution)/shard_map/ppermute | solution.py:245
  26.5 3.6 %collective-permute-start.7 = (bf16[24,32,128]{2,1,0:T(8,128)(2,1)S(1)}, bf16[24,32,128]{2,1,0:T(8,128)(2,1)S(1)}, u32[]{:S(2)}, u32[]{:S(2)}) collective-permute-start(bf16[24,32,128]{2,1,0:T(8,128)(2,1)S(1)} %pad_maximum_fusion.1), channel_id=1, source_target_pairs={{0,32},{32,0},{64,96},{96,64},{128,160},{160,128},{192,224},{224,1... | collective-permute-start | bytes 589832 | tf_op jit(solution)/shard_map/ppermute | solution.py:245
  32.3 8.2 %collective-permute-start.8 = (bf16[28,32,128]{2,1,0:T(8,128)(2,1)S(1)}, bf16[28,32,128]{2,1,0:T(8,128)(2,1)S(1)}, u32[]{:S(2)}, u32[]{:S(2)}) collective-permute-start(bf16[28,32,128]{2,1,0:T(8,128)(2,1)S(1)} %get-tuple-element.27), channel_id=1, source_target_pairs={{0,1},{1,2},{2,3},{3,0},{4,5},{5,6},{6,7},{7,4},{8,9},{9,10},{10,1... | collective-permute-start | bytes 688136 | tf_op jit(solution)/shard_map/ppermute | solution.py:279
  33.6 7.3 %collective-permute-start.9 = (bf16[28,32,128]{2,1,0:T(8,128)(2,1)S(1)}, bf16[28,32,128]{2,1,0:T(8,128)(2,1)S(1)}, u32[]{:S(2)}, u32[]{:S(2)}) collective-permute-start(bf16[28,32,128]{2,1,0:T(8,128)(2,1)S(1)} %get-tuple-element.28), channel_id=1, source_target_pairs={{1,0},{2,1},{3,2},{0,3},{5,4},{6,5},{7,6},{4,7},{9,8},{10,9},{11,1... | collective-permute-start | bytes 688136 | tf_op jit(solution)/shard_map/ppermute | solution.py:279

commit v4 on v3

v4 whole, which is shorter than its diff:
```python
import jax
import jax.numpy as jnp
from jax import lax
from jax.experimental import pallas as pl
from jax.experimental.pallas import tpu as pltpu
from jax.sharding import PartitionSpec as P

SC = 28
PART = 7
ALL = ("row", "col", "depth")
HBM = pl.BlockSpec(memory_space=pltpu.HBM)
VMEM = pl.BlockSpec(memory_space=pltpu.VMEM)
SMEM = pl.BlockSpec(memory_space=pltpu.SMEM)
LIMIT = pltpu.CompilerParams(vmem_limit_bytes=16 * 2**20)
BATCHES = (80, 40)
SMALL = pl.CostEstimate(flops=1000, bytes_accessed=1000, transcendentals=0)
LIST = 320
CUTS = 4
MOVED = 8
SEND, OWN = range(2)
TRASH = 2 * SC


def fold(block):
    half = block.shape[0] // 2
    return jnp.concatenate([block[:half], block[half:]], axis=1)


def unfold(block):
    half = block.shape[1] // 2
    return jnp.concatenate([block[:, :half], block[:, half:]], axis=0)


def pack_kernel(prolong_ref, out_ref):
    for i in range(prolong_ref.shape[0]):
        out_ref[i] = fold(prolong_ref[i])


def blocks_kernel(blocks_hbm, packed_ref, *refs):
    ints_hbm, (first_ref, second_ref, turned_ref, ints_ref), ints, (blocks_ref, sems) = refs[:4], refs[4:8], refs[8:12], refs[12:]
    half = first_ref.shape[0] - 1
    size = 2 * half // CUTS
    copies = [
        pltpu.make_async_copy(blocks_hbm.at[pl.ds(c * size, size)], blocks_ref.at[pl.ds(c * size, size)], sems.at[c])
        for c in range(CUTS)
    ]
    copies += [pltpu.make_async_copy(a, b, sems.at[CUTS + n]) for n, (a, b) in enumerate(zip(ints_hbm, ints))]
    for copy in copies:
        copy.start()
    for i in range(packed_ref.shape[0]):
        turned_ref[i] = unfold(packed_ref[i]).T
    for c in range(CUTS):
        copies[c].wait()
        for n in range(c * size, (c + 1) * size):
            if n < half:
                first_ref[n] = fold(blocks_ref[n])
            else:
                second_ref[n - half] = fold(blocks_ref[n])
    for copy in copies[CUTS:]:
        copy.wait()
    values = jnp.concatenate([ref[...] for ref in ints], axis=0)
    ints_ref[...] = values
    coded = jnp.concatenate([values >> 4, values & 15], axis=0).astype(jnp.float32).astype(first_ref.dtype)
    for out in (first_ref, second_ref):
        out[half] = jnp.zeros(out.shape[1:], out.dtype)
        out[half, :, 0 : values.shape[1]] = coded


def entries_of(ints, depth, source, rel_b, row_ok, shift):
    count, agg = ints[2 * PART : 2 * PART + 1], ints[2 * PART + 1 : 2 * PART + 2]
    j, k = ints[:PART], ints[PART : 2 * PART]
    i = lax.broadcasted_iota(jnp.int32, j.shape, 1)
    s = lax.broadcasted_iota(jnp.int32, j.shape, 0)
    home_r, home_c = lax.axis_index("row"), lax.axis_index("col")
    across, flip = 1 - 2 * (home_c & 1), 1 - 2 * (home_r & 1)
    dest = (k * 37) >> 8
    rel = (dest - depth) & 3
    valid = ((rel == 0) | (rel == rel_b)) & (source * PART + s < count) & row_ok
    target = (jnp.where(rel == 3, PART, 0) + k - dest * PART) * 4 + agg
    dr = ((j >> 7) - home_r) * flip
    dc = ((j >> 4) & 7) - home_c
    side = jnp.where(dc == 0, 0, jnp.where(dc == across, 1, 2))
    place = side + 3 * jnp.where(dr == 0, 0, (dr + 3) >> 1)
    entry = (((((i << 8) + shift + i * PART + s) << 8) + place * 16 + (j & 15)) << 8) + target
    kind = jnp.where(rel == 0, OWN, SEND)
    return entry + jnp.where(valid, 1 << (28 + kind), 0)


def decoded(piece, rows):
    values = piece[:, :rows].astype(jnp.float32).astype(jnp.int32)
    return values[: values.shape[0] // 2] * 16 + values[values.shape[0] // 2 :]


def exact_dot(a, b):
    return jnp.dot(a.astype(jnp.bfloat16), b.astype(jnp.bfloat16), preferred_element_type=jnp.float32)


def make_lists(own_ref, prev_ref, next_ref, list_ref, words_ref):
    rows = own_ref.shape[1]
    depth = lax.axis_index("depth")
    lane = lax.broadcasted_iota(jnp.int32, (PART, rows), 1)
    first = lane < rows // 2
    before, after = (depth + 3) & 3, (depth + 1) & 3
    own = entries_of(own_ref[...], depth, depth, jnp.where(first, 3, 1), lane >= 0, 0)
    from_prev = entries_of(decoded(prev_ref[prev_ref.shape[0] - 1], rows), depth, before, 1, first, rows * PART)
    from_next = entries_of(decoded(next_ref[next_ref.shape[0] - 1], rows), depth, after, 3, ~first, rows * PART)
    words_ref[...] = jnp.zeros_like(words_ref)
    words_ref[0:PART, 0:rows] = own
    words_ref[8 : 8 + PART, 0:rows] = jnp.where(first, from_prev, from_next)
    words = words_ref[...]
    lanes = words.shape[1]
    earlier = lax.broadcasted_iota(jnp.int32, (lanes, lanes), 0) < lax.broadcasted_iota(jnp.int32, (lanes, lanes), 1)
    above = lax.broadcasted_iota(jnp.int32, (16, 16), 0) > lax.broadcasted_iota(jnp.int32, (16, 16), 1)
    earlier, above = earlier.astype(jnp.float32), above.astype(jnp.float32)
    places = jnp.full(words.shape, 2.0 * LIST, jnp.float32)
    totals = []
    for kind in range(2):
        here = (words >> (28 + kind)) & 1
        member = here.astype(jnp.float32)
        count = jnp.sum(member, axis=1, keepdims=True) + jnp.zeros_like(member)
        place = exact_dot(member, earlier) + exact_dot(above, count)
        totals.append(jnp.sum(count, axis=0, keepdims=True)[:, 0:1].astype(jnp.int32))
        places = jnp.where(here == 1, place + kind * LIST, places)
    turned = places.T[0:rows]
    spot = lax.broadcasted_iota(jnp.int32, (rows, 2 * LIST), 1).astype(jnp.float32)
    fields = [TRASH - (words & 255), (words >> 8) & 255, (words >> 16) & 255, (words >> 24) & 15]
    fields = [f[:, 0:rows].astype(jnp.float32) for f in fields]
    blank = jnp.zeros((8 - len(fields), rows), jnp.float32)
    listed = jnp.zeros((8, 2 * LIST), jnp.float32)
    for r in (*range(PART), *range(8, 8 + PART)):
        chosen = jnp.where(turned[:, r : r + 1] == spot, 1.0, 0.0)
        listed = listed + exact_dot(jnp.concatenate([f[r : r + 1] for f in fields] + [blank], axis=0), chosen)
    target, place, block, row = (listed[n : n + 1].astype(jnp.int32) for n in range(4))
    entry = (((((row << 8) + block) << 8) + place) << 8) + TRASH - target
    spot = lax.broadcasted_iota(jnp.int32, entry.shape, 1)
    for kind in range(2):
        entry = jnp.where(spot == (kind + 1) * LIST - 1, totals[kind], entry)
    list_ref[...] = entry


def run_list(list_ref, kind, blocks_ref, turned_ref, halo_ref, acc_ref):
    batch = BATCHES[kind]

    def step(b, carry):
        entries = [list_ref[0, kind * LIST + b * batch + p] for p in range(batch)]
        products = [
            jnp.dot(
                unfold(blocks_ref[(e >> 16) & 255]), unfold(halo_ref[(e >> 8) & 255]), preferred_element_type=jnp.float32
            ).astype(jnp.bfloat16)
            for e in entries
        ]
        for e, product in zip(entries, products):
            term = jnp.dot(turned_ref[(e >> 24) & 15], product, preferred_element_type=jnp.float32)
            acc_ref[e & 255] += fold(term)
        return carry

    lax.fori_loop(0, lax.div(list_ref[0, (kind + 1) * LIST - 1] + (batch - 1), batch), step, 0)


def early_kernel(ints_ref, first_ref, second_ref, prev_ref, next_ref, packed_ref, far_ref, other_ref,
                 list_ref, blocks_ref, halo_ref, words_ref):
    make_lists(ints_ref, prev_ref, next_ref, list_ref, words_ref)
    half = first_ref.shape[0] - 1
    rows = packed_ref.shape[0]
    for at, part in enumerate((first_ref, second_ref, prev_ref, next_ref)):
        blocks_ref[pl.ds(at * half, half)] = part[0:half]
    for at, part in enumerate((packed_ref, far_ref, other_ref)):
        halo_ref[pl.ds(at * rows, part.shape[0])] = part[...]


def late_kernel(list_ref, blocks_ref, turned_ref, chip_pair, core_pair, chip_ref, core_ref, halo_in,
                halo_ref, after_ref, before_ref, acc_ref):
    rows = halo_ref.shape[0] // 9
    for at, (one, two) in ((3, (chip_pair, chip_ref)), (6, (core_pair, core_ref))):
        moved = two.shape[0] - rows
        halo_ref[pl.ds(at * rows, rows - moved)] = one[rows:]
        halo_ref[pl.ds((at + 1) * rows - moved, moved)] = two[rows:]
        halo_ref[pl.ds((at + 1) * rows, rows)] = one[0:rows]
        halo_ref[pl.ds((at + 2) * rows, rows)] = two[0:rows]
    acc_ref[...] = jnp.zeros_like(acc_ref)
    run_list(list_ref, SEND, blocks_ref, turned_ref, halo_ref, acc_ref)
    after_ref[...] = acc_ref[0:SC].astype(after_ref.dtype)
    before_ref[...] = acc_ref[SC : 2 * SC].astype(before_ref.dtype)


def own_kernel(list_ref, blocks_ref, turned_ref, halo_ref, acc_ref):
    acc_ref[...] = jnp.zeros_like(acc_ref)
    run_list(list_ref, OWN, blocks_ref, turned_ref, halo_ref, acc_ref)


def sum_kernel(own_ref, one_ref, two_ref, out_hbm, total_ref, sems):
    aggs, slots = total_ref.shape[:2]
    copies = []
    for a in range(aggs):
        for s in range(slots):
            at = s * aggs + a
            total = own_ref[at] + (one_ref[at].astype(jnp.float32) + two_ref[at].astype(jnp.float32))
            total_ref[a, s] = unfold(total)
        copies.append(pltpu.make_async_copy(total_ref.at[a], out_hbm.at[a], sems.at[a]))
        copies[-1].start()
    for copy in copies:
        copy.wait()


def per_device(blocks, columns, counts, aggregate, coarse_slot, prolong):
    rows, slots, width, _ = blocks.shape
    n_row, n_col, n_depth = (lax.axis_size(a) for a in ALL)
    piece = (width // 2, 2 * width)
    bf16 = jnp.bfloat16
    tie = lax.optimization_barrier

    def struct(*shape, dtype=bf16):
        return jax.ShapeDtypeStruct(shape, dtype)

    packed = pl.pallas_call(
        pack_kernel, out_shape=struct(rows, *piece), in_specs=[VMEM], out_specs=VMEM, compiler_params=LIMIT, name="pack"
    )(prolong)
    far = lax.ppermute(packed, "col", [(c, c ^ 1) for c in range(n_col)])

    half = rows * slots // 2
    blocks_hbm = pltpu.with_memory_space_constraint(blocks.reshape(rows * slots, width, width), pltpu.HBM)
    ints = [pltpu.with_memory_space_constraint(a, pltpu.HBM) for a in (columns.T, coarse_slot.T, counts[None], aggregate[None])]
    first, second, turned, ints = pl.pallas_call(
        blocks_kernel,
        out_shape=[
            struct(half + 1, *piece),
            struct(half + 1, *piece),
            struct(rows, width, width),
            struct(2 * slots + 2, rows, dtype=jnp.int32),
        ],
        in_specs=[HBM, VMEM] + [HBM] * 4,
        out_specs=[VMEM] * 4,
        scratch_shapes=[pltpu.VMEM(a.shape, a.dtype) for a in ints]
        + [pltpu.VMEM((rows * slots, width, width), bf16), pltpu.SemaphoreType.DMA((CUTS + 4,))],
        compiler_params=LIMIT,
        name="blocks",
    )(blocks_hbm, packed, *ints)
    up = [(d, (d + 1) % n_depth) for d in range(n_depth)]
    down = [(b, a) for a, b in up]
    from_prev, from_next = lax.ppermute(first, "depth", up), lax.ppermute(second, "depth", down)

    core = [(r, r ^ 1) for r in range(n_row)]
    chip = [(r, min(max(r - 1 + 2 * (r % 2), 0), n_row - 1)) for r in range(n_row)]

    far, turned = tie((far, turned))
    fetch = [((c - 2 + 4 * (c % 2)) % n_col, c) for c in range(n_col)]
    other = lax.ppermute(far, "col", fetch)
    pair = jnp.concatenate([far, packed[: rows - MOVED]], axis=0)
    other_and = jnp.concatenate([other, packed[rows - MOVED :]], axis=0)
    chip_pair, core_pair = lax.ppermute(pair, "row", chip), lax.ppermute(pair, "row", core)
    chip_other, core_other = lax.ppermute(other_and, "row", chip), lax.ppermute(other_and, "row", core)

    sends = struct(TRASH + 1, *piece, dtype=jnp.float32)
    halos = struct(9 * rows, *piece)
    entries, all_blocks, halo = pl.pallas_call(
        early_kernel,
        out_shape=[struct(1, 2 * LIST, dtype=jnp.int32), struct(2 * rows * slots, *piece), halos],
        in_specs=[VMEM] * 8,
        out_specs=[VMEM] * 3,
        scratch_shapes=[pltpu.VMEM((16, 128), jnp.int32)],
        compiler_params=LIMIT,
        name="early",
    )(ints, first, second, from_prev, from_next, packed, far, other)
    halo, after, before = pl.pallas_call(
        late_kernel,
        out_shape=[halos, struct(SC, *piece), struct(SC, *piece)],
        in_specs=[SMEM] + [VMEM] * 7,
        out_specs=[VMEM] * 3,
        scratch_shapes=[pltpu.VMEM((TRASH + 1, *piece), jnp.float32)],
        input_output_aliases={7: 0},
        compiler_params=LIMIT,
        name="late",
    )(entries, all_blocks, turned, chip_pair, core_pair, chip_other, core_other, halo)
    got_prev, got_next = lax.ppermute(after, "depth", up), lax.ppermute(before, "depth", down)
    own = pl.pallas_call(
        own_kernel,
        out_shape=sends,
        in_specs=[SMEM] + [VMEM] * 3,
        out_specs=VMEM,
        compiler_params=LIMIT,
        name="own",
    )(entries, all_blocks, turned, halo)
    return pl.pallas_call(
        sum_kernel,
        out_shape=struct(4, SC // n_depth, width, width, dtype=jnp.float32),
        in_specs=[VMEM] * 3,
        out_specs=HBM,
        scratch_shapes=[
            pltpu.VMEM((4, SC // n_depth, width, width), jnp.float32),
            pltpu.SemaphoreType.DMA((4,)),
        ],
        compiler_params=LIMIT,
        name="total",
    )(own, got_prev, got_next)


def solution(mesh):
    in_specs = (
        P(("row", "col"), "depth", None, None),
        P(("row", "col"), "depth"),
        P(("row", "col")),
        P(("row", "col")),
        P(("row", "col"), "depth"),
        P(("row", "col"), None, None),
    )
    out_specs = P(("row", "col"), "depth", None, None)
    return jax.shard_map(per_device, mesh=mesh, in_specs=in_specs, out_specs=out_specs, check_vma=False)
```

time: 42.2 us -> 39.2 us (0.929)
  Pallas kernels: 9.16 us -> 7.45 us
  other arithmetic: 0.79 us -> 0.04 us
  starting transfers between devices: 25.7 us -> 25 us
    ppermute x1, starting transfers between devices: 3.2 us -> 1.3 us  [per_device(): other = lax.ppermute(far, 'col', fetch)]
    pallas_call x2, Pallas kernels: 4.13 us -> 2.74 us  [the longest x1 2.04 us: per_device(): pl.pallas_call(own_kernel, out_shape=sends, in_specs=[SMEM] + [VMEM] * 3,...]
    ppermute x1, waiting for transfers between devices: 1.38 us -> 2.5 us  [per_device(): lax.ppermute(other_and, 'row', chip)]
    ppermute x1, starting transfers between devices: 3.37 us -> 4.44 us  [per_device(): lax.ppermute(other_and, 'row', chip)]
    ppermute x1, waiting for transfers between devices: 3.4 us -> 2.59 us  [per_device(): lax.ppermute(after, 'depth', up)]
    concatenate x1 -> x0, other arithmetic: 0.74 us -> none  [per_device(): jnp.concatenate([columns.T, coarse_slot.T, counts[None], aggregate[None]]...]
  transfers between devices with their start and end apart: 10 -> 10, of which waited for: 3 -> 3; matrix products, arithmetic and copies ran while one was open for 0% -> 0% of each run, Pallas kernels for 14% -> 11%
where the time goes in v4:
time: 39.2 us; the launch traced here: 38.9 us
  starting transfers between devices  25 us (64%)
  Pallas kernels  7.45 us (19%)
  waiting for transfers between devices  5.36 us (14%)
  local copies, waits for them, and re-layouts  0.96 us (2%)
    ppermute x1, starting transfers between devices, per_device(): far = lax.ppermute(packed, 'col', [(c, c ^ 1) for c in range(n_col)])  7.83 us
    ppermute x1, starting transfers between devices, per_device(): lax.ppermute(pair, 'row', chip)  5.71 us
    ppermute x1, starting transfers between devices, per_device(): lax.ppermute(other_and, 'row', chip)  4.44 us
    ppermute x1, waiting for transfers between devices, per_device(): lax.ppermute(after, 'depth', up)  2.59 us
    ppermute x1, waiting for transfers between devices, per_device(): lax.ppermute(other_and, 'row', chip)  2.5 us
    pallas_call x1, Pallas kernels, per_device(): pl.pallas_call(own_kernel, out_shape=sends, in_specs=[SMEM] + [VMEM] * 3,...  2.04 us
    pallas_call x1, Pallas kernels, per_device(): pl.pallas_call(late_kernel, out_shape=[halos, struct(SC, *piece), struct(...  1.91 us
    pallas_call x1, Pallas kernels, per_device(): pl.pallas_call(blocks_kernel, out_shape=[struct(half + 1, *piece), struct...  1.65 us
  transfers between devices with their start and end apart: 10, of which 3 were waited for; matrix products, arithmetic and copies ran while one was open for 0% of the time, Pallas kernels for 11%

profile of v4, /device:TPU:1, one launch (start us, length us, event | category | flops | bytes accessed | tf_op | source)
XLA Modules:
  0.0 38.9 jit_solution(5710431310501582754)
XLA Ops:
  0.0 0.0 copy-start
  0.0 0.9 %copy-done = bf16[16,64,64]{2,1,0:T(8,128)(2,1)S(1)} copy-done((bf16[16,64,64]{2,1,0:T(8,128)(2,1)S(1)}, bf16[16,64,64]{2,1,0:T(8,128)(2,1)}, u32[]{:S(2)}) %copy-start) | copy-done | bytes 131096
  1.0 0.1 pack.1.packed_ref
  1.1 7.8 %collective-permute-start.2 = (bf16[16,32,128]{2,1,0:T(8,128)(2,1)S(1)}, bf16[16,32,128]{2,1,0:T(8,128)(2,1)S(1)}, u32[]{:S(2)}, u32[]{:S(2)}) collective-permute-start(bf16[16,32,128]{2,1,0:T(8,128)(2,1)S(1)} %pack.1.packed_ref), channel_id=1, source_target_pairs={{0,4},{4,0},{8,12},{12,8},{16,20},{20,16},{24,28},{28,24},{1,5},{5... | collective-permute-start | bytes 393224 | tf_op jit(solution)/shard_map/ppermute | solution.py:218
  8.9 1.6 %blocks.1 = (bf16[57,32,128]{2,1,0:T(8,128)(2,1)S(1)}, bf16[57,32,128]{2,1,0:T(8,128)(2,1)S(1)}, bf16[16,64,64]{2,1,0:T(8,128)(2,1)S(1)}, s32[16,16]{1,0:T(8,128)S(1)}) custom-call(bf16[112,64,64]{2,1,0:T(8,128)(2,1)} %bitcast.5, bf16[16,32,128]{2,1,0:T(8,128)(2,1)S(1)} %pack.1.packed_ref, s32[7,16]{1,0:T(8,128)} %bitcast.6, s32[7,16]{1,0:T(8,128)} %bitcast.7, ...), custom_call_target="tpu_custom_call" | custom-call | tf_op jit(solution)/shard_map/blocks/pallas_call | solution.py:223
  10.5 1.3 %collective-permute-start = (bf16[57,32,128]{2,1,0:T(8,128)(2,1)S(1)}, bf16[57,32,128]{2,1,0:T(8,128)(2,1)S(1)}, u32[]{:S(2)}, u32[]{:S(2)}) collective-permute-start(bf16[57,32,128]{2,1,0:T(8,128)(2,1)S(1)} %get-tuple-element.18.first_ref), channel_id=1, source_target_pairs={{0,1},{1,2},{2,3},{3,0},{4,5},{5,6},{6,7},{7,4},{8,9},{9,10},{10,1... | collective-permute-start | bytes 1400840 | tf_op jit(solution)/shard_map/ppermute | solution.py:240
  11.8 1.5 %collective-permute-start.1 = (bf16[57,32,128]{2,1,0:T(8,128)(2,1)S(1)}, bf16[57,32,128]{2,1,0:T(8,128)(2,1)S(1)}, u32[]{:S(2)}, u32[]{:S(2)}) collective-permute-start(bf16[57,32,128]{2,1,0:T(8,128)(2,1)S(1)} %get-tuple-element.19.second_ref), channel_id=1, source_target_pairs={{1,0},{2,1},{3,2},{0,3},{5,4},{6,5},{7,6},{4,7},{9,8},{10,9},{11,1... | collective-permute-start | bytes 1400840 | tf_op jit(solution)/shard_map/ppermute | solution.py:240
  13.3 0.0 collective-permute-done.2.far_ref
  13.3 1.3 %collective-permute-start.3 = (bf16[16,32,128]{2,1,0:T(8,128)(2,1)S(1)}, bf16[16,32,128]{2,1,0:T(8,128)(2,1)S(1)}, u32[]{:S(2)}, u32[]{:S(2)}) collective-permute-start(bf16[16,32,128]{2,1,0:T(8,128)(2,1)S(1)} %collective-permute-done.2.far_ref), channel_id=1, source_target_pairs={{24,0},{12,4},{0,8},{20,12},{8,16},{28,20},{16,24},{4,28},{25,1},{... | collective-permute-start | bytes 393224 | tf_op jit(solution)/shard_map/ppermute | solution.py:247
  14.6 5.7 %collective-permute-start.4 = (bf16[24,32,128]{2,1,0:T(8,128)(2,1)S(1)}, bf16[24,32,128]{2,1,0:T(8,128)(2,1)S(1)}, u32[]{:S(2)}, u32[]{:S(2)}) collective-permute-start(bf16[24,32,128]{2,1,0:T(8,128)(2,1)S(1)} %pad_maximum_fusion), channel_id=1, source_target_pairs={{0,0},{32,64},{64,32},{96,128},{128,96},{160,192},{192,160},{224,2... | collective-permute-start | bytes 589832 | tf_op jit(solution)/shard_map/ppermute | solution.py:250
  20.3 0.1 collective-permute-start.5
  20.4 0.0 collective-permute-done.3.other_ref
  20.5 4.4 %collective-permute-start.6 = (bf16[24,32,128]{2,1,0:T(8,128)(2,1)S(1)}, bf16[24,32,128]{2,1,0:T(8,128)(2,1)S(1)}, u32[]{:S(2)}, u32[]{:S(2)}) collective-permute-start(bf16[24,32,128]{2,1,0:T(8,128)(2,1)S(1)} %pad_maximum_fusion.1), channel_id=1, source_target_pairs={{0,0},{32,64},{64,32},{96,128},{128,96},{160,192},{192,160},{224,2... | collective-permute-start | bytes 589832 | tf_op jit(solution)/shard_map/ppermute | solution.py:251
  24.9 0.0 collective-permute-done.prev_ref
  24.9 0.1 collective-permute-start.7
  25.0 0.0 collective-permute-done.1.next_ref
  25.1 0.7 %early.1 = (s32[1,640]{1,0:T(1,128)S(1)}, bf16[224,32,128]{2,1,0:T(8,128)(2,1)S(1)}, bf16[144,32,128]{2,1,0:T(8,128)(2,1)S(1)}) custom-call(s32[16,16]{1,0:T(8,128)S(1)} %get-tuple-element.17.ints_ref, bf16[57,32,128]{2,1,0:T(8,128)(2,1)S(1)} %get-tuple-element.18.first_ref, bf16[57,32,128]{2,1,0:T(8,128)(2,1)S(1)} %get-tuple-element.19.second_ref, ...), custom_call_target="tpu_custom_call" | custom-call | tf_op jit(solution)/shard_map/early/pallas_call | solution.py:255
  25.8 0.0 collective-permute-done.4.chip_pair
  25.8 0.0 collective-permute-done.5.core_pair
  25.8 2.5 %collective-permute-done.6.chip_ref = bf16[24,32,128]{2,1,0:T(8,128)(2,1)S(1)} collective-permute-done((bf16[24,32,128]{2,1,0:T(8,128)(2,1)S(1)}, bf16[24,32,128]{2,1,0:T(8,128)(2,1)S(1)}, u32[]{:S(2)}, u32[]{:S(2)}) %collective-permute-start.6) | collective-permute-done | bytes 196640 | tf_op jit(solution)/shard_map/ppermute | solution.py:251
  28.3 0.0 collective-permute-done.7.core_ref
  28.3 1.9 %late.1 = (bf16[144,32,128]{2,1,0:T(8,128)(2,1)S(1)}, bf16[28,32,128]{2,1,0:T(8,128)(2,1)S(1)}, bf16[28,32,128]{2,1,0:T(8,128)(2,1)S(1)}) custom-call(s32[1,640]{1,0:T(1,128)S(1)} %get-tuple-element.22.list_ref, bf16[224,32,128]{2,1,0:T(8,128)(2,1)S(1)} %get-tuple-element.23.blocks_ref, ...), custom_call_target="tpu_custom_call", output_to_operand_aliasing={{0}: (7, {})} | custom-call | tf_op jit(solution)/shard_map/late/pallas_call | solution.py:264
  30.2 1.3 %collective-permute-start.8 = (bf16[28,32,128]{2,1,0:T(8,128)(2,1)S(1)}, bf16[28,32,128]{2,1,0:T(8,128)(2,1)S(1)}, u32[]{:S(2)}, u32[]{:S(2)}) collective-permute-start(bf16[28,32,128]{2,1,0:T(8,128)(2,1)S(1)} %get-tuple-element.27), channel_id=1, source_target_pairs={{0,1},{1,2},{2,3},{3,0},{4,5},{5,6},{6,7},{7,4},{8,9},{9,10},{10,1... | collective-permute-start | bytes 688136 | tf_op jit(solution)/shard_map/ppermute | solution.py:274
  31.5 1.5 %collective-permute-start.9 = (bf16[28,32,128]{2,1,0:T(8,128)(2,1)S(1)}, bf16[28,32,128]{2,1,0:T(8,128)(2,1)S(1)}, u32[]{:S(2)}, u32[]{:S(2)}) collective-permute-start(bf16[28,32,128]{2,1,0:T(8,128)(2,1)S(1)} %get-tuple-element.28), channel_id=1, source_target_pairs={{1,0},{2,1},{3,2},{0,3},{5,4},{6,5},{7,6},{4,7},{9,8},{10,9},{11,1... | collective-permute-start | bytes 688136 | tf_op jit(solution)/shard_map/ppermute | solution.py:274
  33.0 2.0 %own.1.own_ref = f32[57,32,128]{2,1,0:T(8,128)S(1)} custom-call(s32[1,640]{1,0:T(1,128)S(1)} %get-tuple-element.22.list_ref, bf16[224,32,128]{2,1,0:T(8,128)(2,1)S(1)} %get-tuple-element.23.blocks_ref, bf16[16,64,64]{2,1,0:T(8,128)(2,1)S(1)} %get-tuple-element.24.turned_ref, bf16[144,32,128]{2,1,0:T(8,128)(2,1)S(1)} %get-tuple-element.26.halo_ref), custom_call_target="tpu_custom_call" | custom-call | tf_op jit(solution)/shard_map/own/pallas_call | solution.py:275
  35.0 2.6 %collective-permute-done.8.one_ref = bf16[28,32,128]{2,1,0:T(8,128)(2,1)S(1)} collective-permute-done((bf16[28,32,128]{2,1,0:T(8,128)(2,1)S(1)}, bf16[28,32,128]{2,1,0:T(8,128)(2,1)S(1)}, u32[]{:S(2)}, u32[]{:S(2)}) %collective-permute-start.8) | collective-permute-done | bytes 229408 | tf_op jit(solution)/shard_map/ppermute | solution.py:274
  37.6 0.3 collective-permute-done.9.two_ref
  37.8 1.1 %total.1 = f32[4,7,64,64]{3,2,1,0:T(8,128)} custom-call(f32[57,32,128]{2,1,0:T(8,128)S(1)} %own.1.own_ref, bf16[28,32,128]{2,1,0:T(8,128)(2,1)S(1)} %collective-permute-done.8.one_ref, bf16[28,32,128]{2,1,0:T(8,128)(2,1)S(1)} %collective-permute-done.9.two_ref), custom_call_target="tpu_custom_call" | custom-call | tf_op jit(solution)/shard_map/total/pallas_call | solution.py:283
  (3 shorter events, 0.1 us)
Async XLA Ops:
  0.0 0.9 %copy-start = (bf16[16,64,64]{2,1,0:T(8,128)(2,1)S(1)}, bf16[16,64,64]{2,1,0:T(8,128)(2,1)}, u32[]{:S(2)}) copy-start(bf16[16,64,64]{2,1,0:T(8,128)(2,1)} %prolong_ref.1) | copy-start | bytes 393220
  1.1 12.2 %collective-permute-start.2 = (bf16[16,32,128]{2,1,0:T(8,128)(2,1)S(1)}, bf16[16,32,128]{2,1,0:T(8,128)(2,1)S(1)}, u32[]{:S(2)}, u32[]{:S(2)}) collective-permute-start(bf16[16,32,128]{2,1,0:T(8,128)(2,1)S(1)} %pack.1.packed_ref), channel_id=1, source_target_pairs={{0,4},{4,0},{8,12},{12,8},{16,20},{20,16},{24,28},{28,24},{1,5},{5... | collective-permute-start | bytes 393224 | tf_op jit(solution)/shard_map/ppermute | solution.py:218
  10.5 14.4 %collective-permute-start = (bf16[57,32,128]{2,1,0:T(8,128)(2,1)S(1)}, bf16[57,32,128]{2,1,0:T(8,128)(2,1)S(1)}, u32[]{:S(2)}, u32[]{:S(2)}) collective-permute-start(bf16[57,32,128]{2,1,0:T(8,128)(2,1)S(1)} %get-tuple-element.18.first_ref), channel_id=1, source_target_pairs={{0,1},{1,2},{2,3},{3,0},{4,5},{5,6},{6,7},{7,4},{8,9},{9,10},{10,1... | collective-permute-start | bytes 1400840 | tf_op jit(solution)/shard_map/ppermute | solution.py:240
  11.8 13.2 %collective-permute-start.1 = (bf16[57,32,128]{2,1,0:T(8,128)(2,1)S(1)}, bf16[57,32,128]{2,1,0:T(8,128)(2,1)S(1)}, u32[]{:S(2)}, u32[]{:S(2)}) collective-permute-start(bf16[57,32,128]{2,1,0:T(8,128)(2,1)S(1)} %get-tuple-element.19.second_ref), channel_id=1, source_target_pairs={{1,0},{2,1},{3,2},{0,3},{5,4},{6,5},{7,6},{4,7},{9,8},{10,9},{11,1... | collective-permute-start | bytes 1400840 | tf_op jit(solution)/shard_map/ppermute | solution.py:240
  13.3 7.2 %collective-permute-start.3 = (bf16[16,32,128]{2,1,0:T(8,128)(2,1)S(1)}, bf16[16,32,128]{2,1,0:T(8,128)(2,1)S(1)}, u32[]{:S(2)}, u32[]{:S(2)}) collective-permute-start(bf16[16,32,128]{2,1,0:T(8,128)(2,1)S(1)} %collective-permute-done.2.far_ref), channel_id=1, source_target_pairs={{24,0},{12,4},{0,8},{20,12},{8,16},{28,20},{16,24},{4,28},{25,1},{... | collective-permute-start | bytes 393224 | tf_op jit(solution)/shard_map/ppermute | solution.py:247
  14.6 11.1 %collective-permute-start.4 = (bf16[24,32,128]{2,1,0:T(8,128)(2,1)S(1)}, bf16[24,32,128]{2,1,0:T(8,128)(2,1)S(1)}, u32[]{:S(2)}, u32[]{:S(2)}) collective-permute-start(bf16[24,32,128]{2,1,0:T(8,128)(2,1)S(1)} %pad_maximum_fusion), channel_id=1, source_target_pairs={{0,0},{32,64},{64,32},{96,128},{128,96},{160,192},{192,160},{224,2... | collective-permute-start | bytes 589832 | tf_op jit(solution)/shard_map/ppermute | solution.py:250
  20.3 5.4 %collective-permute-start.5 = (bf16[24,32,128]{2,1,0:T(8,128)(2,1)S(1)}, bf16[24,32,128]{2,1,0:T(8,128)(2,1)S(1)}, u32[]{:S(2)}, u32[]{:S(2)}) collective-permute-start(bf16[24,32,128]{2,1,0:T(8,128)(2,1)S(1)} %pad_maximum_fusion), channel_id=1, source_target_pairs={{0,32},{32,0},{64,96},{96,64},{128,160},{160,128},{192,224},{224,1... | collective-permute-start | bytes 589832 | tf_op jit(solution)/shard_map/ppermute | solution.py:250
  20.5 7.8 %collective-permute-start.6 = (bf16[24,32,128]{2,1,0:T(8,128)(2,1)S(1)}, bf16[24,32,128]{2,1,0:T(8,128)(2,1)S(1)}, u32[]{:S(2)}, u32[]{:S(2)}) collective-permute-start(bf16[24,32,128]{2,1,0:T(8,128)(2,1)S(1)} %pad_maximum_fusion.1), channel_id=1, source_target_pairs={{0,0},{32,64},{64,32},{96,128},{128,96},{160,192},{192,160},{224,2... | collective-permute-start | bytes 589832 | tf_op jit(solution)/shard_map/ppermute | solution.py:251
  24.9 3.3 %collective-permute-start.7 = (bf16[24,32,128]{2,1,0:T(8,128)(2,1)S(1)}, bf16[24,32,128]{2,1,0:T(8,128)(2,1)S(1)}, u32[]{:S(2)}, u32[]{:S(2)}) collective-permute-start(bf16[24,32,128]{2,1,0:T(8,128)(2,1)S(1)} %pad_maximum_fusion.1), channel_id=1, source_target_pairs={{0,32},{32,0},{64,96},{96,64},{128,160},{160,128},{192,224},{224,1... | collective-permute-start | bytes 589832 | tf_op jit(solution)/shard_map/ppermute | solution.py:251
  30.2 7.4 %collective-permute-start.8 = (bf16[28,32,128]{2,1,0:T(8,128)(2,1)S(1)}, bf16[28,32,128]{2,1,0:T(8,128)(2,1)S(1)}, u32[]{:S(2)}, u32[]{:S(2)}) collective-permute-start(bf16[28,32,128]{2,1,0:T(8,128)(2,1)S(1)} %get-tuple-element.27), channel_id=1, source_target_pairs={{0,1},{1,2},{2,3},{3,0},{4,5},{5,6},{6,7},{7,4},{8,9},{9,10},{10,1... | collective-permute-start | bytes 688136 | tf_op jit(solution)/shard_map/ppermute | solution.py:274
  31.5 6.4 %collective-permute-start.9 = (bf16[28,32,128]{2,1,0:T(8,128)(2,1)S(1)}, bf16[28,32,128]{2,1,0:T(8,128)(2,1)S(1)}, u32[]{:S(2)}, u32[]{:S(2)}) collective-permute-start(bf16[28,32,128]{2,1,0:T(8,128)(2,1)S(1)} %get-tuple-element.28), channel_id=1, source_target_pairs={{1,0},{2,1},{3,2},{0,3},{5,4},{6,5},{7,6},{4,7},{9,8},{10,9},{11,1... | collective-permute-start | bytes 688136 | tf_op jit(solution)/shard_map/ppermute | solution.py:274

commit v5 on v4

--- a/solution.py
+++ b/solution.py
@@ -240,15 +240,20 @@
     from_prev, from_next = lax.ppermute(first, "depth", up), lax.ppermute(second, "depth", down)
 
     core = [(r, r ^ 1) for r in range(n_row)]
-    chip = [(r, min(max(r - 1 + 2 * (r % 2), 0), n_row - 1)) for r in range(n_row)]
+    chip = []
+    for r in range(n_row):
+        for c in range(n_col):
+            step = r - 1 + 2 * (r % 2)
+            inside = 0 <= step < n_row
+            chip.append((r * n_col + c, (step % n_row) * n_col + (c if inside else c ^ 1)))
 
     far, turned = tie((far, turned))
     fetch = [((c - 2 + 4 * (c % 2)) % n_col, c) for c in range(n_col)]
     other = lax.ppermute(far, "col", fetch)
     pair = jnp.concatenate([far, packed[: rows - MOVED]], axis=0)
     other_and = jnp.concatenate([other, packed[rows - MOVED :]], axis=0)
-    chip_pair, core_pair = lax.ppermute(pair, "row", chip), lax.ppermute(pair, "row", core)
-    chip_other, core_other = lax.ppermute(other_and, "row", chip), lax.ppermute(other_and, "row", core)
+    chip_pair, core_pair = lax.ppermute(pair, ("row", "col"), chip), lax.ppermute(pair, "row", core)
+    chip_other, core_other = lax.ppermute(other_and, ("row", "col"), chip), lax.ppermute(other_and, "row", core)
 
     sends = struct(TRASH + 1, *piece, dtype=jnp.float32)
     halos = struct(9 * rows, *piece)

time: 39.2 us -> 37.9 us (0.967)
  waiting for transfers between devices: 5.36 us -> 4.09 us
    ppermute x2, starting transfers between devices: 10.1 us -> 5.91 us  [the longest x1 3.89 us: per_device(): lax.ppermute(pair, ('row', 'col'), chip)]
    ppermute x1, starting transfers between devices: 0.09 us -> 2.53 us  [per_device(): lax.ppermute(pair, 'row', core)]
    ppermute x1, starting transfers between devices: 0.09 us -> 1.83 us  [per_device(): lax.ppermute(other_and, 'row', core)]
    ppermute x2, waiting for transfers between devices: 2.5 us -> 1.1 us  [the longest x1 1.1 us: per_device(): lax.ppermute(other_and, ('row', 'col'), chip)]
  transfers between devices with their start and end apart: 10 -> 10, of which waited for: 3 -> 2; matrix products, arithmetic and copies ran while one was open for 0% -> 0% of each run, Pallas kernels for 11% -> 12%
where the time goes in v5:
time: 37.9 us; the launch traced here: 37.5 us
  starting transfers between devices  24.9 us (66%)
  Pallas kernels  7.44 us (20%)
  waiting for transfers between devices  4.09 us (11%)
  local copies, waits for them, and re-layouts  0.96 us (3%)
    ppermute x1, starting transfers between devices, per_device(): far = lax.ppermute(packed, 'col', [(c, c ^ 1) for c in range(n_col)])  7.83 us
    ppermute x1, starting transfers between devices, per_device(): lax.ppermute(pair, ('row', 'col'), chip)  3.89 us
    ppermute x1, waiting for transfers between devices, per_device(): lax.ppermute(after, 'depth', up)  2.97 us
    ppermute x1, starting transfers between devices, per_device(): lax.ppermute(pair, 'row', core)  2.53 us
    ppermute x1, starting transfers between devices, per_device(): lax.ppermute(other_and, ('row', 'col'), chip)  2.02 us
    pallas_call x1, Pallas kernels, per_device(): pl.pallas_call(own_kernel, out_shape=sends, in_specs=[SMEM] + [VMEM] * 3,...  2.02 us
    pallas_call x1, Pallas kernels, per_device(): pl.pallas_call(late_kernel, out_shape=[halos, struct(SC, *piece), struct(...  1.92 us
    ppermute x1, starting transfers between devices, per_device(): lax.ppermute(other_and, 'row', core)  1.83 us
  transfers between devices with their start and end apart: 10, of which 2 were waited for; matrix products, arithmetic and copies ran while one was open for 0% of the time, Pallas kernels for 12%

profile of v5, /device:TPU:1, one launch (start us, length us, event | category | flops | bytes accessed | tf_op | source)
XLA Modules:
  0.0 37.5 jit_solution(16377830382327793825)
XLA Ops:
  0.0 0.0 copy-start
  0.0 0.9 %copy-done = bf16[16,64,64]{2,1,0:T(8,128)(2,1)S(1)} copy-done((bf16[16,64,64]{2,1,0:T(8,128)(2,1)S(1)}, bf16[16,64,64]{2,1,0:T(8,128)(2,1)}, u32[]{:S(2)}) %copy-start) | copy-done | bytes 131096
  1.0 0.1 pack.1.packed_ref
  1.1 7.8 %collective-permute-start.2 = (bf16[16,32,128]{2,1,0:T(8,128)(2,1)S(1)}, bf16[16,32,128]{2,1,0:T(8,128)(2,1)S(1)}, u32[]{:S(2)}, u32[]{:S(2)}) collective-permute-start(bf16[16,32,128]{2,1,0:T(8,128)(2,1)S(1)} %pack.1.packed_ref), channel_id=1, source_target_pairs={{0,4},{4,0},{8,12},{12,8},{16,20},{20,16},{24,28},{28,24},{1,5},{5... | collective-permute-start | bytes 393224 | tf_op jit(solution)/shard_map/ppermute | solution.py:218
  8.9 1.6 %blocks.1 = (bf16[57,32,128]{2,1,0:T(8,128)(2,1)S(1)}, bf16[57,32,128]{2,1,0:T(8,128)(2,1)S(1)}, bf16[16,64,64]{2,1,0:T(8,128)(2,1)S(1)}, s32[16,16]{1,0:T(8,128)S(1)}) custom-call(bf16[112,64,64]{2,1,0:T(8,128)(2,1)} %bitcast.5, bf16[16,32,128]{2,1,0:T(8,128)(2,1)S(1)} %pack.1.packed_ref, s32[7,16]{1,0:T(8,128)} %bitcast.6, s32[7,16]{1,0:T(8,128)} %bitcast.7, ...), custom_call_target="tpu_custom_call" | custom-call | tf_op jit(solution)/shard_map/blocks/pallas_call | solution.py:223
  10.5 1.3 %collective-permute-start = (bf16[57,32,128]{2,1,0:T(8,128)(2,1)S(1)}, bf16[57,32,128]{2,1,0:T(8,128)(2,1)S(1)}, u32[]{:S(2)}, u32[]{:S(2)}) collective-permute-start(bf16[57,32,128]{2,1,0:T(8,128)(2,1)S(1)} %get-tuple-element.18.first_ref), channel_id=1, source_target_pairs={{0,1},{1,2},{2,3},{3,0},{4,5},{5,6},{6,7},{7,4},{8,9},{9,10},{10,1... | collective-permute-start | bytes 1400840 | tf_op jit(solution)/shard_map/ppermute | solution.py:240
  11.8 1.5 %collective-permute-start.1 = (bf16[57,32,128]{2,1,0:T(8,128)(2,1)S(1)}, bf16[57,32,128]{2,1,0:T(8,128)(2,1)S(1)}, u32[]{:S(2)}, u32[]{:S(2)}) collective-permute-start(bf16[57,32,128]{2,1,0:T(8,128)(2,1)S(1)} %get-tuple-element.19.second_ref), channel_id=1, source_target_pairs={{1,0},{2,1},{3,2},{0,3},{5,4},{6,5},{7,6},{4,7},{9,8},{10,9},{11,1... | collective-permute-start | bytes 1400840 | tf_op jit(solution)/shard_map/ppermute | solution.py:240
  13.3 0.0 collective-permute-done.2.far_ref
  13.3 1.3 %collective-permute-start.3 = (bf16[16,32,128]{2,1,0:T(8,128)(2,1)S(1)}, bf16[16,32,128]{2,1,0:T(8,128)(2,1)S(1)}, u32[]{:S(2)}, u32[]{:S(2)}) collective-permute-start(bf16[16,32,128]{2,1,0:T(8,128)(2,1)S(1)} %collective-permute-done.2.far_ref), channel_id=1, source_target_pairs={{24,0},{12,4},{0,8},{20,12},{8,16},{28,20},{16,24},{4,28},{25,1},{... | collective-permute-start | bytes 393224 | tf_op jit(solution)/shard_map/ppermute | solution.py:252
  14.6 3.9 %collective-permute-start.4 = (bf16[24,32,128]{2,1,0:T(8,128)(2,1)S(1)}, bf16[24,32,128]{2,1,0:T(8,128)(2,1)S(1)}, u32[]{:S(2)}, u32[]{:S(2)}) collective-permute-start(bf16[24,32,128]{2,1,0:T(8,128)(2,1)S(1)} %pad_maximum_fusion), channel_id=1, source_target_pairs={{0,228},{4,224},{8,236},{12,232},{16,244},{20,240},{24,252},{28,24... | collective-permute-start | bytes 589832 | tf_op jit(solution)/shard_map/ppermute | solution.py:255
  18.5 2.5 %collective-permute-start.5 = (bf16[24,32,128]{2,1,0:T(8,128)(2,1)S(1)}, bf16[24,32,128]{2,1,0:T(8,128)(2,1)S(1)}, u32[]{:S(2)}, u32[]{:S(2)}) collective-permute-start(bf16[24,32,128]{2,1,0:T(8,128)(2,1)S(1)} %pad_maximum_fusion), channel_id=1, source_target_pairs={{0,32},{32,0},{64,96},{96,64},{128,160},{160,128},{192,224},{224,1... | collective-permute-start | bytes 589832 | tf_op jit(solution)/shard_map/ppermute | solution.py:255
  21.1 0.0 collective-permute-done.3.other_ref
  21.1 2.0 %collective-permute-start.6 = (bf16[24,32,128]{2,1,0:T(8,128)(2,1)S(1)}, bf16[24,32,128]{2,1,0:T(8,128)(2,1)S(1)}, u32[]{:S(2)}, u32[]{:S(2)}) collective-permute-start(bf16[24,32,128]{2,1,0:T(8,128)(2,1)S(1)} %pad_maximum_fusion.1), channel_id=1, source_target_pairs={{0,228},{4,224},{8,236},{12,232},{16,244},{20,240},{24,252},{28,24... | collective-permute-start | bytes 589832 | tf_op jit(solution)/shard_map/ppermute | solution.py:256
  23.1 0.0 collective-permute-done.prev_ref
  23.1 1.8 %collective-permute-start.7 = (bf16[24,32,128]{2,1,0:T(8,128)(2,1)S(1)}, bf16[24,32,128]{2,1,0:T(8,128)(2,1)S(1)}, u32[]{:S(2)}, u32[]{:S(2)}) collective-permute-start(bf16[24,32,128]{2,1,0:T(8,128)(2,1)S(1)} %pad_maximum_fusion.1), channel_id=1, source_target_pairs={{0,32},{32,0},{64,96},{96,64},{128,160},{160,128},{192,224},{224,1... | collective-permute-start | bytes 589832 | tf_op jit(solution)/shard_map/ppermute | solution.py:256
  24.9 0.0 collective-permute-done.1.next_ref
  24.9 0.7 %early.1 = (s32[1,640]{1,0:T(1,128)S(1)}, bf16[224,32,128]{2,1,0:T(8,128)(2,1)S(1)}, bf16[144,32,128]{2,1,0:T(8,128)(2,1)S(1)}) custom-call(s32[16,16]{1,0:T(8,128)S(1)} %get-tuple-element.17.ints_ref, bf16[57,32,128]{2,1,0:T(8,128)(2,1)S(1)} %get-tuple-element.18.first_ref, bf16[57,32,128]{2,1,0:T(8,128)(2,1)S(1)} %get-tuple-element.19.second_ref, ...), custom_call_target="tpu_custom_call" | custom-call | tf_op jit(solution)/shard_map/early/pallas_call | solution.py:260
  25.6 0.0 collective-permute-done.4.chip_pair
  25.6 0.0 collective-permute-done.5.core_pair
  25.7 1.1 %collective-permute-done.6.chip_ref = bf16[24,32,128]{2,1,0:T(8,128)(2,1)S(1)} collective-permute-done((bf16[24,32,128]{2,1,0:T(8,128)(2,1)S(1)}, bf16[24,32,128]{2,1,0:T(8,128)(2,1)S(1)}, u32[]{:S(2)}, u32[]{:S(2)}) %collective-permute-start.6) | collective-permute-done | bytes 196640 | tf_op jit(solution)/shard_map/ppermute | solution.py:256
  26.8 0.0 collective-permute-done.7.core_ref
  26.8 1.9 %late.1 = (bf16[144,32,128]{2,1,0:T(8,128)(2,1)S(1)}, bf16[28,32,128]{2,1,0:T(8,128)(2,1)S(1)}, bf16[28,32,128]{2,1,0:T(8,128)(2,1)S(1)}) custom-call(s32[1,640]{1,0:T(1,128)S(1)} %get-tuple-element.22.list_ref, bf16[224,32,128]{2,1,0:T(8,128)(2,1)S(1)} %get-tuple-element.23.blocks_ref, ...), custom_call_target="tpu_custom_call", output_to_operand_aliasing={{0}: (7, {})} | custom-call | tf_op jit(solution)/shard_map/late/pallas_call | solution.py:269
  28.7 1.2 %collective-permute-start.8 = (bf16[28,32,128]{2,1,0:T(8,128)(2,1)S(1)}, bf16[28,32,128]{2,1,0:T(8,128)(2,1)S(1)}, u32[]{:S(2)}, u32[]{:S(2)}) collective-permute-start(bf16[28,32,128]{2,1,0:T(8,128)(2,1)S(1)} %get-tuple-element.27), channel_id=1, source_target_pairs={{0,1},{1,2},{2,3},{3,0},{4,5},{5,6},{6,7},{7,4},{8,9},{9,10},{10,1... | collective-permute-start | bytes 688136 | tf_op jit(solution)/shard_map/ppermute | solution.py:279
  29.9 1.5 %collective-permute-start.9 = (bf16[28,32,128]{2,1,0:T(8,128)(2,1)S(1)}, bf16[28,32,128]{2,1,0:T(8,128)(2,1)S(1)}, u32[]{:S(2)}, u32[]{:S(2)}) collective-permute-start(bf16[28,32,128]{2,1,0:T(8,128)(2,1)S(1)} %get-tuple-element.28), channel_id=1, source_target_pairs={{1,0},{2,1},{3,2},{0,3},{5,4},{6,5},{7,6},{4,7},{9,8},{10,9},{11,1... | collective-permute-start | bytes 688136 | tf_op jit(solution)/shard_map/ppermute | solution.py:279
  31.4 2.0 %own.1.own_ref = f32[57,32,128]{2,1,0:T(8,128)S(1)} custom-call(s32[1,640]{1,0:T(1,128)S(1)} %get-tuple-element.22.list_ref, bf16[224,32,128]{2,1,0:T(8,128)(2,1)S(1)} %get-tuple-element.23.blocks_ref, bf16[16,64,64]{2,1,0:T(8,128)(2,1)S(1)} %get-tuple-element.24.turned_ref, bf16[144,32,128]{2,1,0:T(8,128)(2,1)S(1)} %get-tuple-element.26.halo_ref), custom_call_target="tpu_custom_call" | custom-call | tf_op jit(solution)/shard_map/own/pallas_call | solution.py:280
  33.5 3.0 %collective-permute-done.8.one_ref = bf16[28,32,128]{2,1,0:T(8,128)(2,1)S(1)} collective-permute-done((bf16[28,32,128]{2,1,0:T(8,128)(2,1)S(1)}, bf16[28,32,128]{2,1,0:T(8,128)(2,1)S(1)}, u32[]{:S(2)}, u32[]{:S(2)}) %collective-permute-start.8) | collective-permute-done | bytes 229408 | tf_op jit(solution)/shard_map/ppermute | solution.py:279
  36.4 0.0 collective-permute-done.9.two_ref
  36.4 1.1 %total.1 = f32[4,7,64,64]{3,2,1,0:T(8,128)} custom-call(f32[57,32,128]{2,1,0:T(8,128)S(1)} %own.1.own_ref, bf16[28,32,128]{2,1,0:T(8,128)(2,1)S(1)} %collective-permute-done.8.one_ref, bf16[28,32,128]{2,1,0:T(8,128)(2,1)S(1)} %collective-permute-done.9.two_ref), custom_call_target="tpu_custom_call" | custom-call | tf_op jit(solution)/shard_map/total/pallas_call | solution.py:288
  (3 shorter events, 0.0 us)
Async XLA Ops:
  0.0 0.9 %copy-start = (bf16[16,64,64]{2,1,0:T(8,128)(2,1)S(1)}, bf16[16,64,64]{2,1,0:T(8,128)(2,1)}, u32[]{:S(2)}) copy-start(bf16[16,64,64]{2,1,0:T(8,128)(2,1)} %prolong_ref.1) | copy-start | bytes 393220
  1.1 12.2 %collective-permute-start.2 = (bf16[16,32,128]{2,1,0:T(8,128)(2,1)S(1)}, bf16[16,32,128]{2,1,0:T(8,128)(2,1)S(1)}, u32[]{:S(2)}, u32[]{:S(2)}) collective-permute-start(bf16[16,32,128]{2,1,0:T(8,128)(2,1)S(1)} %pack.1.packed_ref), channel_id=1, source_target_pairs={{0,4},{4,0},{8,12},{12,8},{16,20},{20,16},{24,28},{28,24},{1,5},{5... | collective-permute-start | bytes 393224 | tf_op jit(solution)/shard_map/ppermute | solution.py:218
  10.5 12.6 %collective-permute-start = (bf16[57,32,128]{2,1,0:T(8,128)(2,1)S(1)}, bf16[57,32,128]{2,1,0:T(8,128)(2,1)S(1)}, u32[]{:S(2)}, u32[]{:S(2)}) collective-permute-start(bf16[57,32,128]{2,1,0:T(8,128)(2,1)S(1)} %get-tuple-element.18.first_ref), channel_id=1, source_target_pairs={{0,1},{1,2},{2,3},{3,0},{4,5},{5,6},{6,7},{7,4},{8,9},{9,10},{10,1... | collective-permute-start | bytes 1400840 | tf_op jit(solution)/shard_map/ppermute | solution.py:240
  11.8 13.1 %collective-permute-start.1 = (bf16[57,32,128]{2,1,0:T(8,128)(2,1)S(1)}, bf16[57,32,128]{2,1,0:T(8,128)(2,1)S(1)}, u32[]{:S(2)}, u32[]{:S(2)}) collective-permute-start(bf16[57,32,128]{2,1,0:T(8,128)(2,1)S(1)} %get-tuple-element.19.second_ref), channel_id=1, source_target_pairs={{1,0},{2,1},{3,2},{0,3},{5,4},{6,5},{7,6},{4,7},{9,8},{10,9},{11,1... | collective-permute-start | bytes 1400840 | tf_op jit(solution)/shard_map/ppermute | solution.py:240
  13.3 7.8 %collective-permute-start.3 = (bf16[16,32,128]{2,1,0:T(8,128)(2,1)S(1)}, bf16[16,32,128]{2,1,0:T(8,128)(2,1)S(1)}, u32[]{:S(2)}, u32[]{:S(2)}) collective-permute-start(bf16[16,32,128]{2,1,0:T(8,128)(2,1)S(1)} %collective-permute-done.2.far_ref), channel_id=1, source_target_pairs={{24,0},{12,4},{0,8},{20,12},{8,16},{28,20},{16,24},{4,28},{25,1},{... | collective-permute-start | bytes 393224 | tf_op jit(solution)/shard_map/ppermute | solution.py:252
  14.6 11.0 %collective-permute-start.4 = (bf16[24,32,128]{2,1,0:T(8,128)(2,1)S(1)}, bf16[24,32,128]{2,1,0:T(8,128)(2,1)S(1)}, u32[]{:S(2)}, u32[]{:S(2)}) collective-permute-start(bf16[24,32,128]{2,1,0:T(8,128)(2,1)S(1)} %pad_maximum_fusion), channel_id=1, source_target_pairs={{0,228},{4,224},{8,236},{12,232},{16,244},{20,240},{24,252},{28,24... | collective-permute-start | bytes 589832 | tf_op jit(solution)/shard_map/ppermute | solution.py:255
  18.5 7.1 %collective-permute-start.5 = (bf16[24,32,128]{2,1,0:T(8,128)(2,1)S(1)}, bf16[24,32,128]{2,1,0:T(8,128)(2,1)S(1)}, u32[]{:S(2)}, u32[]{:S(2)}) collective-permute-start(bf16[24,32,128]{2,1,0:T(8,128)(2,1)S(1)} %pad_maximum_fusion), channel_id=1, source_target_pairs={{0,32},{32,0},{64,96},{96,64},{128,160},{160,128},{192,224},{224,1... | collective-permute-start | bytes 589832 | tf_op jit(solution)/shard_map/ppermute | solution.py:255
  21.1 5.7 %collective-permute-start.6 = (bf16[24,32,128]{2,1,0:T(8,128)(2,1)S(1)}, bf16[24,32,128]{2,1,0:T(8,128)(2,1)S(1)}, u32[]{:S(2)}, u32[]{:S(2)}) collective-permute-start(bf16[24,32,128]{2,1,0:T(8,128)(2,1)S(1)} %pad_maximum_fusion.1), channel_id=1, source_target_pairs={{0,228},{4,224},{8,236},{12,232},{16,244},{20,240},{24,252},{28,24... | collective-permute-start | bytes 589832 | tf_op jit(solution)/shard_map/ppermute | solution.py:256
  23.1 3.6 %collective-permute-start.7 = (bf16[24,32,128]{2,1,0:T(8,128)(2,1)S(1)}, bf16[24,32,128]{2,1,0:T(8,128)(2,1)S(1)}, u32[]{:S(2)}, u32[]{:S(2)}) collective-permute-start(bf16[24,32,128]{2,1,0:T(8,128)(2,1)S(1)} %pad_maximum_fusion.1), channel_id=1, source_target_pairs={{0,32},{32,0},{64,96},{96,64},{128,160},{160,128},{192,224},{224,1... | collective-permute-start | bytes 589832 | tf_op jit(solution)/shard_map/ppermute | solution.py:256
  28.7 7.7 %collective-permute-start.8 = (bf16[28,32,128]{2,1,0:T(8,128)(2,1)S(1)}, bf16[28,32,128]{2,1,0:T(8,128)(2,1)S(1)}, u32[]{:S(2)}, u32[]{:S(2)}) collective-permute-start(bf16[28,32,128]{2,1,0:T(8,128)(2,1)S(1)} %get-tuple-element.27), channel_id=1, source_target_pairs={{0,1},{1,2},{2,3},{3,0},{4,5},{5,6},{6,7},{7,4},{8,9},{9,10},{10,1... | collective-permute-start | bytes 688136 | tf_op jit(solution)/shard_map/ppermute | solution.py:279
  29.9 6.5 %collective-permute-start.9 = (bf16[28,32,128]{2,1,0:T(8,128)(2,1)S(1)}, bf16[28,32,128]{2,1,0:T(8,128)(2,1)S(1)}, u32[]{:S(2)}, u32[]{:S(2)}) collective-permute-start(bf16[28,32,128]{2,1,0:T(8,128)(2,1)S(1)} %get-tuple-element.28), channel_id=1, source_target_pairs={{1,0},{2,1},{3,2},{0,3},{5,4},{6,5},{7,6},{4,7},{9,8},{10,9},{11,1... | collective-permute-start | bytes 688136 | tf_op jit(solution)/shard_map/ppermute | solution.py:279

commit v6 on v5

--- a/solution.py
+++ b/solution.py
@@ -16,7 +16,8 @@
 SMALL = pl.CostEstimate(flops=1000, bytes_accessed=1000, transcendentals=0)
 LIST = 320
 CUTS = 4
-MOVED = 8
+MOVED_CHIP = 2
+MOVED_CORE = 9
 SEND, OWN = range(2)
 TRASH = 2 * SC
 
@@ -250,10 +251,14 @@
     far, turned = tie((far, turned))
     fetch = [((c - 2 + 4 * (c % 2)) % n_col, c) for c in range(n_col)]
     other = lax.ppermute(far, "col", fetch)
-    pair = jnp.concatenate([far, packed[: rows - MOVED]], axis=0)
-    other_and = jnp.concatenate([other, packed[rows - MOVED :]], axis=0)
-    chip_pair, core_pair = lax.ppermute(pair, ("row", "col"), chip), lax.ppermute(pair, "row", core)
-    chip_other, core_other = lax.ppermute(other_and, ("row", "col"), chip), lax.ppermute(other_and, "row", core)
+    def cut(moved):
+        pair = jnp.concatenate([far, packed[: rows - moved]], axis=0)
+        return pair, jnp.concatenate([other, packed[rows - moved :]], axis=0)
+
+    (chip_pair, chip_other), (core_pair, core_other) = (
+        [lax.ppermute(part, axes, perm) for part in cut(moved)]
+        for axes, perm, moved in ((("row", "col"), chip, MOVED_CHIP), ("row", core, MOVED_CORE))
+    )
 
     sends = struct(TRASH + 1, *piece, dtype=jnp.float32)
     halos = struct(9 * rows, *piece)

time: 37.9 us -> 40.1 us (1.058)
  the two profiles are of different devices: /device:TPU:1 before, /device:TPU:6 now
where the time goes in v6:
time: 40.1 us; the launch traced here: 40 us
  starting transfers between devices  20.6 us (51%)
  waiting for transfers between devices  10.7 us (27%)
  Pallas kernels  7.45 us (19%)
  local copies, waits for them, and re-layouts  0.97 us (2%)
    ppermute x4, starting transfers between devices, per_device(): lax.ppermute(part, axes, perm)  7.51 us
    ppermute x1, starting transfers between devices, per_device(): far = lax.ppermute(packed, 'col', [(c, c ^ 1) for c in range(n_col)])  7.28 us
    ppermute x4, waiting for transfers between devices, per_device(): lax.ppermute(part, axes, perm)  3.66 us
    ppermute x1, waiting for transfers between devices, per_device(): lax.ppermute(before, 'depth', down)  2.88 us
    pallas_call x1, Pallas kernels, per_device(): pl.pallas_call(own_kernel, out_shape=sends, in_specs=[SMEM] + [VMEM] * 3,...  2.04 us
    ppermute x1, waiting for transfers between devices, per_device(): lax.ppermute(after, 'depth', up)  1.95 us
    ppermute x1, waiting for transfers between devices, per_device(): lax.ppermute(first, 'depth', up)  1.93 us
    pallas_call x1, Pallas kernels, per_device(): pl.pallas_call(late_kernel, out_shape=[halos, struct(SC, *piece), struct(...  1.91 us
  transfers between devices with their start and end apart: 10, of which 5 were waited for; matrix products, arithmetic and copies ran while one was open for 0% of the time, Pallas kernels for 11%

profile of v6, /device:TPU:6, one launch (start us, length us, event | category | flops | bytes accessed | tf_op | source)
XLA Modules:
  0.0 40.0 jit_solution(10297219022093385390)
XLA Ops:
  0.0 0.0 copy-start
  0.0 0.9 %copy-done = bf16[16,64,64]{2,1,0:T(8,128)(2,1)S(1)} copy-done((bf16[16,64,64]{2,1,0:T(8,128)(2,1)S(1)}, bf16[16,64,64]{2,1,0:T(8,128)(2,1)}, u32[]{:S(2)}) %copy-start) | copy-done | bytes 131096
  1.0 0.1 pack.1.packed_ref
  1.1 7.3 %collective-permute-start.2 = (bf16[16,32,128]{2,1,0:T(8,128)(2,1)S(1)}, bf16[16,32,128]{2,1,0:T(8,128)(2,1)S(1)}, u32[]{:S(2)}, u32[]{:S(2)}) collective-permute-start(bf16[16,32,128]{2,1,0:T(8,128)(2,1)S(1)} %pack.1.packed_ref), channel_id=1, source_target_pairs={{0,4},{4,0},{8,12},{12,8},{16,20},{20,16},{24,28},{28,24},{1,5},{5... | collective-permute-start | bytes 393224 | tf_op jit(solution)/shard_map/ppermute | solution.py:219
  8.3 1.6 %blocks.1 = (bf16[57,32,128]{2,1,0:T(8,128)(2,1)S(1)}, bf16[57,32,128]{2,1,0:T(8,128)(2,1)S(1)}, bf16[16,64,64]{2,1,0:T(8,128)(2,1)S(1)}, s32[16,16]{1,0:T(8,128)S(1)}) custom-call(bf16[112,64,64]{2,1,0:T(8,128)(2,1)} %bitcast.5, bf16[16,32,128]{2,1,0:T(8,128)(2,1)S(1)} %pack.1.packed_ref, s32[7,16]{1,0:T(8,128)} %bitcast.6, s32[7,16]{1,0:T(8,128)} %bitcast.7, ...), custom_call_target="tpu_custom_call" | custom-call | tf_op jit(solution)/shard_map/blocks/pallas_call | solution.py:224
  10.0 0.6 %collective-permute-start = (bf16[57,32,128]{2,1,0:T(8,128)(2,1)S(1)}, bf16[57,32,128]{2,1,0:T(8,128)(2,1)S(1)}, u32[]{:S(2)}, u32[]{:S(2)}) collective-permute-start(bf16[57,32,128]{2,1,0:T(8,128)(2,1)S(1)} %get-tuple-element.18.first_ref), channel_id=1, source_target_pairs={{0,1},{1,2},{2,3},{3,0},{4,5},{5,6},{6,7},{7,4},{8,9},{9,10},{10,1... | collective-permute-start | bytes 1400840 | tf_op jit(solution)/shard_map/ppermute | solution.py:241
  10.5 1.5 %collective-permute-start.1 = (bf16[57,32,128]{2,1,0:T(8,128)(2,1)S(1)}, bf16[57,32,128]{2,1,0:T(8,128)(2,1)S(1)}, u32[]{:S(2)}, u32[]{:S(2)}) collective-permute-start(bf16[57,32,128]{2,1,0:T(8,128)(2,1)S(1)} %get-tuple-element.19.second_ref), channel_id=1, source_target_pairs={{1,0},{2,1},{3,2},{0,3},{5,4},{6,5},{7,6},{4,7},{9,8},{10,9},{11,1... | collective-permute-start | bytes 1400840 | tf_op jit(solution)/shard_map/ppermute | solution.py:241
  12.1 0.0 collective-permute-done.2.far_ref
  12.1 1.7 %collective-permute-start.3 = (bf16[16,32,128]{2,1,0:T(8,128)(2,1)S(1)}, bf16[16,32,128]{2,1,0:T(8,128)(2,1)S(1)}, u32[]{:S(2)}, u32[]{:S(2)}) collective-permute-start(bf16[16,32,128]{2,1,0:T(8,128)(2,1)S(1)} %collective-permute-done.2.far_ref), channel_id=1, source_target_pairs={{24,0},{12,4},{0,8},{20,12},{8,16},{28,20},{16,24},{4,28},{25,1},{... | collective-permute-start | bytes 393224 | tf_op jit(solution)/shard_map/ppermute | solution.py:253
  13.8 5.7 %collective-permute-start.4 = (bf16[30,32,128]{2,1,0:T(8,128)(2,1)S(1)}, bf16[30,32,128]{2,1,0:T(8,128)(2,1)S(1)}, u32[]{:S(2)}, u32[]{:S(2)}) collective-permute-start(bf16[30,32,128]{2,1,0:T(8,128)(2,1)S(1)} %pad_maximum_fusion), channel_id=1, source_target_pairs={{0,228},{4,224},{8,236},{12,232},{16,244},{20,240},{24,252},{28,24... | collective-permute-start | bytes 737288 | tf_op jit(solution)/shard_map/ppermute | solution.py:259
  19.6 0.1 collective-permute-start.5
  19.7 0.0 collective-permute-done.3.other_ref
  19.7 0.6 %collective-permute-start.7 = (bf16[25,32,128]{2,1,0:T(8,128)(2,1)S(1)}, bf16[25,32,128]{2,1,0:T(8,128)(2,1)S(1)}, u32[]{:S(2)}, u32[]{:S(2)}) collective-permute-start(bf16[25,32,128]{2,1,0:T(8,128)(2,1)S(1)} %pad_maximum_fusion.1), channel_id=1, source_target_pairs={{0,32},{32,0},{64,96},{96,64},{128,160},{160,128},{192,224},{224,1... | collective-permute-start | bytes 614408 | tf_op jit(solution)/shard_map/ppermute | solution.py:259
  20.3 1.9 %collective-permute-done.prev_ref = bf16[57,32,128]{2,1,0:T(8,128)(2,1)S(1)} collective-permute-done((bf16[57,32,128]{2,1,0:T(8,128)(2,1)S(1)}, bf16[57,32,128]{2,1,0:T(8,128)(2,1)S(1)}, u32[]{:S(2)}, u32[]{:S(2)}) %collective-permute-start) | collective-permute-done | bytes 466976 | tf_op jit(solution)/shard_map/ppermute | solution.py:241
  22.2 1.1 %collective-permute-start.6 = (bf16[18,32,128]{2,1,0:T(8,128)(2,1)S(1)}, bf16[18,32,128]{2,1,0:T(8,128)(2,1)S(1)}, u32[]{:S(2)}, u32[]{:S(2)}) collective-permute-start(bf16[18,32,128]{2,1,0:T(8,128)(2,1)S(1)} %pad_maximum_fusion.3), channel_id=1, source_target_pairs={{0,228},{4,224},{8,236},{12,232},{16,244},{20,240},{24,252},{28,24... | collective-permute-start | bytes 442376 | tf_op jit(solution)/shard_map/ppermute | solution.py:259
  23.4 0.3 collective-permute-done.1.next_ref
  23.6 0.7 %early.1 = (s32[1,640]{1,0:T(1,128)S(1)}, bf16[224,32,128]{2,1,0:T(8,128)(2,1)S(1)}, bf16[144,32,128]{2,1,0:T(8,128)(2,1)S(1)}) custom-call(s32[16,16]{1,0:T(8,128)S(1)} %get-tuple-element.17.ints_ref, bf16[57,32,128]{2,1,0:T(8,128)(2,1)S(1)} %get-tuple-element.18.first_ref, bf16[57,32,128]{2,1,0:T(8,128)(2,1)S(1)} %get-tuple-element.19.second_ref, ...), custom_call_target="tpu_custom_call" | custom-call | tf_op jit(solution)/shard_map/early/pallas_call | solution.py:265
  24.3 0.0 collective-permute-done.5.core_pair
  24.3 0.0 collective-permute-done.4.chip_pair
  24.3 3.7 %collective-permute-done.6.chip_ref = bf16[18,32,128]{2,1,0:T(8,128)(2,1)S(1)} collective-permute-done((bf16[18,32,128]{2,1,0:T(8,128)(2,1)S(1)}, bf16[18,32,128]{2,1,0:T(8,128)(2,1)S(1)}, u32[]{:S(2)}, u32[]{:S(2)}) %collective-permute-start.6) | collective-permute-done | bytes 147488 | tf_op jit(solution)/shard_map/ppermute | solution.py:259
  28.0 0.0 collective-permute-done.7.core_ref
  28.0 1.9 %late.1 = (bf16[144,32,128]{2,1,0:T(8,128)(2,1)S(1)}, bf16[28,32,128]{2,1,0:T(8,128)(2,1)S(1)}, bf16[28,32,128]{2,1,0:T(8,128)(2,1)S(1)}) custom-call(s32[1,640]{1,0:T(1,128)S(1)} %get-tuple-element.22.list_ref, bf16[224,32,128]{2,1,0:T(8,128)(2,1)S(1)} %get-tuple-element.23.blocks_ref, ...), custom_call_target="tpu_custom_call", output_to_operand_aliasing={{0}: (7, {})} | custom-call | tf_op jit(solution)/shard_map/late/pallas_call | solution.py:274
  29.9 1.8 %collective-permute-start.8 = (bf16[28,32,128]{2,1,0:T(8,128)(2,1)S(1)}, bf16[28,32,128]{2,1,0:T(8,128)(2,1)S(1)}, u32[]{:S(2)}, u32[]{:S(2)}) collective-permute-start(bf16[28,32,128]{2,1,0:T(8,128)(2,1)S(1)} %get-tuple-element.27), channel_id=1, source_target_pairs={{0,1},{1,2},{2,3},{3,0},{4,5},{5,6},{6,7},{7,4},{8,9},{9,10},{10,1... | collective-permute-start | bytes 688136 | tf_op jit(solution)/shard_map/ppermute | solution.py:284
  31.7 0.4 collective-permute-start.9
  32.0 2.0 %own.1.own_ref = f32[57,32,128]{2,1,0:T(8,128)S(1)} custom-call(s32[1,640]{1,0:T(1,128)S(1)} %get-tuple-element.22.list_ref, bf16[224,32,128]{2,1,0:T(8,128)(2,1)S(1)} %get-tuple-element.23.blocks_ref, bf16[16,64,64]{2,1,0:T(8,128)(2,1)S(1)} %get-tuple-element.24.turned_ref, bf16[144,32,128]{2,1,0:T(8,128)(2,1)S(1)} %get-tuple-element.26.halo_ref), custom_call_target="tpu_custom_call" | custom-call | tf_op jit(solution)/shard_map/own/pallas_call | solution.py:285
  34.1 2.0 %collective-permute-done.8.one_ref = bf16[28,32,128]{2,1,0:T(8,128)(2,1)S(1)} collective-permute-done((bf16[28,32,128]{2,1,0:T(8,128)(2,1)S(1)}, bf16[28,32,128]{2,1,0:T(8,128)(2,1)S(1)}, u32[]{:S(2)}, u32[]{:S(2)}) %collective-permute-start.8) | collective-permute-done | bytes 229408 | tf_op jit(solution)/shard_map/ppermute | solution.py:284
  36.0 2.9 %collective-permute-done.9.two_ref = bf16[28,32,128]{2,1,0:T(8,128)(2,1)S(1)} collective-permute-done((bf16[28,32,128]{2,1,0:T(8,128)(2,1)S(1)}, bf16[28,32,128]{2,1,0:T(8,128)(2,1)S(1)}, u32[]{:S(2)}, u32[]{:S(2)}) %collective-permute-start.9) | collective-permute-done | bytes 229408 | tf_op jit(solution)/shard_map/ppermute | solution.py:284
  38.9 1.1 %total.1 = f32[4,7,64,64]{3,2,1,0:T(8,128)} custom-call(f32[57,32,128]{2,1,0:T(8,128)S(1)} %own.1.own_ref, bf16[28,32,128]{2,1,0:T(8,128)(2,1)S(1)} %collective-permute-done.8.one_ref, bf16[28,32,128]{2,1,0:T(8,128)(2,1)S(1)} %collective-permute-done.9.two_ref), custom_call_target="tpu_custom_call" | custom-call | tf_op jit(solution)/shard_map/total/pallas_call | solution.py:293
  (8 shorter events, 0.1 us)
Async XLA Ops:
  0.0 0.9 %copy-start = (bf16[16,64,64]{2,1,0:T(8,128)(2,1)S(1)}, bf16[16,64,64]{2,1,0:T(8,128)(2,1)}, u32[]{:S(2)}) copy-start(bf16[16,64,64]{2,1,0:T(8,128)(2,1)} %prolong_ref.1) | copy-start | bytes 393220
  1.1 11.1 %collective-permute-start.2 = (bf16[16,32,128]{2,1,0:T(8,128)(2,1)S(1)}, bf16[16,32,128]{2,1,0:T(8,128)(2,1)S(1)}, u32[]{:S(2)}, u32[]{:S(2)}) collective-permute-start(bf16[16,32,128]{2,1,0:T(8,128)(2,1)S(1)} %pack.1.packed_ref), channel_id=1, source_target_pairs={{0,4},{4,0},{8,12},{12,8},{16,20},{20,16},{24,28},{28,24},{1,5},{5... | collective-permute-start | bytes 393224 | tf_op jit(solution)/shard_map/ppermute | solution.py:219
  10.0 12.2 %collective-permute-start = (bf16[57,32,128]{2,1,0:T(8,128)(2,1)S(1)}, bf16[57,32,128]{2,1,0:T(8,128)(2,1)S(1)}, u32[]{:S(2)}, u32[]{:S(2)}) collective-permute-start(bf16[57,32,128]{2,1,0:T(8,128)(2,1)S(1)} %get-tuple-element.18.first_ref), channel_id=1, source_target_pairs={{0,1},{1,2},{2,3},{3,0},{4,5},{5,6},{6,7},{7,4},{8,9},{9,10},{10,1... | collective-permute-start | bytes 1400840 | tf_op jit(solution)/shard_map/ppermute | solution.py:241
  10.5 13.1 %collective-permute-start.1 = (bf16[57,32,128]{2,1,0:T(8,128)(2,1)S(1)}, bf16[57,32,128]{2,1,0:T(8,128)(2,1)S(1)}, u32[]{:S(2)}, u32[]{:S(2)}) collective-permute-start(bf16[57,32,128]{2,1,0:T(8,128)(2,1)S(1)} %get-tuple-element.19.second_ref), channel_id=1, source_target_pairs={{1,0},{2,1},{3,2},{0,3},{5,4},{6,5},{7,6},{4,7},{9,8},{10,9},{11,1... | collective-permute-start | bytes 1400840 | tf_op jit(solution)/shard_map/ppermute | solution.py:241
  12.1 7.5 %collective-permute-start.3 = (bf16[16,32,128]{2,1,0:T(8,128)(2,1)S(1)}, bf16[16,32,128]{2,1,0:T(8,128)(2,1)S(1)}, u32[]{:S(2)}, u32[]{:S(2)}) collective-permute-start(bf16[16,32,128]{2,1,0:T(8,128)(2,1)S(1)} %collective-permute-done.2.far_ref), channel_id=1, source_target_pairs={{24,0},{12,4},{0,8},{20,12},{8,16},{28,20},{16,24},{4,28},{25,1},{... | collective-permute-start | bytes 393224 | tf_op jit(solution)/shard_map/ppermute | solution.py:253
  13.8 10.5 %collective-permute-start.4 = (bf16[30,32,128]{2,1,0:T(8,128)(2,1)S(1)}, bf16[30,32,128]{2,1,0:T(8,128)(2,1)S(1)}, u32[]{:S(2)}, u32[]{:S(2)}) collective-permute-start(bf16[30,32,128]{2,1,0:T(8,128)(2,1)S(1)} %pad_maximum_fusion), channel_id=1, source_target_pairs={{0,228},{4,224},{8,236},{12,232},{16,244},{20,240},{24,252},{28,24... | collective-permute-start | bytes 737288 | tf_op jit(solution)/shard_map/ppermute | solution.py:259
  19.6 4.8 %collective-permute-start.5 = (bf16[23,32,128]{2,1,0:T(8,128)(2,1)S(1)}, bf16[23,32,128]{2,1,0:T(8,128)(2,1)S(1)}, u32[]{:S(2)}, u32[]{:S(2)}) collective-permute-start(bf16[23,32,128]{2,1,0:T(8,128)(2,1)S(1)} %pad_maximum_fusion.2), channel_id=1, source_target_pairs={{0,32},{32,0},{64,96},{96,64},{128,160},{160,128},{192,224},{224,1... | collective-permute-start | bytes 565256 | tf_op jit(solution)/shard_map/ppermute | solution.py:259
  19.7 8.3 %collective-permute-start.7 = (bf16[25,32,128]{2,1,0:T(8,128)(2,1)S(1)}, bf16[25,32,128]{2,1,0:T(8,128)(2,1)S(1)}, u32[]{:S(2)}, u32[]{:S(2)}) collective-permute-start(bf16[25,32,128]{2,1,0:T(8,128)(2,1)S(1)} %pad_maximum_fusion.1), channel_id=1, source_target_pairs={{0,32},{32,0},{64,96},{96,64},{128,160},{160,128},{192,224},{224,1... | collective-permute-start | bytes 614408 | tf_op jit(solution)/shard_map/ppermute | solution.py:259
  22.2 5.8 %collective-permute-start.6 = (bf16[18,32,128]{2,1,0:T(8,128)(2,1)S(1)}, bf16[18,32,128]{2,1,0:T(8,128)(2,1)S(1)}, u32[]{:S(2)}, u32[]{:S(2)}) collective-permute-start(bf16[18,32,128]{2,1,0:T(8,128)(2,1)S(1)} %pad_maximum_fusion.3), channel_id=1, source_target_pairs={{0,228},{4,224},{8,236},{12,232},{16,244},{20,240},{24,252},{28,24... | collective-permute-start | bytes 442376 | tf_op jit(solution)/shard_map/ppermute | solution.py:259
  29.9 6.1 %collective-permute-start.8 = (bf16[28,32,128]{2,1,0:T(8,128)(2,1)S(1)}, bf16[28,32,128]{2,1,0:T(8,128)(2,1)S(1)}, u32[]{:S(2)}, u32[]{:S(2)}) collective-permute-start(bf16[28,32,128]{2,1,0:T(8,128)(2,1)S(1)} %get-tuple-element.27), channel_id=1, source_target_pairs={{0,1},{1,2},{2,3},{3,0},{4,5},{5,6},{6,7},{7,4},{8,9},{9,10},{10,1... | collective-permute-start | bytes 688136 | tf_op jit(solution)/shard_map/ppermute | solution.py:284
  31.7 7.2 %collective-permute-start.9 = (bf16[28,32,128]{2,1,0:T(8,128)(2,1)S(1)}, bf16[28,32,128]{2,1,0:T(8,128)(2,1)S(1)}, u32[]{:S(2)}, u32[]{:S(2)}) collective-permute-start(bf16[28,32,128]{2,1,0:T(8,128)(2,1)S(1)} %get-tuple-element.28), channel_id=1, source_target_pairs={{1,0},{2,1},{3,2},{0,3},{5,4},{6,5},{7,6},{4,7},{9,8},{10,9},{11,1... | collective-permute-start | bytes 688136 | tf_op jit(solution)/shard_map/ppermute | solution.py:284

commit v7 on v5

--- a/solution.py
+++ b/solution.py
@@ -31,9 +31,18 @@
     return jnp.concatenate([block[:, :half], block[:, half:]], axis=0)
 
 
-def pack_kernel(prolong_ref, out_ref):
-    for i in range(prolong_ref.shape[0]):
-        out_ref[i] = fold(prolong_ref[i])
+def pack_kernel(prolong_hbm, out_ref, prolong_ref, sems):
+    size = prolong_ref.shape[0] // 2
+    copies = [
+        pltpu.make_async_copy(prolong_hbm.at[pl.ds(c * size, size)], prolong_ref.at[pl.ds(c * size, size)], sems.at[c])
+        for c in range(2)
+    ]
+    for copy in copies:
+        copy.start()
+    for c, copy in enumerate(copies):
+        copy.wait()
+        for i in range(c * size, (c + 1) * size):
+            out_ref[i] = fold(prolong_ref[i])
 
 
 def blocks_kernel(blocks_hbm, packed_ref, *refs):
@@ -213,8 +222,14 @@
         return jax.ShapeDtypeStruct(shape, dtype)
 
     packed = pl.pallas_call(
-        pack_kernel, out_shape=struct(rows, *piece), in_specs=[VMEM], out_specs=VMEM, compiler_params=LIMIT, name="pack"
-    )(prolong)
+        pack_kernel,
+        out_shape=struct(rows, *piece),
+        in_specs=[HBM],
+        out_specs=VMEM,
+        scratch_shapes=[pltpu.VMEM(prolong.shape, prolong.dtype), pltpu.SemaphoreType.DMA((2,))],
+        compiler_params=LIMIT,
+        name="pack",
+    )(pltpu.with_memory_space_constraint(prolong, pltpu.HBM))
     far = lax.ppermute(packed, "col", [(c, c ^ 1) for c in range(n_col)])
 
     half = rows * slots // 2

time: 37.9 us -> 37.9 us (level)
  Pallas kernels: 7.44 us -> 8.43 us
  local copies, waits for them, and re-layouts: 0.96 us -> 0.01 us
    pallas_call x1, Pallas kernels: 0.1 us -> 1.09 us  [per_device(): pl.pallas_call(pack_kernel, out_shape=struct(rows, *piece), in_specs=[HBM...]
    unnamed x2 -> x0, local copies, waits for them, and re-layouts: 0.95 us -> none
where the time goes in v7:
time: 37.9 us; the launch traced here: 37.5 us
  starting transfers between devices  24.9 us (66%)
  Pallas kernels  8.43 us (22%)
  waiting for transfers between devices  4.01 us (11%)
    ppermute x1, starting transfers between devices, per_device(): far = lax.ppermute(packed, 'col', [(c, c ^ 1) for c in range(n_col)])  7.83 us
    ppermute x1, starting transfers between devices, per_device(): lax.ppermute(pair, ('row', 'col'), chip)  3.89 us
    ppermute x1, waiting for transfers between devices, per_device(): lax.ppermute(after, 'depth', up)  2.89 us
    ppermute x1, starting transfers between devices, per_device(): lax.ppermute(pair, 'row', core)  2.53 us
    pallas_call x1, Pallas kernels, per_device(): pl.pallas_call(own_kernel, out_shape=sends, in_specs=[SMEM] + [VMEM] * 3,...  2.03 us
    ppermute x1, starting transfers between devices, per_device(): lax.ppermute(other_and, ('row', 'col'), chip)  2.02 us
    pallas_call x1, Pallas kernels, per_device(): pl.pallas_call(late_kernel, out_shape=[halos, struct(SC, *piece), struct(...  1.91 us
    ppermute x1, starting transfers between devices, per_device(): lax.ppermute(other_and, 'row', core)  1.83 us
  transfers between devices with their start and end apart: 10, of which 2 were waited for; matrix products, arithmetic and copies ran while one was open for 0% of the time, Pallas kernels for 12%

profile of v7, /device:TPU:1, one launch (start us, length us, event | category | flops | bytes accessed | tf_op | source)
XLA Modules:
  0.0 37.5 jit_solution(9096022611888975086)
XLA Ops:
  0.0 1.1 %pack.1.packed_ref = bf16[16,32,128]{2,1,0:T(8,128)(2,1)S(1)} custom-call(bf16[16,64,64]{2,1,0:T(8,128)(2,1)} %prolong_hbm.1), custom_call_target="tpu_custom_call" | custom-call | tf_op jit(solution)/shard_map/pack/pallas_call | solution.py:224
  1.1 7.8 %collective-permute-start.2 = (bf16[16,32,128]{2,1,0:T(8,128)(2,1)S(1)}, bf16[16,32,128]{2,1,0:T(8,128)(2,1)S(1)}, u32[]{:S(2)}, u32[]{:S(2)}) collective-permute-start(bf16[16,32,128]{2,1,0:T(8,128)(2,1)S(1)} %pack.1.packed_ref), channel_id=1, source_target_pairs={{0,4},{4,0},{8,12},{12,8},{16,20},{20,16},{24,28},{28,24},{1,5},{5... | collective-permute-start | bytes 393224 | tf_op jit(solution)/shard_map/ppermute | solution.py:233
  8.9 1.6 %blocks.1 = (bf16[57,32,128]{2,1,0:T(8,128)(2,1)S(1)}, bf16[57,32,128]{2,1,0:T(8,128)(2,1)S(1)}, bf16[16,64,64]{2,1,0:T(8,128)(2,1)S(1)}, s32[16,16]{1,0:T(8,128)S(1)}) custom-call(bf16[112,64,64]{2,1,0:T(8,128)(2,1)} %bitcast.5, bf16[16,32,128]{2,1,0:T(8,128)(2,1)S(1)} %pack.1.packed_ref, s32[7,16]{1,0:T(8,128)} %bitcast.6, s32[7,16]{1,0:T(8,128)} %bitcast.7, ...), custom_call_target="tpu_custom_call" | custom-call | tf_op jit(solution)/shard_map/blocks/pallas_call | solution.py:238
  10.6 1.3 %collective-permute-start = (bf16[57,32,128]{2,1,0:T(8,128)(2,1)S(1)}, bf16[57,32,128]{2,1,0:T(8,128)(2,1)S(1)}, u32[]{:S(2)}, u32[]{:S(2)}) collective-permute-start(bf16[57,32,128]{2,1,0:T(8,128)(2,1)S(1)} %get-tuple-element.18.first_ref), channel_id=1, source_target_pairs={{0,1},{1,2},{2,3},{3,0},{4,5},{5,6},{6,7},{7,4},{8,9},{9,10},{10,1... | collective-permute-start | bytes 1400840 | tf_op jit(solution)/shard_map/ppermute | solution.py:255
  11.9 1.5 %collective-permute-start.1 = (bf16[57,32,128]{2,1,0:T(8,128)(2,1)S(1)}, bf16[57,32,128]{2,1,0:T(8,128)(2,1)S(1)}, u32[]{:S(2)}, u32[]{:S(2)}) collective-permute-start(bf16[57,32,128]{2,1,0:T(8,128)(2,1)S(1)} %get-tuple-element.19.second_ref), channel_id=1, source_target_pairs={{1,0},{2,1},{3,2},{0,3},{5,4},{6,5},{7,6},{4,7},{9,8},{10,9},{11,1... | collective-permute-start | bytes 1400840 | tf_op jit(solution)/shard_map/ppermute | solution.py:255
  13.3 0.0 collective-permute-done.2.far_ref
  13.3 1.3 %collective-permute-start.3 = (bf16[16,32,128]{2,1,0:T(8,128)(2,1)S(1)}, bf16[16,32,128]{2,1,0:T(8,128)(2,1)S(1)}, u32[]{:S(2)}, u32[]{:S(2)}) collective-permute-start(bf16[16,32,128]{2,1,0:T(8,128)(2,1)S(1)} %collective-permute-done.2.far_ref), channel_id=1, source_target_pairs={{24,0},{12,4},{0,8},{20,12},{8,16},{28,20},{16,24},{4,28},{25,1},{... | collective-permute-start | bytes 393224 | tf_op jit(solution)/shard_map/ppermute | solution.py:267
  14.7 3.9 %collective-permute-start.4 = (bf16[24,32,128]{2,1,0:T(8,128)(2,1)S(1)}, bf16[24,32,128]{2,1,0:T(8,128)(2,1)S(1)}, u32[]{:S(2)}, u32[]{:S(2)}) collective-permute-start(bf16[24,32,128]{2,1,0:T(8,128)(2,1)S(1)} %pad_maximum_fusion), channel_id=1, source_target_pairs={{0,228},{4,224},{8,236},{12,232},{16,244},{20,240},{24,252},{28,24... | collective-permute-start | bytes 589832 | tf_op jit(solution)/shard_map/ppermute | solution.py:270
  18.6 2.5 %collective-permute-start.5 = (bf16[24,32,128]{2,1,0:T(8,128)(2,1)S(1)}, bf16[24,32,128]{2,1,0:T(8,128)(2,1)S(1)}, u32[]{:S(2)}, u32[]{:S(2)}) collective-permute-start(bf16[24,32,128]{2,1,0:T(8,128)(2,1)S(1)} %pad_maximum_fusion), channel_id=1, source_target_pairs={{0,32},{32,0},{64,96},{96,64},{128,160},{160,128},{192,224},{224,1... | collective-permute-start | bytes 589832 | tf_op jit(solution)/shard_map/ppermute | solution.py:270
  21.1 0.0 collective-permute-done.3.other_ref
  21.1 2.0 %collective-permute-start.6 = (bf16[24,32,128]{2,1,0:T(8,128)(2,1)S(1)}, bf16[24,32,128]{2,1,0:T(8,128)(2,1)S(1)}, u32[]{:S(2)}, u32[]{:S(2)}) collective-permute-start(bf16[24,32,128]{2,1,0:T(8,128)(2,1)S(1)} %pad_maximum_fusion.1), channel_id=1, source_target_pairs={{0,228},{4,224},{8,236},{12,232},{16,244},{20,240},{24,252},{28,24... | collective-permute-start | bytes 589832 | tf_op jit(solution)/shard_map/ppermute | solution.py:271
  23.1 0.0 collective-permute-done.prev_ref
  23.1 1.8 %collective-permute-start.7 = (bf16[24,32,128]{2,1,0:T(8,128)(2,1)S(1)}, bf16[24,32,128]{2,1,0:T(8,128)(2,1)S(1)}, u32[]{:S(2)}, u32[]{:S(2)}) collective-permute-start(bf16[24,32,128]{2,1,0:T(8,128)(2,1)S(1)} %pad_maximum_fusion.1), channel_id=1, source_target_pairs={{0,32},{32,0},{64,96},{96,64},{128,160},{160,128},{192,224},{224,1... | collective-permute-start | bytes 589832 | tf_op jit(solution)/shard_map/ppermute | solution.py:271
  25.0 0.0 collective-permute-done.1.next_ref
  25.0 0.7 %early.1 = (s32[1,640]{1,0:T(1,128)S(1)}, bf16[224,32,128]{2,1,0:T(8,128)(2,1)S(1)}, bf16[144,32,128]{2,1,0:T(8,128)(2,1)S(1)}) custom-call(s32[16,16]{1,0:T(8,128)S(1)} %get-tuple-element.17.ints_ref, bf16[57,32,128]{2,1,0:T(8,128)(2,1)S(1)} %get-tuple-element.18.first_ref, bf16[57,32,128]{2,1,0:T(8,128)(2,1)S(1)} %get-tuple-element.19.second_ref, ...), custom_call_target="tpu_custom_call" | custom-call | tf_op jit(solution)/shard_map/early/pallas_call | solution.py:275
  25.7 0.0 collective-permute-done.4.chip_pair
  25.7 0.0 collective-permute-done.5.core_pair
  25.7 1.1 %collective-permute-done.6.chip_ref = bf16[24,32,128]{2,1,0:T(8,128)(2,1)S(1)} collective-permute-done((bf16[24,32,128]{2,1,0:T(8,128)(2,1)S(1)}, bf16[24,32,128]{2,1,0:T(8,128)(2,1)S(1)}, u32[]{:S(2)}, u32[]{:S(2)}) %collective-permute-start.6) | collective-permute-done | bytes 196640 | tf_op jit(solution)/shard_map/ppermute | solution.py:271
  26.8 0.0 collective-permute-done.7.core_ref
  26.8 1.9 %late.1 = (bf16[144,32,128]{2,1,0:T(8,128)(2,1)S(1)}, bf16[28,32,128]{2,1,0:T(8,128)(2,1)S(1)}, bf16[28,32,128]{2,1,0:T(8,128)(2,1)S(1)}) custom-call(s32[1,640]{1,0:T(1,128)S(1)} %get-tuple-element.22.list_ref, bf16[224,32,128]{2,1,0:T(8,128)(2,1)S(1)} %get-tuple-element.23.blocks_ref, ...), custom_call_target="tpu_custom_call", output_to_operand_aliasing={{0}: (7, {})} | custom-call | tf_op jit(solution)/shard_map/late/pallas_call | solution.py:284
  28.7 1.3 %collective-permute-start.8 = (bf16[28,32,128]{2,1,0:T(8,128)(2,1)S(1)}, bf16[28,32,128]{2,1,0:T(8,128)(2,1)S(1)}, u32[]{:S(2)}, u32[]{:S(2)}) collective-permute-start(bf16[28,32,128]{2,1,0:T(8,128)(2,1)S(1)} %get-tuple-element.27), channel_id=1, source_target_pairs={{0,1},{1,2},{2,3},{3,0},{4,5},{5,6},{6,7},{7,4},{8,9},{9,10},{10,1... | collective-permute-start | bytes 688136 | tf_op jit(solution)/shard_map/ppermute | solution.py:294
  30.0 1.5 %collective-permute-start.9 = (bf16[28,32,128]{2,1,0:T(8,128)(2,1)S(1)}, bf16[28,32,128]{2,1,0:T(8,128)(2,1)S(1)}, u32[]{:S(2)}, u32[]{:S(2)}) collective-permute-start(bf16[28,32,128]{2,1,0:T(8,128)(2,1)S(1)} %get-tuple-element.28), channel_id=1, source_target_pairs={{1,0},{2,1},{3,2},{0,3},{5,4},{6,5},{7,6},{4,7},{9,8},{10,9},{11,1... | collective-permute-start | bytes 688136 | tf_op jit(solution)/shard_map/ppermute | solution.py:294
  31.5 2.0 %own.1.own_ref = f32[57,32,128]{2,1,0:T(8,128)S(1)} custom-call(s32[1,640]{1,0:T(1,128)S(1)} %get-tuple-element.22.list_ref, bf16[224,32,128]{2,1,0:T(8,128)(2,1)S(1)} %get-tuple-element.23.blocks_ref, bf16[16,64,64]{2,1,0:T(8,128)(2,1)S(1)} %get-tuple-element.24.turned_ref, bf16[144,32,128]{2,1,0:T(8,128)(2,1)S(1)} %get-tuple-element.26.halo_ref), custom_call_target="tpu_custom_call" | custom-call | tf_op jit(solution)/shard_map/own/pallas_call | solution.py:295
  33.5 2.9 %collective-permute-done.8.one_ref = bf16[28,32,128]{2,1,0:T(8,128)(2,1)S(1)} collective-permute-done((bf16[28,32,128]{2,1,0:T(8,128)(2,1)S(1)}, bf16[28,32,128]{2,1,0:T(8,128)(2,1)S(1)}, u32[]{:S(2)}, u32[]{:S(2)}) %collective-permute-start.8) | collective-permute-done | bytes 229408 | tf_op jit(solution)/shard_map/ppermute | solution.py:294
  36.4 0.0 collective-permute-done.9.two_ref
  36.4 1.1 %total.1 = f32[4,7,64,64]{3,2,1,0:T(8,128)} custom-call(f32[57,32,128]{2,1,0:T(8,128)S(1)} %own.1.own_ref, bf16[28,32,128]{2,1,0:T(8,128)(2,1)S(1)} %collective-permute-done.8.one_ref, bf16[28,32,128]{2,1,0:T(8,128)(2,1)S(1)} %collective-permute-done.9.two_ref), custom_call_target="tpu_custom_call" | custom-call | tf_op jit(solution)/shard_map/total/pallas_call | solution.py:303
  (3 shorter events, 0.1 us)
Async XLA Ops:
  1.1 12.2 %collective-permute-start.2 = (bf16[16,32,128]{2,1,0:T(8,128)(2,1)S(1)}, bf16[16,32,128]{2,1,0:T(8,128)(2,1)S(1)}, u32[]{:S(2)}, u32[]{:S(2)}) collective-permute-start(bf16[16,32,128]{2,1,0:T(8,128)(2,1)S(1)} %pack.1.packed_ref), channel_id=1, source_target_pairs={{0,4},{4,0},{8,12},{12,8},{16,20},{20,16},{24,28},{28,24},{1,5},{5... | collective-permute-start | bytes 393224 | tf_op jit(solution)/shard_map/ppermute | solution.py:233
  10.6 12.6 %collective-permute-start = (bf16[57,32,128]{2,1,0:T(8,128)(2,1)S(1)}, bf16[57,32,128]{2,1,0:T(8,128)(2,1)S(1)}, u32[]{:S(2)}, u32[]{:S(2)}) collective-permute-start(bf16[57,32,128]{2,1,0:T(8,128)(2,1)S(1)} %get-tuple-element.18.first_ref), channel_id=1, source_target_pairs={{0,1},{1,2},{2,3},{3,0},{4,5},{5,6},{6,7},{7,4},{8,9},{9,10},{10,1... | collective-permute-start | bytes 1400840 | tf_op jit(solution)/shard_map/ppermute | solution.py:255
  11.9 13.1 %collective-permute-start.1 = (bf16[57,32,128]{2,1,0:T(8,128)(2,1)S(1)}, bf16[57,32,128]{2,1,0:T(8,128)(2,1)S(1)}, u32[]{:S(2)}, u32[]{:S(2)}) collective-permute-start(bf16[57,32,128]{2,1,0:T(8,128)(2,1)S(1)} %get-tuple-element.19.second_ref), channel_id=1, source_target_pairs={{1,0},{2,1},{3,2},{0,3},{5,4},{6,5},{7,6},{4,7},{9,8},{10,9},{11,1... | collective-permute-start | bytes 1400840 | tf_op jit(solution)/shard_map/ppermute | solution.py:255
  13.3 7.8 %collective-permute-start.3 = (bf16[16,32,128]{2,1,0:T(8,128)(2,1)S(1)}, bf16[16,32,128]{2,1,0:T(8,128)(2,1)S(1)}, u32[]{:S(2)}, u32[]{:S(2)}) collective-permute-start(bf16[16,32,128]{2,1,0:T(8,128)(2,1)S(1)} %collective-permute-done.2.far_ref), channel_id=1, source_target_pairs={{24,0},{12,4},{0,8},{20,12},{8,16},{28,20},{16,24},{4,28},{25,1},{... | collective-permute-start | bytes 393224 | tf_op jit(solution)/shard_map/ppermute | solution.py:267
  14.7 11.0 %collective-permute-start.4 = (bf16[24,32,128]{2,1,0:T(8,128)(2,1)S(1)}, bf16[24,32,128]{2,1,0:T(8,128)(2,1)S(1)}, u32[]{:S(2)}, u32[]{:S(2)}) collective-permute-start(bf16[24,32,128]{2,1,0:T(8,128)(2,1)S(1)} %pad_maximum_fusion), channel_id=1, source_target_pairs={{0,228},{4,224},{8,236},{12,232},{16,244},{20,240},{24,252},{28,24... | collective-permute-start | bytes 589832 | tf_op jit(solution)/shard_map/ppermute | solution.py:270
  18.6 7.1 %collective-permute-start.5 = (bf16[24,32,128]{2,1,0:T(8,128)(2,1)S(1)}, bf16[24,32,128]{2,1,0:T(8,128)(2,1)S(1)}, u32[]{:S(2)}, u32[]{:S(2)}) collective-permute-start(bf16[24,32,128]{2,1,0:T(8,128)(2,1)S(1)} %pad_maximum_fusion), channel_id=1, source_target_pairs={{0,32},{32,0},{64,96},{96,64},{128,160},{160,128},{192,224},{224,1... | collective-permute-start | bytes 589832 | tf_op jit(solution)/shard_map/ppermute | solution.py:270
  21.1 5.7 %collective-permute-start.6 = (bf16[24,32,128]{2,1,0:T(8,128)(2,1)S(1)}, bf16[24,32,128]{2,1,0:T(8,128)(2,1)S(1)}, u32[]{:S(2)}, u32[]{:S(2)}) collective-permute-start(bf16[24,32,128]{2,1,0:T(8,128)(2,1)S(1)} %pad_maximum_fusion.1), channel_id=1, source_target_pairs={{0,228},{4,224},{8,236},{12,232},{16,244},{20,240},{24,252},{28,24... | collective-permute-start | bytes 589832 | tf_op jit(solution)/shard_map/ppermute | solution.py:271
  23.1 3.6 %collective-permute-start.7 = (bf16[24,32,128]{2,1,0:T(8,128)(2,1)S(1)}, bf16[24,32,128]{2,1,0:T(8,128)(2,1)S(1)}, u32[]{:S(2)}, u32[]{:S(2)}) collective-permute-start(bf16[24,32,128]{2,1,0:T(8,128)(2,1)S(1)} %pad_maximum_fusion.1), channel_id=1, source_target_pairs={{0,32},{32,0},{64,96},{96,64},{128,160},{160,128},{192,224},{224,1... | collective-permute-start | bytes 589832 | tf_op jit(solution)/shard_map/ppermute | solution.py:271
  28.7 7.7 %collective-permute-start.8 = (bf16[28,32,128]{2,1,0:T(8,128)(2,1)S(1)}, bf16[28,32,128]{2,1,0:T(8,128)(2,1)S(1)}, u32[]{:S(2)}, u32[]{:S(2)}) collective-permute-start(bf16[28,32,128]{2,1,0:T(8,128)(2,1)S(1)} %get-tuple-element.27), channel_id=1, source_target_pairs={{0,1},{1,2},{2,3},{3,0},{4,5},{5,6},{6,7},{7,4},{8,9},{9,10},{10,1... | collective-permute-start | bytes 688136 | tf_op jit(solution)/shard_map/ppermute | solution.py:294
  30.0 6.4 %collective-permute-start.9 = (bf16[28,32,128]{2,1,0:T(8,128)(2,1)S(1)}, bf16[28,32,128]{2,1,0:T(8,128)(2,1)S(1)}, u32[]{:S(2)}, u32[]{:S(2)}) collective-permute-start(bf16[28,32,128]{2,1,0:T(8,128)(2,1)S(1)} %get-tuple-element.28), channel_id=1, source_target_pairs={{1,0},{2,1},{3,2},{0,3},{5,4},{6,5},{7,6},{4,7},{9,8},{10,9},{11,1... | collective-permute-start | bytes 688136 | tf_op jit(solution)/shard_map/ppermute | solution.py:294
